TPU v7x, 32 devices: a whole 2x2x4 slice. The times are simulated.
32 devices in a mesh: gx: 4 (over y, core), gy: 8 (over z, x).
Axes of the slice: x: 2, y: 2, z: 4, core: 2. Of those that a mesh axis runs over, the one named last changes fastest.
Arguments:
- tokens: bfloat16 [10960, 8, 128], P('gx', 'gy'), may hold values from -6 to 6
- project_in: bfloat16 [1024, 3, 1024], P('gy', None, 'gx'), may hold values from -0.1875 to 0.1875
- query_bias: float32 [1024], P('gx'), may hold values from -3 to 3
- value_bias: float32 [1024], P('gx'), may hold values from -3 to 3
- project_out: bfloat16 [1024, 1024], P('gx', 'gy'), may hold values from -0.75 to 0.75
- output_bias: float32 [1024], P('gy'), may hold values from -2 to 2
- attention_scale: float32 [1024], P('gy'), may hold values from 0.5 to 2
- first_norm_gain: float32 [1024], P('gy'), may hold values from 0.1 to 1.9
- first_norm_bias: float32 [1024], P('gy'), may hold values from -2 to 2
- second_norm_gain: float32 [1024], P('gy'), may hold values from 0.1 to 1.9
- second_norm_bias: float32 [1024], P('gy'), may hold values from -2 to 2
- expand_weight: bfloat16 [1024, 4096], P('gy', 'gx'), may hold values from -0.1875 to 0.1875
- expand_bias: float32 [4096], P('gx'), may hold values from -3 to 3
- shrink_weight: bfloat16 [4096, 1024], P('gx', 'gy'), may hold values from -0.09375 to 0.09375
- shrink_bias: float32 [1024], P('gy'), may hold values from -2 to 2
- feedforward_scale: float32 [1024], P('gy'), may hold values from 0.5 to 2
- cotangent: bfloat16 [10960, 8, 128], P('gx', 'gy'), may hold values from -6 to 6
Outputs:
- block_output: bfloat16 [10960, 8, 128], P('gx', 'gy')
- input_gradient: float32 [10960, 8, 128], P('gx', 'gy')
- project_in_grad: float32 [1024, 3, 1024], P('gy', None, 'gx')
- query_bias_grad: float32 [1024], P('gx')
- value_bias_grad: float32 [1024], P('gx')
- project_out_grad: float32 [1024, 1024], P('gx', 'gy')
- output_bias_grad: float32 [1024], P('gy')
- attention_scale_grad: float32 [1024], P('gy')
- first_gain_grad: float32 [1024], P('gy')
- first_shift_grad: float32 [1024], P('gy')
- second_gain_grad: float32 [1024], P('gy')
- second_shift_grad: float32 [1024], P('gy')
- expand_weight_grad: float32 [1024, 4096], P('gy', 'gx')
- expand_bias_grad: float32 [4096], P('gx')
- shrink_weight_grad: float32 [4096, 1024], P('gx', 'gy')
- shrink_bias_grad: float32 [1024], P('gy')
- feedforward_scale_grad: float32 [1024], P('gy')
All inputs are finite; a program needn't handle non-finite values.
Results may differ from a plain program's by a relative error of at most 0.012.
The roundings to bfloat16 on the way count: a program that leaves them out, or rounds other values in their place, can miss the bound.
Values may be sent and summed in bfloat16 or wider, within the bound.
No kernel may reach another device: no remote copies, remote signals or barrier semaphores. Data moves between devices by JAX's collectives and lax.ppermute only.
A program may use at most 512 MiB of HBM per device.

v0:
```python
import jax
import jax.numpy as jnp
from jax import lax
from jax.sharding import PartitionSpec as P

D = 1024
HEAD_DIM = 64
SEQ = 1370


def width_stats(first_term, second_term):
    return lax.psum((first_term, second_term), "gy")


def layer_norm_forward(values, gain, shift):
    total, squares = width_stats(
        jnp.sum(values, axis=1, keepdims=True), jnp.sum(values * values, axis=1, keepdims=True)
    )
    center = total / D
    spread = squares / D - center * center
    rstd = lax.rsqrt(spread + 1e-06)
    normed = (values - center) * rstd
    return (normed * gain + shift, normed, rstd)


def layer_norm_backward(grad_norm, gain, normed, rstd):
    scaled = grad_norm * gain
    total, along = width_stats(
        jnp.sum(scaled, axis=1, keepdims=True), jnp.sum(scaled * normed, axis=1, keepdims=True)
    )
    return rstd * (scaled - total / D - normed * (along / D))


def all_rows(values):
    return lax.all_gather(values, "gx", axis=0, tiled=True)


def all_heads(values):
    return lax.all_gather(values, "gy", axis=0, tiled=True)


def head_sums(whole, weight):
    owned_rows = lax.all_to_all(whole, "gy", split_axis=0, concat_axis=1, tiled=True)
    full_weight = lax.all_gather(weight, "gy", axis=0, tiled=True)
    return jnp.dot(owned_rows, full_weight, preferred_element_type=jnp.float32)


def row_sums(whole, weight):
    owned_rows = lax.all_to_all(whole, "gx", split_axis=0, concat_axis=1, tiled=True)
    full_weight = lax.all_gather(weight, "gx", axis=0, tiled=True)
    return jnp.dot(owned_rows, full_weight, preferred_element_type=jnp.float32)


def inner_rows(left, right):
    return lax.dot_general(
        left, right, (((0,), (0,)), ((), ())), preferred_element_type=jnp.float32
    )


def gelu_exact(values):
    return jax.nn.gelu(values, approximate=False)


def attend_forward(parts):
    query, keys, values = parts
    scores = jnp.einsum(
        "qhd,khd->hqk", query, keys, preferred_element_type=jnp.float32
    ) * HEAD_DIM ** (-0.5)
    peak = jnp.max(scores, axis=-1, keepdims=True)
    raised = jnp.exp(scores - peak)
    total = jnp.sum(raised, axis=-1, keepdims=True)
    weights = (raised / total).astype(jnp.bfloat16)
    attended = jnp.einsum(
        "hqk,khd->qhd", weights, values, preferred_element_type=jnp.float32
    ).astype(jnp.bfloat16)
    return (attended, peak + jnp.log(total))


def attend_backward(parts):
    query, keys, values, grad_out, log_total = parts
    scores = jnp.einsum(
        "qhd,khd->hqk", query, keys, preferred_element_type=jnp.float32
    ) * HEAD_DIM ** (-0.5)
    probs = jnp.exp(scores - log_total)
    grad_probs = jnp.einsum("qhd,khd->hqk", grad_out, values, preferred_element_type=jnp.float32)
    grad_scores = (
        probs * (grad_probs - jnp.sum(probs * grad_probs, axis=-1, keepdims=True))
    ).astype(jnp.bfloat16)
    grad_query = (
        jnp.einsum("hqk,khd->qhd", grad_scores, keys, preferred_element_type=jnp.float32)
        * HEAD_DIM ** (-0.5)
    ).astype(jnp.bfloat16)
    grad_keys = (
        jnp.einsum("hqk,qhd->khd", grad_scores, query, preferred_element_type=jnp.float32)
        * HEAD_DIM ** (-0.5)
    ).astype(jnp.bfloat16)
    grad_values = jnp.einsum(
        "hqk,qhd->khd", probs.astype(jnp.bfloat16), grad_out, preferred_element_type=jnp.float32
    ).astype(jnp.bfloat16)
    return (grad_query, grad_keys, grad_values)


def on_device(
    tokens,
    project_in,
    query_bias,
    value_bias,
    project_out,
    output_bias,
    attention_scale,
    first_norm_gain,
    first_norm_bias,
    second_norm_gain,
    second_norm_bias,
    expand_weight,
    expand_bias,
    shrink_weight,
    shrink_bias,
    feedforward_scale,
    cotangent,
):
    head_cols = project_out.shape[0]
    heads_here = head_cols // HEAD_DIM
    width_here = D // lax.axis_size("gy")
    packed_shape = tokens.shape
    joined_weight = project_in.reshape(width_here, 3 * head_cols)
    input_tokens = tokens.reshape(-1, width_here).astype(jnp.float32)
    first_normed, first_standardized, first_inverse_deviation = layer_norm_forward(
        input_tokens, first_norm_gain, first_norm_bias
    )
    first_low = first_normed.astype(jnp.bfloat16)
    first_all = all_rows(first_low)
    mixed = head_sums(first_all, joined_weight)
    query = (mixed[:, :head_cols] + query_bias).astype(jnp.bfloat16)
    keys = mixed[:, head_cols : 2 * head_cols].astype(jnp.bfloat16)
    values = (mixed[:, 2 * head_cols :] + value_bias).astype(jnp.bfloat16)
    image_count = query.shape[0] // SEQ
    shape_four = (image_count, SEQ, heads_here, HEAD_DIM)
    query_four = query.reshape(shape_four)
    keys_four = keys.reshape(shape_four)
    values_four = values.reshape(shape_four)
    attended, log_totals = lax.map(attend_forward, (query_four, keys_four, values_four))
    attended = attended.reshape(-1, head_cols)
    attended_all = all_heads(attended)
    branch_a = row_sums(attended_all, project_out) + output_bias
    middle_residual = input_tokens + attention_scale * branch_a
    second_normed, second_standardized, second_inverse_deviation = layer_norm_forward(
        middle_residual, second_norm_gain, second_norm_bias
    )
    second_low = second_normed.astype(jnp.bfloat16)
    second_all = all_rows(second_low)
    preact = head_sums(second_all, expand_weight) + expand_bias
    hidden = gelu_exact(preact).astype(jnp.bfloat16)
    hidden_all = all_heads(hidden)
    branch_b = row_sums(hidden_all, shrink_weight) + shrink_bias
    block_output = (middle_residual + feedforward_scale * branch_b).astype(jnp.bfloat16)
    output_gradient = cotangent.reshape(-1, width_here).astype(jnp.float32)
    feedforward_part = jnp.sum(output_gradient * branch_b, axis=0)
    grad_branch_b = output_gradient * feedforward_scale
    shrink_bias_part = jnp.sum(grad_branch_b, axis=0)
    grad_b_low = grad_branch_b.astype(jnp.bfloat16)
    grad_b_all = all_rows(grad_b_low)
    grad_hidden = head_sums(grad_b_all, shrink_weight.T)
    hidden_back = all_heads(hidden)
    shrink_weight_grad = inner_rows(hidden_back, grad_b_all)
    unused, gelu_pull = jax.vjp(gelu_exact, preact)
    grad_pre = gelu_pull(grad_hidden)[0].astype(jnp.bfloat16)
    expand_bias_part = jnp.sum(grad_pre.astype(jnp.float32), axis=0)
    grad_pre_all = all_heads(grad_pre)
    second_back = all_rows(second_low)
    expand_weight_grad = inner_rows(second_back, grad_pre_all)
    second_normed_gradient = row_sums(grad_pre_all, expand_weight.T)
    second_gain_slice = jnp.sum(second_normed_gradient * second_standardized, axis=0)
    second_shift_part = jnp.sum(second_normed_gradient, axis=0)
    middle_gradient = output_gradient + layer_norm_backward(
        second_normed_gradient, second_norm_gain, second_standardized, second_inverse_deviation
    )
    attention_part = jnp.sum(middle_gradient * branch_a, axis=0)
    grad_branch_a = middle_gradient * attention_scale
    output_bias_part = jnp.sum(grad_branch_a, axis=0)
    grad_a_low = grad_branch_a.astype(jnp.bfloat16)
    grad_a_all = all_rows(grad_a_low)
    grad_attended = head_sums(grad_a_all, project_out.T).astype(jnp.bfloat16)
    attended_back = all_heads(attended)
    project_out_grad = inner_rows(attended_back, grad_a_all)
    grad_query, grad_keys, grad_values = lax.map(
        attend_backward,
        (query_four, keys_four, values_four, grad_attended.reshape(shape_four), log_totals),
    )
    grad_query = grad_query.reshape(-1, head_cols)
    grad_keys = grad_keys.reshape(-1, head_cols)
    grad_values = grad_values.reshape(-1, head_cols)
    query_bias_part = jnp.sum(grad_query.astype(jnp.float32), axis=0)
    value_bias_part = jnp.sum(grad_values.astype(jnp.float32), axis=0)
    grad_mixed = jnp.concatenate((grad_query, grad_keys, grad_values), axis=1)
    grad_mixed_all = all_heads(grad_mixed)
    first_back = all_rows(first_low)
    project_in_grad = inner_rows(first_back, grad_mixed_all).reshape(width_here, 3, head_cols)
    first_normed_gradient = row_sums(grad_mixed_all, joined_weight.T)
    first_gain_slice = jnp.sum(first_normed_gradient * first_standardized, axis=0)
    first_shift_part = jnp.sum(first_normed_gradient, axis=0)
    input_gradient = middle_gradient + layer_norm_backward(
        first_normed_gradient, first_norm_gain, first_standardized, first_inverse_deviation
    )
    query_bias_grad, value_bias_grad, expand_bias_grad = lax.psum(
        (query_bias_part, value_bias_part, expand_bias_part), "gy"
    )
    (
        output_bias_grad,
        attention_scale_grad,
        first_gain_grad,
        first_shift_grad,
        second_gain_grad,
        second_shift_grad,
        shrink_bias_grad,
        feedforward_scale_grad,
    ) = lax.psum(
        (
            output_bias_part,
            attention_part,
            first_gain_slice,
            first_shift_part,
            second_gain_slice,
            second_shift_part,
            shrink_bias_part,
            feedforward_part,
        ),
        "gx",
    )
    return (
        block_output.reshape(packed_shape),
        input_gradient.reshape(packed_shape),
        project_in_grad,
        query_bias_grad,
        value_bias_grad,
        project_out_grad,
        output_bias_grad,
        attention_scale_grad,
        first_gain_grad,
        first_shift_grad,
        second_gain_grad,
        second_shift_grad,
        expand_weight_grad,
        expand_bias_grad,
        shrink_weight_grad,
        shrink_bias_grad,
        feedforward_scale_grad,
    )


def solution(mesh):
    placed = (
        P("gx", "gy", None),
        P("gy", None, "gx"),
        P("gx"),
        P("gx"),
        P("gx", "gy"),
        P("gy"),
        P("gy"),
        P("gy"),
        P("gy"),
        P("gy"),
        P("gy"),
        P("gy", "gx"),
        P("gx"),
        P("gx", "gy"),
        P("gy"),
        P("gy"),
        P("gx", "gy", None),
    )
    return jax.shard_map(
        on_device,
        mesh=mesh,
        in_specs=placed,
        out_specs=(
            P("gx", "gy", None),
            P("gx", "gy", None),
            P("gy", None, "gx"),
            P("gx"),
            P("gx"),
            P("gx", "gy"),
            P("gy"),
            P("gy"),
            P("gy"),
            P("gy"),
            P("gy"),
            P("gy"),
            P("gy", "gx"),
            P("gx"),
            P("gx", "gy"),
            P("gy"),
            P("gy"),
        ),
        check_vma=False,
    )
```

profile of v0, /device:TPU:0, one launch (start us, length us, event | category | flops | bytes accessed | tf_op | source)
XLA Modules:
  0.0 2867.6 jit_solution(1286184907756061786)
XLA Ops:
  11.0 38.8 %all-reduce.3 = (f32[2740,1]{0,1:T(1,128)S(1)}, f32[2740,1]{0,1:T(1,128)S(1)}) all-reduce(f32[2740,1]{0,1:T(1,128)S(1)} %broadcast_in_dim.58, f32[2740,1]{0,1:T(1,128)S(1)} %broadcast_in_dim.59), channel_id=1, replica_groups=mesh['gx'=4,'gy'=8] {'gy'}, use_global_device_ids=true, to_apply=%region_1.0 | all-reduce | flops 5480 | bytes 43840 | tf_op jit(solution)/shard_map/psum | solution.py:12
  53.8 24.1 all-gather.32.cloned.1.call-done
  88.8 82.0 %all-to-all-done = bf16[8,1370,128]{2,1,0:T(8,128)(2,1)S(1)} async-done(((bf16[8,1370,128]{2,1,0:T(8,128)(2,1)}), bf16[8,1370,128]{2,1,0:T(8,128)(2,1)S(1)}, u32[]{:S(2)}, u32[]{:S(2)}) %all-to-all-start) | async-done | bytes 2805792 | tf_op jit(solution)/shard_map/all_to_all | solution.py:43
  218.6 88.7 %all-gather.34.cloned.1.call-done = bf16[8,1370,256]{2,1,0:T(8,128)(2,1)} async-done(((bf16[1,1370,256]{2,1,0:T(8,128)(2,1)}), bf16[8,1370,256]{2,1,0:T(8,128)(2,1)}) %all-gather.34.cloned.1.call-update) | async-done | bytes 5611536 | tf_op jit(solution)/shard_map/all_gather | solution.py:39
  319.5 79.5 %all_gather.55 = bf16[1024,128]{1,0:T(8,128)(2,1)S(1)} all-gather(bf16[256,128]{1,0:T(8,128)(2,1)S(1)} %copy-done.22), channel_id=1, replica_groups=mesh['gx'=4,'gy'=8] {'gx'}, dimensions={0}, use_global_device_ids=true | all-gather | bytes 327680 | tf_op jit(solution)/shard_map/all_gather | solution.py:50
  413.4 34.3 %all-reduce.2 = (f32[2740,1]{0,1:T(1,128)S(1)}, f32[2740,1]{0,1:T(1,128)S(1)}) all-reduce(f32[2740,1]{0,1:T(1,128)S(1)} %broadcast_in_dim.60, f32[2740,1]{0,1:T(1,128)S(1)} %broadcast_in_dim.61), channel_id=1, replica_groups=mesh['gx'=4,'gy'=8] {'gy'}, use_global_device_ids=true, to_apply=%region_7.8 | all-reduce | flops 5480 | bytes 43840 | tf_op jit(solution)/shard_map/psum | solution.py:12
  458.7 14.3 all-gather.36.cloned.1.call-done
  477.3 59.9 %all-to-all-done.4 = bf16[8,1370,128]{2,1,0:T(8,128)(2,1)S(1)} async-done(((bf16[8,1370,128]{2,1,0:T(8,128)(2,1)}), bf16[8,1370,128]{2,1,0:T(8,128)(2,1)S(1)}, u32[]{:S(2)}, u32[]{:S(2)}) %all-to-all-start.4) | async-done | bytes 2805792 | tf_op jit(solution)/shard_map/all_to_all | solution.py:43
  550.5 76.4 %all-to-all-done.2 = bf16[8,1370,128]{2,1,0:T(8,128)(2,1)} async-done(((bf16[8,1370,128]{2,1,0:T(8,128)(2,1)}), bf16[8,1370,128]{2,1,0:T(8,128)(2,1)}, u32[]{:S(2)}, u32[]{:S(2)}) %all-to-all-start.2) | async-done | bytes 2805792 | tf_op jit(solution)/shard_map/all_to_all | solution.py:43
  639.6 19.5 convert_reduce_fusion
  662.9 426.4 %all-gather.38.cloned.1.call-done = bf16[8,1370,1024]{2,1,0:T(8,128)(2,1)} async-done(((bf16[1,1370,1024]{2,1,0:T(8,128)(2,1)}), bf16[8,1370,1024]{2,1,0:T(8,128)(2,1)}) %all-gather.38.cloned.1.call-update) | async-done | bytes 22446096 | tf_op jit(solution)/shard_map/all_gather | solution.py:39
  1089.4 24.8 all_to_all.124
  1122.3 399.8 %all-gather.42.cloned.1.call-done = bf16[8,1370,1024]{2,1,0:T(8,128)(2,1)} async-done(((bf16[1,1370,1024]{2,1,0:T(8,128)(2,1)}), bf16[8,1370,1024]{2,1,0:T(8,128)(2,1)}) %all-gather.42.cloned.1.call-update) | async-done | bytes 22446096 | tf_op jit(solution)/shard_map/all_gather | solution.py:39
  1522.2 24.4 all_to_all.132
  1556.0 28.8 %copy.81 = bf16[2740,4,1024]{0,2,1:T(8,128)(2,1)} copy(bf16[2740,4,1024]{2,0,1:T(8,128)(2,1)} %bitcast.16) | data formatting | bytes 44892160 | tf_op jit(solution)/shard_map/all_to_all | solution.py:49
  1584.8 225.2 %all-to-all-done.5 = bf16[4,2740,1024]{2,1,0:T(8,128)(2,1)} async-done(((bf16[4,2740,1024]{2,1,0:T(8,128)(2,1)}), bf16[4,2740,1024]{2,1,0:T(8,128)(2,1)}, u32[]{:S(2)}, u32[]{:S(2)}) %all-to-all-start.5) | async-done | bytes 22446112 | tf_op jit(solution)/shard_map/all_to_all | solution.py:49
  1810.0 29.1 %copy.83 = bf16[2740,4,1024]{0,2,1:T(8,128)(2,1)} copy(bf16[2740,4,1024]{2,0,1:T(8,128)(2,1)} %bitcast.26) | data formatting | bytes 44892160 | tf_op jit(solution)/shard_map/all_to_all | solution.py:49
  1839.1 15.3 multiply_reduce_fusion.1
  1855.0 37.2 %all-reduce.1 = (f32[2740,1]{0,1:T(1,128)}, f32[2740,1]{0,1:T(1,128)}) all-reduce(f32[2740,1]{0,1:T(1,128)S(1)} %broadcast_in_dim.63, f32[2740,1]{0,1:T(1,128)} %broadcast_in_dim.62), channel_id=1, replica_groups=mesh['gx'=4,'gy'=8] {'gy'}, use_global_device_ids=true, to_apply=%region_13.14 | all-reduce | flops 5480 | bytes 43840 | tf_op jit(solution)/shard_map/psum | solution.py:12
  1893.6 15.4 fusion.40
  1911.1 22.9 all-gather.44.cloned.1.call-done
  1943.8 85.1 %all_gather.65 = bf16[1024,256]{0,1:T(8,128)(2,1)S(1)} all-gather(bf16[128,256]{0,1:T(8,128)(2,1)S(1)} %bitcast.167), channel_id=1, replica_groups=mesh['gx'=4,'gy'=8] {'gy'}, dimensions={0}, use_global_device_ids=true | all-gather | bytes 589824 | tf_op jit(solution)/shard_map/all_gather | solution.py:44
  2047.6 20.2 multiply_reduce_fusion
  2067.8 25.7 multiply_convert_fusion
  2114.1 322.1 %all-gather.46.cloned.1.call-done = bf16[8,1370,768]{2,1,0:T(8,128)(2,1)} async-done(((bf16[1,1370,768]{2,1,0:T(8,128)(2,1)}), bf16[8,1370,768]{2,1,0:T(8,128)(2,1)}) %all-gather.46.cloned.1.call-update) | async-done | bytes 16834576 | tf_op jit(solution)/shard_map/all_gather | solution.py:39
  2436.1 20.2 all_to_all.140
  2463.5 189.4 %all_gather.67 = bf16[3072,128]{1,0:T(8,128)(2,1)} all-gather(bf16[768,128]{1,0:T(8,128)(2,1)S(1)} %bitcast.162), channel_id=1, replica_groups=mesh['gx'=4,'gy'=8] {'gx'}, dimensions={0}, use_global_device_ids=true | all-gather | bytes 983040 | tf_op jit(solution)/shard_map/all_gather | solution.py:50
  2664.9 22.6 reshape.141
  2687.4 22.4 reshape.145
  2738.7 17.8 reshape.149
  2767.6 21.8 copy.92
  2802.4 37.2 %all-reduce = (f32[2740,1]{0,1:T(1,128)}, f32[2740,1]{0,1:T(1,128)}, f32[256]{0:T(256)}, f32[256]{0:T(256)}, f32[1024]{0:T(1024)}) all-reduce(f32[2740,1]{0,1:T(1,128)S(1)} %broadcast_in_dim.65, f32[2740,1]{0,1:T(1,128)} %broadcast_in_dim.64, f32[256]{0:T(256)} %reduce_sum.206, ...), channel_id=1, replica_groups=mesh['gx'=4,'gy'=8] {'gy'}, use_global_device_ids=true, to_apply=%region_18.19 | all-reduce | flops 7016 | bytes 56128 | tf_op jit(solution)/shard_map/psum | solution.py:12
  (205 shorter events, 299.9 us)
Async XLA Ops:
  8.0 69.8 %all-gather.32.cloned.1.call-start = ((), (), s32[]{:S(2)}) async-start(), calls=%async_computation.13 | async-start | bytes 3512320 | tf_op jit(solution)/shard_map/all_gather | solution.py:35
  53.8 33.9 %copy-start.26 = (bf16[128,3,256]{2,0,1:T(8,128)(2,1)S(1)}, bf16[128,3,256]{2,0,1:T(8,128)(2,1)}, u32[]{:S(2)}) copy-start(bf16[128,3,256]{2,0,1:T(8,128)(2,1)} %param.18) | copy-start | bytes 589828
  82.1 88.6 %all-to-all-start = ((bf16[8,1370,128]{2,1,0:T(8,128)(2,1)}), bf16[8,1370,128]{2,1,0:T(8,128)(2,1)S(1)}, u32[]{:S(2)}, u32[]{:S(2)}) async-start(bf16[8,1370,128]{2,1,0:T(8,128)(2,1)} %all_to_all.112), calls=%async_computation | async-start | bytes 5636096 | tf_op jit(solution)/shard_map/all_to_all | solution.py:43
  87.6 85.9 %all-gather.22.cloned.1.call-start = ((), (), s32[]{:S(2)}) async-start(), calls=%async_computation.8 | async-start | bytes 1769472 | tf_op jit(solution)/shard_map/all_gather | solution.py:44
  88.5 218.7 %all-gather.34.cloned.1.call-start = ((), (), s32[]{:S(2)}) async-start(), calls=%async_computation.14 | async-start | bytes 6340608 | tf_op jit(solution)/shard_map/all_gather | solution.py:39
  313.1 86.0 %all-to-all-start.1 = ((bf16[4,2740,256]{2,1,0:T(8,128)(2,1)}), bf16[4,2740,256]{2,1,0:T(8,128)(2,1)}, u32[]{:S(2)}, u32[]{:S(2)}) async-start(bf16[4,2740,256]{2,1,0:T(8,128)(2,1)} %all_to_all.116), calls=%async_computation.1 | async-start | bytes 11239424 | tf_op jit(solution)/shard_map/all_to_all | solution.py:49
  318.4 131.7 %all-gather.40.cloned.1.call-start = ((), (), s32[]{:S(2)}) async-start(), calls=%async_computation.17 | async-start | bytes 3512320 | tf_op jit(solution)/shard_map/all_gather | solution.py:35
  319.5 153.5 %all-gather.36.cloned.1.call-start = ((), (), s32[]{:S(2)}) async-start(), calls=%async_computation.15 | async-start | bytes 3512320 | tf_op jit(solution)/shard_map/all_gather | solution.py:35
  407.4 40.4 %copy-start.42 = (f32[128]{0:T(128)S(1)}, f32[128]{0:T(128)}, u32[]{:S(2)}) copy-start(f32[128]{0:T(128)} %param.27) | copy-start | bytes 1540
  407.4 40.4 %copy-start.43 = (f32[128]{0:T(128)S(1)}, f32[128]{0:T(128)}, u32[]{:S(2)}) copy-start(f32[128]{0:T(128)} %param.26) | copy-start | bytes 1540
  413.4 41.1 %copy-start.8 = (f32[2740,128]{1,0:T(8,128)}, f32[2740,128]{1,0:T(8,128)S(1)}, u32[]{:S(2)}) copy-start(f32[2740,128]{1,0:T(8,128)S(1)} %get-tuple-element.154) | copy-start | bytes 4208644
  454.5 82.7 %all-to-all-start.4 = ((bf16[8,1370,128]{2,1,0:T(8,128)(2,1)}), bf16[8,1370,128]{2,1,0:T(8,128)(2,1)S(1)}, u32[]{:S(2)}, u32[]{:S(2)}) async-start(bf16[8,1370,128]{2,1,0:T(8,128)(2,1)} %all_to_all.128), calls=%async_computation.4 | async-start | bytes 5636096 | tf_op jit(solution)/shard_map/all_to_all | solution.py:43
  458.1 173.3 %all-gather.24.cloned.1.call-start = ((), (), s32[]{:S(2)}) async-start(), calls=%async_computation.9 | async-start | bytes 2359296 | tf_op jit(solution)/shard_map/all_gather | solution.py:44
  537.2 89.7 %all-to-all-start.2 = ((bf16[8,1370,128]{2,1,0:T(8,128)(2,1)}), bf16[8,1370,128]{2,1,0:T(8,128)(2,1)}, u32[]{:S(2)}, u32[]{:S(2)}) async-start(bf16[8,1370,128]{2,1,0:T(8,128)(2,1)} %all_to_all.120), calls=%async_computation.2 | async-start | bytes 5636096 | tf_op jit(solution)/shard_map/all_to_all | solution.py:43
  547.1 92.5 %all-gather.28.cloned.1.call-start = ((), (), s32[]{:S(2)}) async-start(), calls=%async_computation.11 | async-start | bytes 2359296 | tf_op jit(solution)/shard_map/all_gather | solution.py:44
  547.7 541.7 %all-gather.38.cloned.1.call-start = ((), (), s32[]{:S(2)}) async-start(), calls=%async_computation.16 | async-start | bytes 25362432 | tf_op jit(solution)/shard_map/all_gather | solution.py:39
  662.2 860.0 %all-gather.42.cloned.1.call-start = ((), (), s32[]{:S(2)}) async-start(), calls=%async_computation.18 | async-start | bytes 25362432 | tf_op jit(solution)/shard_map/all_gather | solution.py:39
  1114.2 432.4 %all-to-all-start.3 = ((bf16[4,2740,1024]{2,1,0:T(8,128)(2,1)}), bf16[4,2740,1024]{2,1,0:T(8,128)(2,1)}, u32[]{:S(2)}, u32[]{:S(2)}) async-start(bf16[4,2740,1024]{2,1,0:T(8,128)(2,1)} %all_to_all.124), calls=%async_computation.3 | async-start | bytes 44957696 | tf_op jit(solution)/shard_map/all_to_all | solution.py:49
  1546.6 263.4 %all-to-all-start.5 = ((bf16[4,2740,1024]{2,1,0:T(8,128)(2,1)}), bf16[4,2740,1024]{2,1,0:T(8,128)(2,1)}, u32[]{:S(2)}, u32[]{:S(2)}) async-start(bf16[4,2740,1024]{2,1,0:T(8,128)(2,1)} %all_to_all.132), calls=%async_computation.5 | async-start | bytes 44957696 | tf_op jit(solution)/shard_map/all_to_all | solution.py:49
  1554.6 284.5 %all-gather.30.cloned.1.call-start = ((), (), s32[]{:S(2)}) async-start(), calls=%async_computation.12 | async-start | bytes 1310720 | tf_op jit(solution)/shard_map/all_gather | solution.py:50
  1555.2 338.4 %all-gather.26.cloned.1.call-start = ((), (), s32[]{:S(2)}) async-start(), calls=%async_computation.10 | async-start | bytes 1310720 | tf_op jit(solution)/shard_map/all_gather | solution.py:50
  1555.9 378.0 %all-gather.44.cloned.1.call-start = ((), (), s32[]{:S(2)}) async-start(), calls=%async_computation.19 | async-start | bytes 3512320 | tf_op jit(solution)/shard_map/all_gather | solution.py:35
  1839.1 54.5 %copy-start.18 = (f32[2740,128]{1,0:T(8,128)S(1)}, f32[2740,128]{1,0:T(8,128)}, u32[]{:S(2)}) copy-start(f32[2740,128]{1,0:T(8,128)} %get-tuple-element.163) | copy-start | bytes 4208644
  1839.1 54.5 %copy-start.21 = (bf16[2740,1,128]{2,0,1:T(8,128)(2,1)S(1)}, bf16[2740,1,128]{2,0,1:T(8,128)(2,1)}, u32[]{:S(2)}) copy-start(bf16[2740,1,128]{2,0,1:T(8,128)(2,1)} %param.33) | copy-start | bytes 2104324
  1839.1 54.5 %copy-start.34 = (f32[128]{0:T(128)S(1)}, f32[128]{0:T(128)}, u32[]{:S(2)}) copy-start(f32[128]{0:T(128)} %param.23) | copy-start | bytes 1540
  1911.1 117.9 %copy-start.25 = (f32[4,1370]{1,0:T(4,128)S(1)}, f32[4,1370]{1,0:T(4,128)}, u32[]{:S(2)}) copy-start(f32[4,1370]{1,0:T(4,128)} %copy-done.24) | copy-start | bytes 65764
  1911.1 117.9 %copy-start.32 = (f32[4,1370]{1,0:T(4,128)S(1)}, f32[4,1370]{1,0:T(4,128)}, u32[]{:S(2)}) copy-start(f32[4,1370]{1,0:T(4,128)} %copy-done.31) | copy-start | bytes 65764
  1938.3 90.7 %all-to-all-start.6 = ((bf16[8,1370,128]{2,1,0:T(8,128)(2,1)}), bf16[8,1370,128]{2,1,0:T(8,128)(2,1)S(1)}, u32[]{:S(2)}, u32[]{:S(2)}) async-start(bf16[8,1370,128]{2,1,0:T(8,128)(2,1)} %all_to_all.136), calls=%async_computation.6 | async-start | bytes 5636096 | tf_op jit(solution)/shard_map/all_to_all | solution.py:43
  1943.8 492.4 %all-gather.46.cloned.1.call-start = ((), (), s32[]{:S(2)}) async-start(), calls=%async_computation.20 | async-start | bytes 19021824 | tf_op jit(solution)/shard_map/all_gather | solution.py:39
  2456.3 311.3 %all-to-all-start.7 = ((bf16[4,2740,768]{2,1,0:T(8,128)(2,1)}), bf16[4,2740,768]{2,1,0:T(8,128)(2,1)}, u32[]{:S(2)}, u32[]{:S(2)}) async-start(bf16[4,2740,768]{2,1,0:T(8,128)(2,1)} %all_to_all.140), calls=%async_computation.7 | async-start | bytes 33718272 | tf_op jit(solution)/shard_map/all_to_all | solution.py:49
  2463.5 192.6 %copy-start.3 = (bf16[4,2740,128]{2,1,0:T(8,128)(2,1)S(1)}, bf16[4,2740,128]{2,1,0:T(8,128)(2,1)}, u32[]{:S(2)}) copy-start(bf16[4,2740,128]{2,1,0:T(8,128)(2,1)} %all-gather.32.cloned.1.call-done) | copy-start | bytes 8417284
  2789.4 51.7 %copy-start.14 = (f32[2740,128]{1,0:T(8,128)S(1)}, f32[2740,128]{1,0:T(8,128)}, u32[]{:S(2)}) copy-start(f32[2740,128]{1,0:T(8,128)} %copy-done.13) | copy-start | bytes 4208644
  (35 other events, 448.5 us)
Sparse Core Ops, SparseCore 0:
  53.9 23.9 all-gather.31
  320.8 40.4 all-gather.39
  450.2 22.7 all-gather.35
  475.0 67.0 all-gather.23
  549.7 77.6 all-gather.27
  1556.7 22.9 all-gather.29
  1581.2 22.4 all-gather.25
  1911.2 22.7 all-gather.43
  2114.2 321.8 all-gather.45
Sparse Core Ops, SparseCore 1:
  90.7 80.1 all-gather.21
  218.7 88.5 all-gather.33
  662.3 427.0 all-gather.37
  1090.9 431.2 all-gather.41
where the time goes:
time: 2870 us
  waiting for transfers between devices  1740 us (61%)
  blocking collectives  508 us (18%)
  local copies, waits for them, and re-layouts  292 us (10%)
  matrix products  193 us (7%)
  other arithmetic  59.5 us (2%)
  starting transfers between devices  53.9 us (2%)
    all_gather x4, waiting for transfers between devices, all_heads(): return lax.all_gather(values, 'gy', axis=0, tiled=True)  1240 us
    all_gather x2, blocking collectives, row_sums(): full_weight = lax.all_gather(weight, 'gx', axis=0, tiled=True)  269 us
    all_to_all x4, waiting for transfers between devices, row_sums(): lax.all_to_all(whole, 'gx', split_axis=0, concat_axis=1, tiled=True)  225 us
    all_to_all x4, waiting for transfers between devices, head_sums(): lax.all_to_all(whole, 'gy', split_axis=0, concat_axis=1, tiled=True)  218 us
    all_to_all x8, local copies, waits for them, and re-layouts, row_sums(): lax.all_to_all(whole, 'gx', split_axis=0, concat_axis=1, tiled=True)  163 us
    psum x4, blocking collectives, width_stats(): return lax.psum((first_term, second_term), 'gy')  148 us
    unnamed x104, local copies, waits for them, and re-layouts  93.5 us
    all_gather x1, blocking collectives, head_sums(): full_weight = lax.all_gather(weight, 'gy', axis=0, tiled=True)  85.1 us
  transfers between devices with their start and end apart: 21, of which 11 were waited for; matrix products, arithmetic and copies ran while one was open for 8% of the time, Pallas kernels for 0%

commit v1 on v0

v1 whole, which is shorter than its diff:
```python
import jax
import jax.numpy as jnp
from jax import lax
from jax.sharding import PartitionSpec as P

D = 1024
HEAD_DIM = 64
SEQ = 1370
SCALE = HEAD_DIM ** (-0.5)
LOW = jnp.bfloat16
WIDE = jnp.float32


def swap(values, axis, bit):
    size = lax.axis_size(axis)
    return lax.ppermute(values, axis, [(k, k ^ bit) for k in range(size)])


def gather_rows(values):
    bit = lax.axis_size("gx") // 2
    while bit:
        values = jnp.concatenate((values, swap(values, "gx", bit)), axis=0)
        bit //= 2
    return values


def slot_blocks(count):
    order = [0]
    bit = count // 2
    while bit:
        order = order + [k ^ bit for k in order]
        bit //= 2
    return order


def scatter_rows(partial):
    bit = 1
    while bit < lax.axis_size("gx"):
        half = partial.shape[0] // 2
        received = swap(partial[half:].astype(LOW), "gx", bit)
        partial = partial[:half] + received.astype(WIDE)
        bit *= 2
    return partial


def owner_pairs(nx, ny):
    images = ny // nx
    return [
        (i * ny + h * nx + q, q * ny + i * images + h)
        for i in range(nx)
        for h in range(images)
        for q in range(nx)
    ]


def to_owner(values, block):
    nx, ny = lax.axis_size("gx"), lax.axis_size("gy")
    width = D // ny
    images = values.reshape(-1, SEQ, width)
    images = jnp.pad(images, ((0, 0), (0, nx * block - SEQ), (0, 0)))
    blocks = images.reshape(ny, block, width)
    blocks = lax.all_to_all(blocks, "gy", split_axis=0, concat_axis=0, tiled=True)
    blocks = lax.ppermute(blocks, ("gx", "gy"), owner_pairs(nx, ny))
    return blocks.transpose(1, 0, 2).reshape(block, D)


def from_owner(values, packed_shape):
    nx, ny = lax.axis_size("gx"), lax.axis_size("gy")
    width = D // ny
    block = values.shape[0]
    blocks = values.reshape(block, ny, width).transpose(1, 0, 2)
    blocks = lax.ppermute(blocks, ("gx", "gy"), [(b, a) for a, b in owner_pairs(nx, ny)])
    blocks = lax.all_to_all(blocks, "gy", split_axis=0, concat_axis=0, tiled=True)
    return blocks.reshape(ny // nx, nx * block, width)[:, :SEQ].reshape(packed_shape)


def norm_forward(values, gain, shift):
    center = jnp.mean(values, axis=1, keepdims=True)
    spread = jnp.mean(values * values, axis=1, keepdims=True) - center * center
    rstd = lax.rsqrt(spread + 1e-06)
    normed = (values - center) * rstd
    return (normed * gain + shift).astype(LOW), normed, rstd


def norm_backward(grad, gain, normed, rstd):
    scaled = grad * gain
    total = jnp.mean(scaled, axis=1, keepdims=True)
    along = jnp.mean(scaled * normed, axis=1, keepdims=True)
    return rstd * (scaled - total - normed * along)


def times(left, right):
    return jnp.dot(left, right, preferred_element_type=WIDE)


def times_t(left, right):
    return lax.dot_general(left, right, (((1,), (1,)), ((), ())), preferred_element_type=WIDE)


def inner_rows(left, right):
    return lax.dot_general(left, right, (((0,), (0,)), ((), ())), preferred_element_type=WIDE)


def gelu_exact(values):
    return jax.nn.gelu(values, approximate=False)


def heads_of(values):
    return values.reshape(values.shape[0], -1, HEAD_DIM)


def attend_forward(query, keys, values, bias):
    scores = jnp.einsum("qhd,khd->hqk", heads_of(query), heads_of(keys), preferred_element_type=WIDE)
    scores = scores * SCALE + bias
    peak = jnp.max(scores, axis=-1, keepdims=True)
    raised = jnp.exp(scores - peak)
    total = jnp.sum(raised, axis=-1, keepdims=True)
    weights = (raised / total).astype(LOW)
    attended = jnp.einsum("hqk,khd->qhd", weights, heads_of(values), preferred_element_type=WIDE)
    return attended.astype(LOW).reshape(query.shape), peak + jnp.log(total)


def attend_backward(query, keys, values, grad_out, log_total, bias):
    q, k, v, g = heads_of(query), heads_of(keys), heads_of(values), heads_of(grad_out)
    scores = jnp.einsum("qhd,khd->hqk", q, k, preferred_element_type=WIDE) * SCALE + bias
    probs = jnp.exp(scores - log_total)
    grad_probs = jnp.einsum("qhd,khd->hqk", g, v, preferred_element_type=WIDE)
    grad_scores = (
        probs * (grad_probs - jnp.sum(probs * grad_probs, axis=-1, keepdims=True))
    ).astype(LOW)
    grad_query = jnp.einsum("hqk,khd->qhd", grad_scores, k, preferred_element_type=WIDE) * SCALE
    grad_keys = jnp.einsum("hqk,qhd->khd", grad_scores, q, preferred_element_type=WIDE) * SCALE
    grad_values = jnp.einsum("hqk,qhd->khd", probs.astype(LOW), g, preferred_element_type=WIDE)
    return tuple(item.astype(LOW).reshape(query.shape) for item in (grad_query, grad_keys, grad_values))


def token_sums(vectors):
    flat = vectors.reshape(vectors.shape[0], lax.axis_size("gy"), -1)
    flat = flat.transpose(1, 0, 2)
    bit = lax.axis_size("gy") // 2
    place = lax.axis_index("gy")
    while bit:
        half = flat.shape[0] // 2
        upper = (place & bit) != 0
        kept = jnp.where(upper, flat[half:], flat[:half])
        sent = jnp.where(upper, flat[:half], flat[half:])
        flat = kept + swap(sent, "gy", bit)
        bit //= 2
    flat = flat[0]
    bit = 1
    while bit < lax.axis_size("gx"):
        flat = flat + swap(flat, "gx", bit)
        bit *= 2
    return flat


def image_sums(vector):
    bit = 1
    while bit < lax.axis_size("gy"):
        vector = vector + swap(vector, "gy", bit)
        bit *= 2
    return vector


def on_device(
    tokens,
    project_in,
    query_bias,
    value_bias,
    project_out,
    output_bias,
    attention_scale,
    first_norm_gain,
    first_norm_bias,
    second_norm_gain,
    second_norm_bias,
    expand_weight,
    expand_bias,
    shrink_weight,
    shrink_bias,
    feedforward_scale,
    cotangent,
):
    nx, ny = lax.axis_size("gx"), lax.axis_size("gy")
    head_cols = project_out.shape[0]
    hidden_cols = expand_weight.shape[1]
    packed_shape = tokens.shape
    block = -(-SEQ // (nx * 16)) * 16
    column = jnp.arange(block)
    bias = jnp.concatenate(
        [
            jnp.where((lax.axis_index("gx") ^ k) * block + column < SEQ, 0.0, -1e30)
            for k in slot_blocks(nx)
        ]
    ).astype(WIDE)

    small = jnp.stack(
        (
            output_bias,
            attention_scale,
            first_norm_gain,
            first_norm_bias,
            second_norm_gain,
            second_norm_bias,
            shrink_bias,
            feedforward_scale,
        )
    )
    small = lax.all_gather(small, "gy", axis=1, tiled=True)
    out_shift, attn_scale, gain_one, shift_one, gain_two, shift_two, shrink_shift, ff_scale = [
        small[k] for k in range(8)
    ]
    inputs = to_owner(tokens, block).astype(WIDE)
    weight_in = lax.all_gather(project_in.reshape(-1, 3 * head_cols), "gy", axis=0, tiled=True)
    later = jnp.concatenate((project_out.T, expand_weight, shrink_weight.T), axis=1)
    later = lax.all_gather(later, "gy", axis=0, tiled=True)
    weight_out = later[:, :head_cols]
    weight_expand = later[:, head_cols : head_cols + hidden_cols]
    weight_shrink = later[:, head_cols + hidden_cols :]

    first, first_hat, first_rstd = norm_forward(inputs, gain_one, shift_one)
    first_all = gather_rows(first)
    mixed = times(first_all, weight_in)
    query = (mixed[:, :head_cols] + query_bias).astype(LOW)
    keys = mixed[:, head_cols : 2 * head_cols].astype(LOW)
    values = (mixed[:, 2 * head_cols :] + value_bias).astype(LOW)
    attended, log_total = attend_forward(query, keys, values, bias)

    grad = to_owner(cotangent, block).astype(WIDE)
    grad_b = grad * ff_scale
    grad_b_all = gather_rows(grad_b.astype(LOW))

    branch_a = scatter_rows(times_t(attended, weight_out)) + out_shift
    middle = inputs + attn_scale * branch_a
    second, second_hat, second_rstd = norm_forward(middle, gain_two, shift_two)
    second_all = gather_rows(second)
    preact = times(second_all, weight_expand) + expand_bias
    hidden = gelu_exact(preact).astype(LOW)
    grad_hidden = times(grad_b_all, weight_shrink)
    unused, gelu_pull = jax.vjp(gelu_exact, preact)
    grad_pre_wide = gelu_pull(grad_hidden)[0]
    grad_pre = grad_pre_wide.astype(LOW)
    grad_second = scatter_rows(times_t(grad_pre, weight_expand))
    branch_b = scatter_rows(times_t(hidden, weight_shrink)) + shrink_shift
    block_output = from_owner((middle + ff_scale * branch_b).astype(LOW), packed_shape)

    shrink_grad = inner_rows(grad_b_all, hidden)
    expand_grad = inner_rows(second_all, grad_pre)
    wide_grads = jnp.concatenate((shrink_grad, expand_grad), axis=1).astype(LOW)
    wide_grads = lax.psum_scatter(wide_grads, "gy", scatter_dimension=0, tiled=True).astype(WIDE)

    grad_middle = grad + norm_backward(grad_second, gain_two, second_hat, second_rstd)
    grad_a = grad_middle * attn_scale
    grad_a_all = gather_rows(grad_a.astype(LOW))
    grad_attended = times(grad_a_all, weight_out).astype(LOW)
    grad_query, grad_keys, grad_values = attend_backward(
        query, keys, values, grad_attended, log_total, bias
    )
    grad_mixed = jnp.concatenate((grad_query, grad_keys, grad_values), axis=1)
    grad_first = scatter_rows(times_t(grad_mixed, weight_in))
    input_gradient = grad_middle + norm_backward(grad_first, gain_one, first_hat, first_rstd)
    input_gradient = from_owner(input_gradient.astype(LOW), packed_shape).astype(WIDE)

    out_grad = inner_rows(grad_a_all, attended)
    in_grad = inner_rows(first_all, grad_mixed)
    head_grads = jnp.concatenate((out_grad, in_grad), axis=1).astype(LOW)
    head_grads = lax.psum_scatter(head_grads, "gy", scatter_dimension=0, tiled=True).astype(WIDE)

    sums = token_sums(
        jnp.stack(
            [
                jnp.sum(item, axis=0)
                for item in (
                    grad_a,
                    grad_middle * branch_a,
                    grad_first * first_hat,
                    grad_first,
                    grad_second * second_hat,
                    grad_second,
                    grad_b,
                    grad * branch_b,
                )
            ]
        )
    )
    biases = image_sums(
        jnp.concatenate(
            (
                jnp.sum(grad_query.astype(WIDE), axis=0),
                jnp.sum(grad_values.astype(WIDE), axis=0),
                jnp.sum(grad_pre.astype(WIDE), axis=0),
            )
        )
    )
    return (
        block_output,
        input_gradient,
        head_grads[:, head_cols:].reshape(-1, 3, head_cols),
        biases[:head_cols],
        biases[head_cols : 2 * head_cols],
        head_grads[:, :head_cols].T,
        sums[0],
        sums[1],
        sums[2],
        sums[3],
        sums[4],
        sums[5],
        wide_grads[:, hidden_cols:],
        biases[2 * head_cols :],
        wide_grads[:, :hidden_cols].T,
        sums[6],
        sums[7],
    )


def solution(mesh):
    rows = P("gx", "gy", None)
    wide, heads = P("gy"), P("gx")
    placed = (
        rows, P("gy", None, "gx"), heads, heads, P("gx", "gy"), wide, wide, wide, wide, wide, wide,
        P("gy", "gx"), heads, P("gx", "gy"), wide, wide, rows,
    )
    results = (
        rows, rows, P("gy", None, "gx"), heads, heads, P("gx", "gy"), wide, wide, wide, wide, wide,
        wide, P("gy", "gx"), heads, P("gx", "gy"), wide, wide,
    )
    return jax.shard_map(
        on_device, mesh=mesh, in_specs=placed, out_specs=results, check_vma=False
    )
```

time: 2870 us -> 692 us (0.24)
  waiting for transfers between devices: 1740 us -> 186 us
  blocking collectives: 508 us -> 89.4 us
  local copies, waits for them, and re-layouts: 292 us -> 34.3 us
  starting transfers between devices: 53.9 us -> 136 us
  matrix products: 193 us -> 157 us
    all_gather x13 -> x2, waiting for transfers between devices: 1300 us -> 36.6 us  [the longest x1 36.6 us: on_device(): later = lax.all_gather(later, 'gy', axis=0, tiled=True)]
    all_to_all x8 -> x3, waiting for transfers between devices: 444 us -> 4.69 us  [the longest x1 4.69 us: to_owner(): lax.all_to_all(blocks, 'gy', split_axis=0, concat_axis=0, tiled=True)]
    all_gather x3 -> x1, blocking collectives: 354 us -> 63.5 us  [on_device(): small = lax.all_gather(small, 'gy', axis=1, tiled=True)]
    all_to_all x16 -> x0, local copies, waits for them, and re-layouts: 194 us -> none  [the longest x8 163 us: row_sums(): lax.all_to_all(whole, 'gx', split_axis=0, concat_axis=1, tiled=True)]
    psum x5 -> x0, blocking collectives: 154 us -> none  [the longest x4 148 us: width_stats(): return lax.psum((first_term, second_term), 'gy')]
    ppermute x0 -> x28, waiting for transfers between devices: none -> 144 us  [the longest x24 144 us: swap(): return lax.ppermute(values, axis, [(k, k ^ bit) for k in range(size)])]
    unnamed x104 -> x106, local copies, waits for them, and re-layouts: 93.5 us -> 19.8 us
    ppermute x0 -> x28, starting transfers between devices: none -> 46 us  [the longest x24 29.2 us: swap(): return lax.ppermute(values, axis, [(k, k ^ bit) for k in range(size)])]
  transfers between devices with their start and end apart: 21 -> 35, of which waited for: 11 -> 16; matrix products, arithmetic and copies ran while one was open for 8% -> 31% of each run, Pallas kernels for 0% -> 0%
where the time goes in v1:
time: 692 us; the launch traced here: 681 us
  waiting for transfers between devices  186 us (27%)
  matrix products  157 us (23%)
  starting transfers between devices  136 us (20%)
  blocking collectives  89.4 us (13%)
  other arithmetic  62.9 us (9%)
  local copies, waits for them, and re-layouts  34.3 us (5%)
  between operations  15.3 us (2%)
    ppermute x24, waiting for transfers between devices, swap(): return lax.ppermute(values, axis, [(k, k ^ bit) for k in range(size)])  144 us
    all_to_all x2, starting transfers between devices, from_owner(): lax.all_to_all(blocks, 'gy', split_axis=0, concat_axis=0, tiled=True)  85.6 us
    all_gather x1, blocking collectives, on_device(): small = lax.all_gather(small, 'gy', axis=1, tiled=True)  63.5 us
    dot_general x4, matrix products, times(): return jnp.dot(left, right, preferred_element_type=WIDE)  48.6 us
    all_gather x1, waiting for transfers between devices, on_device(): later = lax.all_gather(later, 'gy', axis=0, tiled=True)  36.6 us
    ppermute x24, starting transfers between devices, swap(): return lax.ppermute(values, axis, [(k, k ^ bit) for k in range(size)])  29.2 us
    convert_element_type x1, other arithmetic, attend_backward(): grad_scores = (probs * (grad_probs - jnp.sum(probs * grad_probs, axis=-1,...  27.3 us
    all_to_all x1, blocking collectives, to_owner(): lax.all_to_all(blocks, 'gy', split_axis=0, concat_axis=0, tiled=True)  25.9 us
  transfers between devices with their start and end apart: 35, of which 16 were waited for; matrix products, arithmetic and copies ran while one was open for 31% of the time, Pallas kernels for 0%

profile of v1, /device:TPU:0, one launch (start us, length us, event | category | flops | bytes accessed | tf_op | source)
XLA Modules:
  0.0 680.9 jit_solution(9877071245981006273)
XLA Ops:
  8.7 25.9 %all_to_all.20 = bf16[8,352,128]{2,1,0:T(8,128)(2,1)S(1)} all-to-all(bf16[8,352,128]{2,1,0:T(8,128)(2,1)S(1)} %bitcast.158), channel_id=1, replica_groups=mesh['gx'=4,'gy'=8] {'gy'}, dimensions={0} | all-to-all | bytes 1441792 | tf_op jit(solution)/shard_map/all_to_all | solution.py:62
  36.5 63.5 %all_gather.9 = f32[8,1024]{1,0:T(8,128)S(1)} all-gather(f32[8,128]{1,0:T(8,128)S(1)} %stack.62), channel_id=1, replica_groups=mesh['gx'=4,'gy'=8] {'gy'}, dimensions={1}, use_global_device_ids=true | all-gather | bytes 36864 | tf_op jit(solution)/shard_map/all_gather | solution.py:209
  102.1 10.5 %collective-permute-done.1 = bf16[352,1024]{1,0:T(8,128)(2,1)S(1)} collective-permute-done((bf16[352,1024]{1,0:T(8,128)(2,1)S(1)}, bf16[352,1024]{1,0:T(8,128)(2,1)S(1)}, u32[]{:S(2)}, u32[]{:S(2)}) %collective-permute-start.1) | collective-permute-done | bytes 720928 | tf_op jit(solution)/shard_map/ppermute | solution.py:16
  116.8 4.7 fusion.38
  121.9 12.8 %fusion.65 = (f32[4,1408]{1,0:T(4,128)S(1)}, f32[4,1408,1408]{1,2,0:T(8,128)}) fusion(f32[1408]{0:T(1024)S(1)} %concatenate.51, bf16[1408,4,64]{0,2,1:T(8,128)(2,1)S(1)} %bitcast.154, bf16[1408,4,64]{0,2,1:T(8,128)(2,1)S(1)} %bitcast.150), kind=kOutput, calls=%fused_computation.175 | convolution fusion | flops 1038805504 | bytes 33189376 | tf_op jit(solution)/shard_map/qhd,khd->hqk/dot_general | solution.py:113
  134.7 12.9 %fusion.1 = f32[4,1408]{1,0:T(4,128)S(1)} fusion(f32[4,1408,1408]{1,2,0:T(8,128)} %get-tuple-element.116, f32[4,1408]{1,0:T(4,128)S(1)} %get-tuple-element.115), kind=kLoop, calls=%fused_computation.7 | loop fusion | flops 15854080 | bytes 31764480 | tf_op jit(solution)/shard_map/reduce_sum | solution.py:117
  147.5 13.4 %fusion.18 = bf16[4,64,1408]{2,1,0:T(8,128)(2,1)S(1)} fusion(bf16[1408,4,64]{0,2,1:T(8,128)(2,1)S(1)} %bitcast.159, f32[4,1408,1408]{1,2,0:T(8,128)} %get-tuple-element.116, f32[4,1408]{1,0:T(4,128)S(1)} %fusion.1, f32[4,1408]{1,0:T(4,128)S(1)} %get-tuple-element.115), kind=kOutput, calls=%fused_computation.49 | convolution fusion | flops 1039171584 | bytes 33206272 | tf_op jit(solution)/shard_map/hqk,khd->qhd/dot_general | solution.py:119
  160.9 36.6 %all-gather.5.cloned.1.call-done = bf16[1024,2304]{0,1:T(8,128)(2,1)} async-done(((bf16[128,2304]{0,1:T(8,128)(2,1)}), bf16[1024,2304]{0,1:T(8,128)(2,1)}) %all-gather.5.cloned.1.call-update) | async-done | bytes 4718608 | tf_op jit(solution)/shard_map/all_gather | solution.py:216
  209.1 4.2 all-to-all-start.2
  213.6 9.9 %collective-permute-done.4 = bf16[352,1024]{1,0:T(8,128)(2,1)S(1)} collective-permute-done((bf16[352,1024]{1,0:T(8,128)(2,1)S(1)}, bf16[352,1024]{1,0:T(8,128)(2,1)S(1)}, u32[]{:S(2)}, u32[]{:S(2)}) %collective-permute-start.4) | collective-permute-done | bytes 720928 | tf_op jit(solution)/shard_map/ppermute | solution.py:16
  227.7 4.7 all-to-all-done.2
  234.1 23.9 %collective-permute-done.5 = bf16[352,1024]{1,0:T(8,128)(2,1)} collective-permute-done((bf16[352,1024]{1,0:T(8,128)(2,1)S(1)}, bf16[352,1024]{1,0:T(8,128)(2,1)}, u32[]{:S(2)}, u32[]{:S(2)}) %collective-permute-start.5) | collective-permute-done | bytes 720928 | tf_op jit(solution)/shard_map/ppermute | solution.py:16
  262.1 16.8 %collective-permute-done.11 = bf16[352,1024]{1,0:T(8,128)(2,1)S(1)} collective-permute-done((bf16[352,1024]{1,0:T(8,128)(2,1)S(1)}, bf16[352,1024]{1,0:T(8,128)(2,1)S(1)}, u32[]{:S(2)}, u32[]{:S(2)}) %collective-permute-start.11) | collective-permute-done | bytes 720928 | tf_op jit(solution)/shard_map/ppermute | solution.py:16
  279.1 20.7 %multiply_convert_fusion.1 = (bf16[1408,1024]{1,0:T(8,128)(2,1)S(1)}, f32[1408,1024]{1,0:T(8,128)}, f32[1408,1024]{1,0:T(8,128)}) fusion(f32[1024]{0:T(1024)S(1)} %copy-done.46, bf16[1024,2304]{0,1:T(8,128)(2,1)} %all-gather.5.cloned.1.call-done, bf16[704,1024]{1,0:T(8,128)(2,1)S(1)} %collective-permute-done.6, ...), kind=kOutput, calls=%fused_computation.16 | convolution fusion | flops 3056599040 | bytes 19402752 | tf_op jit(solution)/shard_map/dot_general | solution.py:93
  299.8 20.5 %convert_reduce_fusion = (f32[1024]{0:T(1024)S(1)}, bf16[1408,1024]{1,0:T(8,128)(2,1)S(1)}) fusion(f32[1408,1024]{1,0:T(8,128)} %get-tuple-element.84, bf16[1024,2304]{0,1:T(8,128)(2,1)S(1)} %bitcast.188, bf16[704,1024]{1,0:T(8,128)(2,1)S(1)} %collective-permute-done.12, bf16[352,1024]{1,0:T(8,128)(2,1)S(1)} %collective-permute-done.11, ...), kind=kOutput, calls=%fused_computation.14 | convolution fusion | flops 2985950208 | bytes 19406848 | tf_op jit(solution)/shard_map/dot_general | solution.py:93
  333.9 13.9 %collective-permute-done.14 = bf16[352,1024]{1,0:T(8,128)(2,1)S(1)} collective-permute-done((bf16[352,1024]{1,0:T(8,128)(2,1)S(1)}, bf16[352,1024]{1,0:T(8,128)(2,1)S(1)}, u32[]{:S(2)}, u32[]{:S(2)}) %collective-permute-start.14) | collective-permute-done | bytes 720928 | tf_op jit(solution)/shard_map/ppermute | solution.py:16
  348.6 14.3 %collective-permute-done.8 = bf16[352,1024]{1,0:T(8,128)(2,1)S(1)} collective-permute-done((bf16[352,1024]{1,0:T(8,128)(2,1)S(1)}, bf16[352,1024]{1,0:T(8,128)(2,1)S(1)}, u32[]{:S(2)}, u32[]{:S(2)}) %collective-permute-start.8) | collective-permute-done | bytes 720928 | tf_op jit(solution)/shard_map/ppermute | solution.py:16
  368.7 16.0 %collective-permute-done.15 = bf16[352,1024]{1,0:T(8,128)(2,1)S(1)} collective-permute-done((bf16[352,1024]{1,0:T(8,128)(2,1)S(1)}, bf16[352,1024]{1,0:T(8,128)(2,1)S(1)}, u32[]{:S(2)}, u32[]{:S(2)}) %collective-permute-start.15) | collective-permute-done | bytes 720928 | tf_op jit(solution)/shard_map/ppermute | solution.py:16
  389.8 4.9 convolution_convert_fusion.1
  397.2 6.5 copy.73
  406.6 21.0 %multiply_reduce_fusion = (f32[4,1408]{1,0:T(4,128)S(1)}, f32[4,1408,1408]{1,2,0:T(8,128)}) fusion(f32[4,1408,1408]{1,2,0:T(8,128)} %get-tuple-element.116, f32[4,1408]{1,0:T(4,128)S(1)} %log_add_fusion, bf16[1408,4,64]{0,2,1:T(8,128)(2,1)S(1)} %bitcast.156, bf16[1408,4,64]{0,2,1:T(8,128)(2,1)S(1)} %bitcast.160), kind=kOutput, calls=%fused_computation.3 | convolution fusion | flops 1038805504 | bytes 64925696 | tf_op jit(solution)/shard_map/qhd,khd->hqk/dot_general | solution.py:127
  427.6 27.3 %multiply_convert_fusion = bf16[4,1408,1408]{1,2,0:T(8,128)(2,1)} fusion(f32[4,1408,1408]{1,2,0:T(8,128)} %get-tuple-element.119, f32[4,1408,1408]{1,2,0:T(8,128)} %get-tuple-element.116, f32[4,1408]{1,0:T(4,128)S(1)} %get-tuple-element.118, f32[4,1408]{1,0:T(4,128)S(1)} %log_add_fusion), kind=kLoop, calls=%fused_computation.2 | loop fusion | flops 31719424 | bytes 79343616 | tf_op jit(solution)/shard_map/convert_element_type | solution.py:130
  454.9 11.5 %fusion.17 = bf16[4,64,1408]{2,1,0:T(8,128)(2,1)} fusion(bf16[1408,4,64]{0,2,1:T(8,128)(2,1)S(1)} %bitcast.155, bf16[4,1408,1408]{1,2,0:T(8,128)(2,1)} %multiply_convert_fusion), kind=kOutput, calls=%fused_computation.48 | convolution fusion | flops 1015742464 | bytes 17301504 | tf_op jit(solution)/shard_map/hqk,qhd->khd/dot_general | solution.py:132
  466.4 8.4 %convert_reduce_fusion.3 = (f32[4,64]{1,0:T(4,128)S(1)}, bf16[4,64,1408]{2,1,0:T(8,128)(2,1)S(1)}) fusion(bf16[1408,4,64]{0,2,1:T(8,128)(2,1)S(1)} %bitcast.151, bf16[4,1408,1408]{1,2,0:T(8,128)(2,1)} %multiply_convert_fusion), kind=kOutput, calls=%fused_computation.101 | convolution fusion | flops 1016463104 | bytes 17302528 | tf_op jit(solution)/shard_map/hqk,khd->qhd/dot_general | solution.py:131
  474.8 13.9 %convert_reduce_fusion.2 = (f32[4,64]{1,0:T(4,128)S(1)}, bf16[4,64,1408]{2,1,0:T(8,128)(2,1)}) fusion(bf16[1408,4,64]{0,2,1:T(8,128)(2,1)S(1)} %bitcast.157, f32[4,1408,1408]{1,2,0:T(8,128)} %get-tuple-element.116, f32[4,1408]{1,0:T(4,128)S(1)} %log_add_fusion), kind=kOutput, calls=%fused_computation.100 | convolution fusion | flops 1031962368 | bytes 33184768 | tf_op jit(solution)/shard_map/hqk,qhd->khd/dot_general | solution.py:133
  488.7 4.3 fusion.39
  495.2 7.3 %collective-permute-start.9 = (bf16[8,352,128]{2,1,0:T(8,128)(2,1)}, bf16[8,352,128]{2,1,0:T(8,128)(2,1)}, u32[]{:S(2)}, u32[]{:S(2)}) collective-permute-start(bf16[8,352,128]{2,1,0:T(8,128)(2,1)} %bitcast.149), channel_id=1, source_target_pairs={{0,0},{8,1},{16,2},{24,3},{1,4},{9,5},{17,6},{25,7},{2,8},{10,9},{... | collective-permute-start | bytes 2162696 | tf_op jit(solution)/shard_map/ppermute | solution.py:72
  516.9 50.9 %all-to-all-start.1 = ((bf16[8,352,128]{2,1,0:T(8,128)(2,1)}), bf16[8,352,128]{2,1,0:T(8,128)(2,1)S(1)}, u32[]{:S(2)}, u32[]{:S(2)}) async-start(bf16[8,352,128]{2,1,0:T(8,128)(2,1)} %collective-permute-done.9), calls=%async_computation.1 | async-start | bytes 1441792 | tf_op jit(solution)/shard_map/all_to_all | solution.py:73
  576.5 6.9 %collective-permute-start.19 = (bf16[8,352,128]{2,1,0:T(8,128)(2,1)}, bf16[8,352,128]{2,1,0:T(8,128)(2,1)}, u32[]{:S(2)}, u32[]{:S(2)}) collective-permute-start(bf16[8,352,128]{2,1,0:T(8,128)(2,1)} %bitcast_bitcast_fusion), channel_id=1, source_target_pairs={{0,0},{8,1},{16,2},{24,3},{1,4},{9,5},{17,6},{25,7},{2,8},{10,9},{... | collective-permute-start | bytes 2162696 | tf_op jit(solution)/shard_map/ppermute | solution.py:72
  583.4 21.8 %collective-permute-done.23 = f32[4,8,128]{2,1,0:T(8,128)S(1)} collective-permute-done((f32[4,8,128]{2,1,0:T(8,128)S(1)}, f32[4,8,128]{2,1,0:T(8,128)S(1)}, u32[]{:S(2)}, u32[]{:S(2)}) %collective-permute-start.23) | collective-permute-done | bytes 16416 | tf_op jit(solution)/shard_map/ppermute | solution.py:16
  607.4 34.7 %all-to-all-start.3 = ((bf16[8,352,128]{2,1,0:T(8,128)(2,1)}), bf16[8,352,128]{2,1,0:T(8,128)(2,1)S(1)}, u32[]{:S(2)}, u32[]{:S(2)}) async-start(bf16[8,352,128]{2,1,0:T(8,128)(2,1)} %collective-permute-done.19), calls=%async_computation.3 | async-start | bytes 1441792 | tf_op jit(solution)/shard_map/all_to_all | solution.py:73
  651.8 9.3 %collective-permute-done.22 = f32[1536]{0:T(1024)S(1)} collective-permute-done((f32[1536]{0:T(1024)S(1)}, f32[1536]{0:T(1024)S(1)}, u32[]{:S(2)}, u32[]{:S(2)}) %collective-permute-start.22) | collective-permute-done | bytes 6176 | tf_op jit(solution)/shard_map/ppermute | solution.py:16
  (248 shorter events, 111.9 us)
Async XLA Ops:
  7.3 108.4 %all-gather.3.cloned.1.call-start = ((), (), s32[]{:S(2)}) async-start(), calls=%async_computation.6 | async-start | bytes 1769472 | tf_op jit(solution)/shard_map/all_gather | solution.py:214
  34.6 66.0 %collective-permute-start = (bf16[8,352,128]{2,1,0:T(8,128)(2,1)S(1)}, bf16[8,352,128]{2,1,0:T(8,128)(2,1)S(1)}, u32[]{:S(2)}, u32[]{:S(2)}) collective-permute-start(bf16[8,352,128]{2,1,0:T(8,128)(2,1)S(1)} %all_to_all.20), channel_id=1, source_target_pairs={{0,0},{1,8},{2,16},{3,24},{4,1},{5,9},{6,17},{7,25},{8,2},{9,10},{... | collective-permute-start | bytes 2162696 | tf_op jit(solution)/shard_map/ppermute | solution.py:63
  36.3 161.2 %all-gather.5.cloned.1.call-start = ((), (), s32[]{:S(2)}) async-start(), calls=%async_computation.7 | async-start | bytes 5308416 | tf_op jit(solution)/shard_map/all_gather | solution.py:216
  101.3 11.4 %collective-permute-start.1 = (bf16[352,1024]{1,0:T(8,128)(2,1)S(1)}, bf16[352,1024]{1,0:T(8,128)(2,1)S(1)}, u32[]{:S(2)}, u32[]{:S(2)}) collective-permute-start(bf16[352,1024]{1,0:T(8,128)(2,1)S(1)} %add_convert_fusion.4), channel_id=1, source_target_pairs={{0,16},{8,24},{16,0},{24,8},{1,17},{9,25},{17,1},{25,9},{2,18},{10... | collective-permute-start | bytes 2162696 | tf_op jit(solution)/shard_map/ppermute | solution.py:16
  205.3 18.2 %collective-permute-start.4 = (bf16[352,1024]{1,0:T(8,128)(2,1)S(1)}, bf16[352,1024]{1,0:T(8,128)(2,1)S(1)}, u32[]{:S(2)}, u32[]{:S(2)}) collective-permute-start(bf16[352,1024]{1,0:T(8,128)(2,1)S(1)} %slice.373), channel_id=1, source_target_pairs={{0,16},{8,24},{16,0},{24,8},{1,17},{9,25},{17,1},{25,9},{2,18},{10... | collective-permute-start | bytes 2162696 | tf_op jit(solution)/shard_map/ppermute | solution.py:16
  209.1 23.2 %all-to-all-start.2 = ((bf16[8,352,128]{2,1,0:T(8,128)(2,1)}), bf16[8,352,128]{2,1,0:T(8,128)(2,1)}, u32[]{:S(2)}, u32[]{:S(2)}) async-start(bf16[8,352,128]{2,1,0:T(8,128)(2,1)} %bitcast.28), calls=%async_computation.2 | async-start | bytes 1441792 | tf_op jit(solution)/shard_map/all_to_all | solution.py:62
  213.3 452.0 %reduce-scatter.9.cloned.1.call-start = ((), (), s32[]{:S(2)}) async-start(), calls=%async_computation.9 | async-start | bytes 4718592
  226.1 31.9 %collective-permute-start.5 = (bf16[352,1024]{1,0:T(8,128)(2,1)S(1)}, bf16[352,1024]{1,0:T(8,128)(2,1)}, u32[]{:S(2)}, u32[]{:S(2)}) collective-permute-start(bf16[352,1024]{1,0:T(8,128)(2,1)S(1)} %add_convert_fusion.3), channel_id=1, source_target_pairs={{0,16},{8,24},{16,0},{24,8},{1,17},{9,25},{17,1},{25,9},{2,18},{10... | collective-permute-start | bytes 2162696 | tf_op jit(solution)/shard_map/ppermute | solution.py:16
  232.3 26.9 %collective-permute-start.10 = (bf16[8,352,128]{2,1,0:T(8,128)(2,1)}, bf16[8,352,128]{2,1,0:T(8,128)(2,1)S(1)}, u32[]{:S(2)}, u32[]{:S(2)}) collective-permute-start(bf16[8,352,128]{2,1,0:T(8,128)(2,1)} %all-to-all-done.2), channel_id=1, source_target_pairs={{0,0},{1,8},{2,16},{3,24},{4,1},{5,9},{6,17},{7,25},{8,2},{9,10},{... | collective-permute-start | bytes 2162696 | tf_op jit(solution)/shard_map/ppermute | solution.py:63
  259.2 19.9 %collective-permute-start.6 = (bf16[704,1024]{1,0:T(8,128)(2,1)S(1)}, bf16[704,1024]{1,0:T(8,128)(2,1)S(1)}, u32[]{:S(2)}, u32[]{:S(2)}) collective-permute-start(bf16[704,1024]{1,0:T(8,128)(2,1)S(1)} %pad_maximum_fusion.8), channel_id=1, source_target_pairs={{0,8},{8,0},{16,24},{24,16},{1,9},{9,1},{17,25},{25,17},{2,10},{10... | collective-permute-start | bytes 4325384 | tf_op jit(solution)/shard_map/ppermute | solution.py:16
  259.4 19.4 %collective-permute-start.11 = (bf16[352,1024]{1,0:T(8,128)(2,1)S(1)}, bf16[352,1024]{1,0:T(8,128)(2,1)S(1)}, u32[]{:S(2)}, u32[]{:S(2)}) collective-permute-start(bf16[352,1024]{1,0:T(8,128)(2,1)S(1)} %fusion.31), channel_id=1, source_target_pairs={{0,16},{8,24},{16,0},{24,8},{1,17},{9,25},{17,1},{25,9},{2,18},{10... | collective-permute-start | bytes 2162696 | tf_op jit(solution)/shard_map/ppermute | solution.py:16
  279.0 20.8 %collective-permute-start.12 = (bf16[704,1024]{1,0:T(8,128)(2,1)S(1)}, bf16[704,1024]{1,0:T(8,128)(2,1)S(1)}, u32[]{:S(2)}, u32[]{:S(2)}) collective-permute-start(bf16[704,1024]{1,0:T(8,128)(2,1)S(1)} %pad_maximum_fusion.9), channel_id=1, source_target_pairs={{0,8},{8,0},{16,24},{24,16},{1,9},{9,1},{17,25},{25,17},{2,10},{10... | collective-permute-start | bytes 4325384 | tf_op jit(solution)/shard_map/ppermute | solution.py:16
  323.7 4.3 collective-permute-start.13
  328.8 19.0 %collective-permute-start.14 = (bf16[352,1024]{1,0:T(8,128)(2,1)S(1)}, bf16[352,1024]{1,0:T(8,128)(2,1)S(1)}, u32[]{:S(2)}, u32[]{:S(2)}) collective-permute-start(bf16[352,1024]{1,0:T(8,128)(2,1)S(1)} %slice.371), channel_id=1, source_target_pairs={{0,16},{8,24},{16,0},{24,8},{1,17},{9,25},{17,1},{25,9},{2,18},{10... | collective-permute-start | bytes 2162696 | tf_op jit(solution)/shard_map/ppermute | solution.py:16
  332.0 30.8 %collective-permute-start.8 = (bf16[352,1024]{1,0:T(8,128)(2,1)S(1)}, bf16[352,1024]{1,0:T(8,128)(2,1)S(1)}, u32[]{:S(2)}, u32[]{:S(2)}) collective-permute-start(bf16[352,1024]{1,0:T(8,128)(2,1)S(1)} %slice.372), channel_id=1, source_target_pairs={{0,16},{8,24},{16,0},{24,8},{1,17},{9,25},{17,1},{25,9},{2,18},{10... | collective-permute-start | bytes 2162696 | tf_op jit(solution)/shard_map/ppermute | solution.py:16
  366.9 17.8 %collective-permute-start.15 = (bf16[352,1024]{1,0:T(8,128)(2,1)S(1)}, bf16[352,1024]{1,0:T(8,128)(2,1)S(1)}, u32[]{:S(2)}, u32[]{:S(2)}) collective-permute-start(bf16[352,1024]{1,0:T(8,128)(2,1)S(1)} %multiply_convert_fusion.2), channel_id=1, source_target_pairs={{0,16},{8,24},{16,0},{24,8},{1,17},{9,25},{17,1},{25,9},{2,18},{10... | collective-permute-start | bytes 2162696 | tf_op jit(solution)/shard_map/ppermute | solution.py:16
  386.1 17.7 %collective-permute-start.16 = (bf16[704,1024]{1,0:T(8,128)(2,1)}, bf16[704,1024]{1,0:T(8,128)(2,1)}, u32[]{:S(2)}, u32[]{:S(2)}) collective-permute-start(bf16[704,1024]{1,0:T(8,128)(2,1)} %pad_maximum_fusion.10), channel_id=1, source_target_pairs={{0,8},{8,0},{16,24},{24,16},{1,9},{9,1},{17,25},{25,17},{2,10},{10... | collective-permute-start | bytes 4325384 | tf_op jit(solution)/shard_map/ppermute | solution.py:16
  403.8 267.4 %reduce-scatter.7.cloned.1.call-start = ((), (), s32[]{:S(2)}) async-start(), calls=%async_computation.8 | async-start | bytes 2359296
  493.3 9.2 %collective-permute-start.17 = (bf16[704,1024]{1,0:T(8,128)(2,1)S(1)}, bf16[704,1024]{1,0:T(8,128)(2,1)S(1)}, u32[]{:S(2)}, u32[]{:S(2)}) collective-permute-start(bf16[704,1024]{1,0:T(8,128)(2,1)S(1)} %slice.366), channel_id=1, source_target_pairs={{0,8},{8,0},{16,24},{24,16},{1,9},{9,1},{17,25},{25,17},{2,10},{10... | collective-permute-start | bytes 4325384 | tf_op jit(solution)/shard_map/ppermute | solution.py:16
  495.2 21.7 %collective-permute-start.9 = (bf16[8,352,128]{2,1,0:T(8,128)(2,1)}, bf16[8,352,128]{2,1,0:T(8,128)(2,1)}, u32[]{:S(2)}, u32[]{:S(2)}) collective-permute-start(bf16[8,352,128]{2,1,0:T(8,128)(2,1)} %bitcast.149), channel_id=1, source_target_pairs={{0,0},{8,1},{16,2},{24,3},{1,4},{9,5},{17,6},{25,7},{2,8},{10,9},{... | collective-permute-start | bytes 2162696 | tf_op jit(solution)/shard_map/ppermute | solution.py:72
  505.7 62.2 %collective-permute-start.18 = (bf16[352,1024]{1,0:T(8,128)(2,1)}, bf16[352,1024]{1,0:T(8,128)(2,1)}, u32[]{:S(2)}, u32[]{:S(2)}) collective-permute-start(bf16[352,1024]{1,0:T(8,128)(2,1)} %slice.370), channel_id=1, source_target_pairs={{0,16},{8,24},{16,0},{24,8},{1,17},{9,25},{17,1},{25,9},{2,18},{10... | collective-permute-start | bytes 2162696 | tf_op jit(solution)/shard_map/ppermute | solution.py:16
  516.9 90.5 %all-to-all-start.1 = ((bf16[8,352,128]{2,1,0:T(8,128)(2,1)}), bf16[8,352,128]{2,1,0:T(8,128)(2,1)S(1)}, u32[]{:S(2)}, u32[]{:S(2)}) async-start(bf16[8,352,128]{2,1,0:T(8,128)(2,1)} %collective-permute-done.9), calls=%async_computation.1 | async-start | bytes 1441792 | tf_op jit(solution)/shard_map/all_to_all | solution.py:73
  570.4 34.8 %collective-permute-start.23 = (f32[4,8,128]{2,1,0:T(8,128)S(1)}, f32[4,8,128]{2,1,0:T(8,128)S(1)}, u32[]{:S(2)}, u32[]{:S(2)}) collective-permute-start(f32[4,8,128]{2,1,0:T(8,128)S(1)} %slice_select_fusion), channel_id=1, source_target_pairs={{0,4},{1,5},{2,6},{3,7},{4,0},{5,1},{6,2},{7,3},{8,12},{9,13},{10,... | collective-permute-start | bytes 49160 | tf_op jit(solution)/shard_map/ppermute | solution.py:16
  576.5 30.9 %collective-permute-start.19 = (bf16[8,352,128]{2,1,0:T(8,128)(2,1)}, bf16[8,352,128]{2,1,0:T(8,128)(2,1)}, u32[]{:S(2)}, u32[]{:S(2)}) collective-permute-start(bf16[8,352,128]{2,1,0:T(8,128)(2,1)} %bitcast_bitcast_fusion), channel_id=1, source_target_pairs={{0,0},{8,1},{16,2},{24,3},{1,4},{9,5},{17,6},{25,7},{2,8},{10,9},{... | collective-permute-start | bytes 2162696 | tf_op jit(solution)/shard_map/ppermute | solution.py:72
  583.3 22.0 %collective-permute-start.20 = (f32[1536]{0:T(1024)S(1)}, f32[1536]{0:T(1024)S(1)}, u32[]{:S(2)}, u32[]{:S(2)}) collective-permute-start(f32[1536]{0:T(1024)S(1)} %pad_maximum_fusion.22), channel_id=1, source_target_pairs={{0,1},{1,0},{2,3},{3,2},{4,5},{5,4},{6,7},{7,6},{8,9},{9,8},{10,11... | collective-permute-start | bytes 18440 | tf_op jit(solution)/shard_map/ppermute | solution.py:16
  605.2 36.9 %collective-permute-start.24 = (f32[2,8,128]{2,1,0:T(8,128)S(1)}, f32[2,8,128]{2,1,0:T(8,128)S(1)}, u32[]{:S(2)}, u32[]{:S(2)}) collective-permute-start(f32[2,8,128]{2,1,0:T(8,128)S(1)} %slice_select_fusion.1), channel_id=1, source_target_pairs={{0,2},{1,3},{2,0},{3,1},{4,6},{5,7},{6,4},{7,5},{8,10},{9,11},{10,... | collective-permute-start | bytes 24584 | tf_op jit(solution)/shard_map/ppermute | solution.py:16
  605.3 38.9 %collective-permute-start.21 = (f32[1536]{0:T(1024)S(1)}, f32[1536]{0:T(1024)S(1)}, u32[]{:S(2)}, u32[]{:S(2)}) collective-permute-start(f32[1536]{0:T(1024)S(1)} %fusion.58), channel_id=1, source_target_pairs={{0,2},{1,3},{2,0},{3,1},{4,6},{5,7},{6,4},{7,5},{8,10},{9,11},{10,... | collective-permute-start | bytes 18440 | tf_op jit(solution)/shard_map/ppermute | solution.py:16
  607.4 61.2 %all-to-all-start.3 = ((bf16[8,352,128]{2,1,0:T(8,128)(2,1)}), bf16[8,352,128]{2,1,0:T(8,128)(2,1)S(1)}, u32[]{:S(2)}, u32[]{:S(2)}) async-start(bf16[8,352,128]{2,1,0:T(8,128)(2,1)} %collective-permute-done.19), calls=%async_computation.3 | async-start | bytes 1441792 | tf_op jit(solution)/shard_map/all_to_all | solution.py:73
  642.2 4.7 collective-permute-start.25
  644.2 16.9 %collective-permute-start.22 = (f32[1536]{0:T(1024)S(1)}, f32[1536]{0:T(1024)S(1)}, u32[]{:S(2)}, u32[]{:S(2)}) collective-permute-start(f32[1536]{0:T(1024)S(1)} %add.236), channel_id=1, source_target_pairs={{0,4},{1,5},{2,6},{3,7},{4,0},{5,1},{6,2},{7,3},{8,12},{9,13},{10,... | collective-permute-start | bytes 18440 | tf_op jit(solution)/shard_map/ppermute | solution.py:16
  646.9 14.2 %collective-permute-start.26 = (f32[8,128]{1,0:T(8,128)S(1)}, f32[8,128]{1,0:T(8,128)S(1)}, u32[]{:S(2)}, u32[]{:S(2)}) collective-permute-start(f32[8,128]{1,0:T(8,128)S(1)} %add_bitcast_fusion), channel_id=1, source_target_pairs={{0,8},{8,0},{16,24},{24,16},{1,9},{9,1},{17,25},{25,17},{2,10},{10... | collective-permute-start | bytes 12296 | tf_op jit(solution)/shard_map/ppermute | solution.py:16
  661.1 3.7 collective-permute-start.27
  (52 other events, 1209.6 us)
Sparse Core Ops, SparseCore 0:
  36.4 54.7 all-gather.2
  115.6 81.8 all-gather.4
  403.9 92.3 reduce-scatter.8
  516.8 116.2 reduce-scatter.6

commit v2 on v1

v2 whole, which is shorter than its diff:
```python
import math

import jax
import jax.numpy as jnp
from jax import lax
from jax.experimental import pallas as pl
from jax.experimental.pallas import tpu as pltpu
from jax.sharding import PartitionSpec as P

D = 1024
HEAD_DIM = 64
SEQ = 1370
SCALE = HEAD_DIM ** (-0.5)
LOW = jnp.bfloat16
WIDE = jnp.float32


def swap(values, axis, bit):
    size = lax.axis_size(axis)
    return lax.ppermute(values, axis, [(k, k ^ bit) for k in range(size)])


def gather_rows(values):
    bit = lax.axis_size("gx") // 2
    while bit:
        values = jnp.concatenate((values, swap(values, "gx", bit)), axis=0)
        bit //= 2
    return values


def slot_blocks(count):
    order = [0]
    bit = count // 2
    while bit:
        order = order + [k ^ bit for k in order]
        bit //= 2
    return order


def scatter_rows(partial):
    bit = 1
    while bit < lax.axis_size("gx"):
        half = partial.shape[0] // 2
        received = swap(partial[half:].astype(LOW), "gx", bit)
        partial = partial[:half] + received.astype(WIDE)
        bit *= 2
    return partial


def reversed_bits(value, count):
    turned = 0
    while count > 1:
        turned = turned * 2 + value % 2
        value //= 2
        count //= 2
    return turned


def owner_pairs(nx, ny):
    return [
        (i * ny + h * nx + q, reversed_bits(q, nx) * ny + h * nx + reversed_bits(i, nx))
        for i in range(nx)
        for h in range(ny // nx)
        for q in range(nx)
    ]


def cut_rows(values, block):
    nx, ny = lax.axis_size("gx"), lax.axis_size("gy")
    images = values.reshape(ny // nx, SEQ, D // ny)
    images = jnp.pad(images, ((0, 0), (0, nx * block - SEQ), (0, 0)))
    parts = images.reshape(ny // nx, nx, block, D // ny)
    parts = jnp.stack([parts[:, reversed_bits(q, nx)] for q in range(nx)], axis=1)
    parts = parts.reshape(ny, block, D // ny)
    return lax.all_to_all(parts, "gy", split_axis=0, concat_axis=0, tiled=True)


def to_owner(parts):
    nx, ny = lax.axis_size("gx"), lax.axis_size("gy")
    parts = lax.ppermute(parts, ("gx", "gy"), owner_pairs(nx, ny))
    return parts.transpose(1, 0, 2).reshape(parts.shape[1], D)


def leave_owner(values):
    nx, ny = lax.axis_size("gx"), lax.axis_size("gy")
    parts = values.reshape(values.shape[0], ny, D // ny).transpose(1, 0, 2)
    return lax.ppermute(parts, ("gx", "gy"), [(b, a) for a, b in owner_pairs(nx, ny)])


def join_rows(parts, packed_shape):
    nx, ny = lax.axis_size("gx"), lax.axis_size("gy")
    block = parts.shape[1]
    parts = lax.all_to_all(parts, "gy", split_axis=0, concat_axis=0, tiled=True)
    parts = parts.reshape(ny // nx, nx, block, D // ny)
    parts = jnp.stack([parts[:, reversed_bits(q, nx)] for q in range(nx)], axis=1)
    return parts.reshape(ny // nx, nx * block, D // ny)[:, :SEQ].reshape(packed_shape)


def norm_forward(values, gain, shift):
    center = jnp.mean(values, axis=1, keepdims=True)
    spread = jnp.mean(values * values, axis=1, keepdims=True) - center * center
    rstd = lax.rsqrt(spread + 1e-06)
    normed = (values - center) * rstd
    return (normed * gain + shift).astype(LOW), normed, rstd


def norm_backward(grad, gain, normed, rstd):
    scaled = grad * gain
    total = jnp.mean(scaled, axis=1, keepdims=True)
    along = jnp.mean(scaled * normed, axis=1, keepdims=True)
    return rstd * (scaled - total - normed * along)


def times(left, right):
    return jnp.dot(left, right, preferred_element_type=WIDE)


def times_t(left, right):
    return lax.dot_general(left, right, (((1,), (1,)), ((), ())), preferred_element_type=WIDE)


def inner_rows(left, right):
    return lax.dot_general(left, right, (((0,), (0,)), ((), ())), preferred_element_type=WIDE)


def lane_blocks(size):
    return [(start, min(256, size - start)) for start in range(0, size, 256)]


def with_row(head, row):
    return jnp.concatenate((head, row), axis=0)


def attend_forward_body(q_ref, k_ref, v_ref, mask_ref, ones_ref, low_ref, wide_ref, log_ref):
    keys = with_row(k_ref[...], mask_ref[...]).T
    query = with_row((q_ref[...].astype(WIDE) * SCALE).astype(LOW), ones_ref[...])
    values = with_row(v_ref[...], ones_ref[...])
    for start, size in lane_blocks(query.shape[1]):
        lanes = slice(start, start + size)
        scores = jnp.dot(keys, query[:, lanes], preferred_element_type=WIDE)
        peak = jnp.max(scores, axis=0, keepdims=True)
        raised = jnp.exp(scores - peak).astype(LOW)
        mixed = jnp.dot(values, raised, preferred_element_type=WIDE)
        total = mixed[HEAD_DIM : HEAD_DIM + 1]
        attended = mixed[:HEAD_DIM] / total
        wide_ref[:, lanes] = attended
        low_ref[:, lanes] = attended.astype(LOW)
        log_ref[0, :, lanes] = peak + jnp.log(total)


def attend_forward(query, keys, values, mask, ones):
    cols, rows = query.shape
    heads = cols // HEAD_DIM
    head = pl.BlockSpec((HEAD_DIM, rows), lambda h: (h, 0))
    shared = pl.BlockSpec((HEAD_DIM, rows), lambda h: (0, 0))
    return pl.pallas_call(
        attend_forward_body,
        grid=(heads,),
        in_specs=[head, head, head, shared, shared],
        out_specs=[head, head, pl.BlockSpec((1, 1, rows), lambda h: (h, 0, 0))],
        out_shape=[
            jax.ShapeDtypeStruct((cols, rows), LOW),
            jax.ShapeDtypeStruct((cols, rows), WIDE),
            jax.ShapeDtypeStruct((heads, 1, rows), WIDE),
        ],
        compiler_params=pltpu.CompilerParams(vmem_limit_bytes=48 * 1024 * 1024),
        cost_estimate=pl.CostEstimate(
            flops=8 * heads * rows * rows * HEAD_DIM,
            bytes_accessed=12 * cols * rows,
            transcendentals=heads * rows * rows,
        ),
    )(query, keys, values, mask, ones)


def attend_backward_body(
    q_ref, k_ref, v_ref, g_ref, wide_ref, log_ref, mask_ref, ones_ref, out_ref
):
    rows = q_ref.shape[1]
    keys_t = k_ref[...]
    keys = with_row(keys_t, mask_ref[...]).T
    query = with_row((q_ref[...].astype(WIDE) * SCALE).astype(LOW), ones_ref[...])
    values = with_row(v_ref[...], mask_ref[...]).T[:, :HEAD_DIM]
    both = with_row(q_ref[...], g_ref[...]).T
    grad_keys = jnp.zeros((rows, HEAD_DIM), WIDE)
    grad_values = jnp.zeros((rows, HEAD_DIM), WIDE)
    for start, size in lane_blocks(rows):
        lanes = slice(start, start + size)
        grad_out = g_ref[:, lanes]
        scores = jnp.dot(keys, query[:, lanes], preferred_element_type=WIDE)
        probs = jnp.exp(scores - log_ref[0, :, lanes])
        grad_probs = jnp.dot(values, grad_out, preferred_element_type=WIDE)
        along = jnp.sum(grad_out.astype(WIDE) * wide_ref[:, lanes], axis=0, keepdims=True)
        grad_scores = (probs * (grad_probs - along)).astype(LOW)
        grad_query = jnp.dot(keys_t, grad_scores, preferred_element_type=WIDE) * SCALE
        out_ref[0, :, lanes] = grad_query.astype(LOW)
        grad_keys += jnp.dot(
            grad_scores, both[lanes, :HEAD_DIM], preferred_element_type=WIDE
        )
        grad_values += jnp.dot(
            probs.astype(LOW), both[lanes, HEAD_DIM:], preferred_element_type=WIDE
        )
    joined = jnp.concatenate((grad_keys * SCALE, grad_values), axis=1).T
    out_ref[1] = joined[:HEAD_DIM].astype(LOW)
    out_ref[2] = joined[HEAD_DIM:].astype(LOW)


def attend_backward(query, keys, values, grad_out, wide, log_total, mask, ones):
    cols, rows = query.shape
    heads = cols // HEAD_DIM
    head = pl.BlockSpec((HEAD_DIM, rows), lambda h: (h, 0))
    shared = pl.BlockSpec((HEAD_DIM, rows), lambda h: (0, 0))
    return pl.pallas_call(
        attend_backward_body,
        grid=(heads,),
        in_specs=[
            head,
            head,
            head,
            head,
            head,
            pl.BlockSpec((1, 1, rows), lambda h: (h, 0, 0)),
            shared,
            shared,
        ],
        out_specs=pl.BlockSpec((3, HEAD_DIM, rows), lambda h: (0, h, 0)),
        out_shape=jax.ShapeDtypeStruct((3, cols, rows), LOW),
        compiler_params=pltpu.CompilerParams(vmem_limit_bytes=48 * 1024 * 1024),
        cost_estimate=pl.CostEstimate(
            flops=16 * heads * rows * rows * HEAD_DIM,
            bytes_accessed=20 * cols * rows,
            transcendentals=heads * rows * rows,
        ),
    )(query, keys, values, grad_out, wide, log_total, mask, ones)


def hidden_body(
    second_ref, grad_ref, expand_ref, shrink_ref, bias_ref,
    hidden_ref, pre_ref, down_ref, back_ref, sum_ref,
):
    preact = jnp.dot(second_ref[...], expand_ref[...], preferred_element_type=WIDE) + bias_ref[...]
    share = 0.5 * (1.0 + lax.erf(preact * 0.5**0.5))
    hidden = (preact * share).astype(LOW)
    slope = share + preact * (jnp.exp(preact * preact * -0.5) * (0.5 / math.pi) ** 0.5)
    grad_hidden = jnp.dot(grad_ref[...], shrink_ref[...], preferred_element_type=WIDE)
    grad_pre = (grad_hidden * slope).astype(LOW)
    hidden_ref[...] = hidden
    pre_ref[...] = grad_pre
    back_ref[...] = times_t(grad_pre, expand_ref[...])
    down_ref[...] = times_t(hidden, shrink_ref[...])
    sums = jnp.sum(grad_pre.astype(WIDE), axis=0, keepdims=True)

    @pl.when(pl.program_id(0) == 0)
    def _():
        sum_ref[...] = sums

    @pl.when(pl.program_id(0) != 0)
    def _():
        sum_ref[...] += sums


def hidden_layer(second, grad, expand, shrink, bias):
    rows, width = second.shape
    cols = expand.shape[1]
    step = rows // 4
    narrow = pl.BlockSpec((step, width), lambda r: (r, 0))
    units = pl.BlockSpec((step, cols), lambda r: (r, 0))
    weight = pl.BlockSpec((width, cols), lambda r: (0, 0))
    line = pl.BlockSpec((1, cols), lambda r: (0, 0))
    return pl.pallas_call(
        hidden_body,
        grid=(4,),
        in_specs=[narrow, narrow, weight, weight, line],
        out_specs=[units, units, narrow, narrow, line],
        out_shape=[
            jax.ShapeDtypeStruct((rows, cols), LOW),
            jax.ShapeDtypeStruct((rows, cols), LOW),
            jax.ShapeDtypeStruct((rows, width), WIDE),
            jax.ShapeDtypeStruct((rows, width), WIDE),
            jax.ShapeDtypeStruct((1, cols), WIDE),
        ],
        compiler_params=pltpu.CompilerParams(vmem_limit_bytes=48 * 1024 * 1024),
        cost_estimate=pl.CostEstimate(
            flops=8 * rows * cols * width,
            bytes_accessed=4 * rows * width + 4 * rows * cols + 8 * rows * width + 4 * width * cols,
            transcendentals=2 * rows * cols,
        ),
    )(second, grad, expand, shrink, bias)


def gather_small(values):
    bit = 1
    place = lax.axis_index("gy")
    while bit < lax.axis_size("gy"):
        other = swap(values, "gy", bit)
        values = jnp.where(
            (place & bit) != 0,
            jnp.concatenate((other, values), axis=0),
            jnp.concatenate((values, other), axis=0),
        )
        bit *= 2
    return values


def token_sums(vectors):
    flat = vectors.reshape(vectors.shape[0], lax.axis_size("gy"), -1)
    flat = flat.transpose(1, 0, 2)
    bit = lax.axis_size("gy") // 2
    place = lax.axis_index("gy")
    while bit:
        half = flat.shape[0] // 2
        upper = (place & bit) != 0
        kept = jnp.where(upper, flat[half:], flat[:half])
        sent = jnp.where(upper, flat[:half], flat[half:])
        flat = kept + swap(sent, "gy", bit)
        bit //= 2
    flat = flat[0]
    bit = 1
    while bit < lax.axis_size("gx"):
        flat = flat + swap(flat, "gx", bit)
        bit *= 2
    return flat


def image_sums(vector):
    bit = 1
    while bit < lax.axis_size("gy"):
        vector = vector + swap(vector, "gy", bit)
        bit *= 2
    return vector


def on_device(
    tokens,
    project_in,
    query_bias,
    value_bias,
    project_out,
    output_bias,
    attention_scale,
    first_norm_gain,
    first_norm_bias,
    second_norm_gain,
    second_norm_bias,
    expand_weight,
    expand_bias,
    shrink_weight,
    shrink_bias,
    feedforward_scale,
    cotangent,
):
    nx, ny = lax.axis_size("gx"), lax.axis_size("gy")
    head_cols = project_out.shape[0]
    hidden_cols = expand_weight.shape[1]
    packed_shape = tokens.shape
    block = -(-SEQ // (nx * 16)) * 16
    column = jnp.arange(block)
    mask = jnp.concatenate(
        [
            jnp.where((lax.axis_index("gx") ^ k) * block + column < SEQ, 0.0, -1e30)
            for k in slot_blocks(nx)
        ]
    )
    top = jnp.arange(HEAD_DIM)[:, None] == 0
    mask = jnp.where(top, mask[None], 0.0).astype(LOW)
    ones = jnp.where(top, jnp.ones((1, nx * block), WIDE), 0.0).astype(LOW)

    small = jnp.stack(
        (
            output_bias,
            attention_scale,
            first_norm_gain,
            first_norm_bias,
            second_norm_gain,
            second_norm_bias,
            shrink_bias,
            feedforward_scale,
        )
    )
    small = gather_small(small[None])
    out_shift, attn_scale, gain_one, shift_one, gain_two, shift_two, shrink_shift, ff_scale = [
        small[:, k].reshape(D) for k in range(8)
    ]
    weights = jnp.concatenate(
        (project_in.reshape(-1, 3 * head_cols), project_out.T, expand_weight, shrink_weight.T),
        axis=1,
    )
    weights = lax.all_gather(weights, "gy", axis=0, tiled=True)
    weight_in, weight_out, weight_expand, weight_shrink = jnp.split(
        weights, (3 * head_cols, 4 * head_cols, 4 * head_cols + hidden_cols), axis=1
    )
    inputs = to_owner(cut_rows(tokens, block)).astype(WIDE)
    grad_parts = cut_rows(cotangent, block)
    inputs, grad_parts = lax.optimization_barrier((inputs, grad_parts))
    grad = to_owner(grad_parts).astype(WIDE)

    first, first_hat, first_rstd = norm_forward(inputs, gain_one, shift_one)
    first_all = gather_rows(first)
    mixed = lax.dot_general(
        weight_in, first_all, (((0,), (1,)), ((), ())), preferred_element_type=WIDE
    )
    query = (mixed[:head_cols] + query_bias[:, None]).astype(LOW)
    keys = mixed[head_cols : 2 * head_cols].astype(LOW)
    values = (mixed[2 * head_cols :] + value_bias[:, None]).astype(LOW)
    attended, attended_wide, log_total = attend_forward(query, keys, values, mask, ones)

    grad_b = grad * ff_scale
    grad_b_all = gather_rows(grad_b.astype(LOW))

    branch_a = scatter_rows(inner_rows(attended, weight_out.T)) + out_shift
    middle = inputs + attn_scale * branch_a
    second, second_hat, second_rstd = norm_forward(middle, gain_two, shift_two)
    second_all = gather_rows(second)
    hidden, grad_pre, branch_part, second_part, pre_sum = hidden_layer(
        second_all, grad_b_all, weight_expand, weight_shrink, expand_bias[None]
    )
    grad_second = scatter_rows(second_part)
    branch_b = scatter_rows(branch_part) + shrink_shift
    output_parts = leave_owner((middle + ff_scale * branch_b).astype(LOW))

    shrink_grad = inner_rows(grad_b_all, hidden)
    expand_grad = inner_rows(second_all, grad_pre)
    wide_grads = jnp.concatenate((shrink_grad, expand_grad), axis=1).astype(LOW)
    wide_grads = lax.psum_scatter(wide_grads, "gy", scatter_dimension=0, tiled=True).astype(WIDE)

    grad_middle = grad + norm_backward(grad_second, gain_two, second_hat, second_rstd)
    grad_a = grad_middle * attn_scale
    grad_a_all = gather_rows(grad_a.astype(LOW))
    grad_attended = lax.dot_general(
        weight_out, grad_a_all, (((0,), (1,)), ((), ())), preferred_element_type=WIDE
    ).astype(LOW)
    grad_mixed = attend_backward(
        query, keys, values, grad_attended, attended_wide, log_total, mask, ones
    )
    block_output = join_rows(output_parts, packed_shape)
    grad_mixed, block_output = lax.optimization_barrier((grad_mixed, block_output))
    joined = grad_mixed.reshape(3 * head_cols, nx * block)
    grad_first = scatter_rows(inner_rows(joined, weight_in.T))
    input_gradient = grad_middle + norm_backward(grad_first, gain_one, first_hat, first_rstd)
    input_gradient = join_rows(leave_owner(input_gradient.astype(LOW)), packed_shape).astype(WIDE)

    out_grad = times_t(attended, grad_a_all.T).T
    in_grad = times_t(joined, first_all.T).T
    head_grads = jnp.concatenate((out_grad, in_grad), axis=1).astype(LOW)
    head_grads = lax.psum_scatter(head_grads, "gy", scatter_dimension=0, tiled=True).astype(WIDE)

    sums = token_sums(
        jnp.stack(
            [
                jnp.sum(item, axis=0)
                for item in (
                    grad_a,
                    grad_middle * branch_a,
                    grad_first * first_hat,
                    grad_first,
                    grad_second * second_hat,
                    grad_second,
                    grad_b,
                    grad * branch_b,
                )
            ]
        )
    )
    biases = image_sums(
        jnp.concatenate(
            (
                jnp.sum(grad_mixed[0].astype(WIDE), axis=1),
                jnp.sum(grad_mixed[2].astype(WIDE), axis=1),
                pre_sum[0],
            )
        )
    )
    return (
        block_output,
        input_gradient,
        head_grads[:, head_cols:].reshape(-1, 3, head_cols),
        biases[:head_cols],
        biases[head_cols : 2 * head_cols],
        head_grads[:, :head_cols].T,
        sums[0],
        sums[1],
        sums[2],
        sums[3],
        sums[4],
        sums[5],
        wide_grads[:, hidden_cols:],
        biases[2 * head_cols :],
        wide_grads[:, :hidden_cols].T,
        sums[6],
        sums[7],
    )


def solution(mesh):
    rows = P("gx", "gy", None)
    wide, heads = P("gy"), P("gx")
    placed = (
        rows, P("gy", None, "gx"), heads, heads, P("gx", "gy"), wide, wide, wide, wide, wide, wide,
        P("gy", "gx"), heads, P("gx", "gy"), wide, wide, rows,
    )
    results = (
        rows, rows, P("gy", None, "gx"), heads, heads, P("gx", "gy"), wide, wide, wide, wide, wide,
        wide, P("gy", "gx"), heads, P("gx", "gy"), wide, wide,
    )
    return jax.shard_map(
        on_device, mesh=mesh, in_specs=placed, out_specs=results, check_vma=False
    )
```

time: 692 us -> 511 us (0.74)
  matrix products: 157 us -> 28.8 us
  blocking collectives: 89.4 us -> 0 us
  Pallas kernels: 0 us -> 60.7 us
  starting transfers between devices: 136 us -> 88.9 us
  waiting for transfers between devices: 186 us -> 233 us
  other arithmetic: 62.9 us -> 33.3 us
  local copies, waits for them, and re-layouts: 34.3 us -> 41.9 us
    dot_general x10 -> x2, matrix products: 130 us -> 7.55 us  [the longest x1 4.48 us: on_device(): lax.dot_general(weight_in, first_all, (((0,), (1,)), ((), ())), preferred...]
    all_gather x1 -> x0, blocking collectives: 63.5 us -> none  [on_device(): small = lax.all_gather(small, 'gy', axis=1, tiled=True)]
    pallas_call x0 -> x3, Pallas kernels: none -> 60.7 us  [the longest x1 23 us: attend_backward(): pl.pallas_call(attend_backward_body, grid=(heads,), in_specs=[head, head,...]
    all_to_all x3 -> x4, starting transfers between devices: 89.8 us -> 40.5 us  [the longest x2 28.4 us: join_rows(): parts = lax.all_to_all(parts, 'gy', split_axis=0, concat_axis=0, tiled=True)]
    all_to_all x3 -> x4, waiting for transfers between devices: 4.69 us -> 43.4 us  [the longest x2 34.1 us: cut_rows(): return lax.all_to_all(parts, 'gy', split_axis=0, concat_axis=0, tiled=True)]
    ppermute x24 -> x27, waiting for transfers between devices: 144 us -> 180 us  [swap(): return lax.ppermute(values, axis, [(k, k ^ bit) for k in range(size)])]
    all_gather x2 -> x1, waiting for transfers between devices: 36.6 us -> 8.61 us  [on_device(): weights = lax.all_gather(weights, 'gy', axis=0, tiled=True)]
    convert_element_type x3 -> x5, other arithmetic: 27.6 us -> 0.58 us  [the longest x1 0.22 us: on_device(): values = (mixed[2 * head_cols:] + value_bias[:, None]).astype(LOW)]
  transfers between devices with their start and end apart: 35 -> 38, of which waited for: 16 -> 21; matrix products, arithmetic and copies ran while one was open for 31% -> 16% of each run, Pallas kernels for 0% -> 5%
where the time goes in v2:
time: 511 us; the launch traced here: 501 us
  waiting for transfers between devices  233 us (46%)
  starting transfers between devices  88.9 us (17%)
  Pallas kernels  60.7 us (12%)
  local copies, waits for them, and re-layouts  41.9 us (8%)
  other arithmetic  33.3 us (7%)
  matrix products  28.8 us (6%)
  between operations  15.2 us (3%)
    ppermute x27, waiting for transfers between devices, swap(): return lax.ppermute(values, axis, [(k, k ^ bit) for k in range(size)])  180 us
    ppermute x27, starting transfers between devices, swap(): return lax.ppermute(values, axis, [(k, k ^ bit) for k in range(size)])  43.4 us
    all_to_all x2, waiting for transfers between devices, cut_rows(): return lax.all_to_all(parts, 'gy', split_axis=0, concat_axis=0, tiled=True)  34.1 us
    all_to_all x2, starting transfers between devices, join_rows(): parts = lax.all_to_all(parts, 'gy', split_axis=0, concat_axis=0, tiled=True)  28.4 us
    pallas_call x1, Pallas kernels, attend_backward(): pl.pallas_call(attend_backward_body, grid=(heads,), in_specs=[head, head,...  23 us
    unnamed x113, local copies, waits for them, and re-layouts  22.1 us
    pallas_call x1, Pallas kernels, attend_forward(): pl.pallas_call(attend_forward_body, grid=(heads,), in_specs=[head, head,...  20.5 us
    pallas_call x1, Pallas kernels, hidden_layer(): pl.pallas_call(hidden_body, grid=(4,), in_specs=[narrow, narrow, weight,...  17.2 us
  transfers between devices with their start and end apart: 38, of which 21 were waited for; matrix products, arithmetic and copies ran while one was open for 16% of the time, Pallas kernels for 5%

profile of v2, /device:TPU:0, one launch (start us, length us, event | category | flops | bytes accessed | tf_op | source)
XLA Modules:
  0.0 501.3 jit_solution(3787953968384118001)
XLA Ops:
  12.9 7.3 %all-to-all-start = ((bf16[8,352,128]{2,1,0:T(8,128)(2,1)}), bf16[8,352,128]{2,1,0:T(8,128)(2,1)S(1)}, u32[]{:S(2)}, u32[]{:S(2)}) async-start(bf16[8,352,128]{2,1,0:T(8,128)(2,1)} %bitcast.4), calls=%async_computation | async-start | bytes 1441792 | tf_op jit(solution)/shard_map/all_to_all | solution.py:75
  21.5 34.1 %all-to-all-done = bf16[8,352,128]{2,1,0:T(8,128)(2,1)S(1)} async-done(((bf16[8,352,128]{2,1,0:T(8,128)(2,1)}), bf16[8,352,128]{2,1,0:T(8,128)(2,1)S(1)}, u32[]{:S(2)}, u32[]{:S(2)}) %all-to-all-start) | async-done | bytes 720928 | tf_op jit(solution)/shard_map/all_to_all | solution.py:75
  55.6 4.9 all-to-all-start.1
  61.3 4.3 collective-permute-start.1
  65.6 29.4 %collective-permute-done.1 = f32[1,8,128]{2,1,0:T(8,128)S(1)} collective-permute-done((f32[1,8,128]{2,1,0:T(8,128)S(1)}, f32[1,8,128]{2,1,0:T(8,128)S(1)}, u32[]{:S(2)}, u32[]{:S(2)}) %collective-permute-start.1) | collective-permute-done | bytes 4128 | tf_op jit(solution)/shard_map/ppermute | solution.py:20
  95.0 9.2 %collective-permute-done.2 = f32[2,8,128]{2,1,0:T(8,128)S(1)} collective-permute-done((f32[2,8,128]{2,1,0:T(8,128)S(1)}, f32[2,8,128]{2,1,0:T(8,128)S(1)}, u32[]{:S(2)}, u32[]{:S(2)}) %collective-permute-start.2) | collective-permute-done | bytes 8224 | tf_op jit(solution)/shard_map/ppermute | solution.py:20
  104.2 4.8 collective-permute-done.3
  110.6 4.6 collective-permute-start.4
  115.2 12.7 %collective-permute-done.4 = bf16[352,1024]{1,0:T(8,128)(2,1)S(1)} collective-permute-done((bf16[352,1024]{1,0:T(8,128)(2,1)S(1)}, bf16[352,1024]{1,0:T(8,128)(2,1)S(1)}, u32[]{:S(2)}, u32[]{:S(2)}) %collective-permute-start.4) | collective-permute-done | bytes 720928 | tf_op jit(solution)/shard_map/ppermute | solution.py:20
  132.9 8.6 %all-gather.2.cloned.1.call-done = bf16[1024,3072]{1,0:T(8,128)(2,1)} async-done(((bf16[128,3072]{1,0:T(8,128)(2,1)}), bf16[1024,3072]{1,0:T(8,128)(2,1)}) %all-gather.2.cloned.1.call-update) | async-done | bytes 6291472 | tf_op jit(solution)/shard_map/all_gather | solution.py:387
  141.5 4.5 fusion.9
  146.4 20.5 %shard_map.296 = (bf16[256,1408]{1,0:T(8,128)(2,1)S(1)}, f32[256,1408]{1,0:T(8,128)S(1)}, f32[4,1,1408]{2,1,0:T(1,128)S(1)}) custom-call(bf16[256,1408]{1,0:T(8,128)(2,1)S(1)} %get-tuple-element.113.q_ref, bf16[256,1408]{1,0:T(8,128)(2,1)S(1)} %slice.433.k_ref, bf16[256,1408]{1,0:T(8,128)(2,1)S(1)} %get-tuple-element.112.v_ref, ...), custom_call_target="tpu_custom_call" | custom-call | flops 4060086272 | bytes 4325376 | tf_op jit(solution)/shard_map/pallas_call | solution.py:156
  173.9 13.9 %collective-permute-start.11 = (bf16[352,1024]{1,0:T(8,128)(2,1)S(1)}, bf16[352,1024]{1,0:T(8,128)(2,1)S(1)}, u32[]{:S(2)}, u32[]{:S(2)}) collective-permute-start(bf16[352,1024]{1,0:T(8,128)(2,1)S(1)} %fusion.1), channel_id=1, source_target_pairs={{0,16},{8,24},{16,0},{24,8},{1,17},{9,25},{17,1},{25,9},{2,18},{10... | collective-permute-start | bytes 2162696 | tf_op jit(solution)/shard_map/ppermute | solution.py:20
  187.8 12.7 %collective-permute-done.8 = bf16[352,1024]{1,0:T(8,128)(2,1)S(1)} collective-permute-done((bf16[352,1024]{1,0:T(8,128)(2,1)S(1)}, bf16[352,1024]{1,0:T(8,128)(2,1)S(1)}, u32[]{:S(2)}, u32[]{:S(2)}) %collective-permute-start.8) | collective-permute-done | bytes 720928 | tf_op jit(solution)/shard_map/ppermute | solution.py:20
  204.1 11.7 %collective-permute-done.11 = bf16[352,1024]{1,0:T(8,128)(2,1)S(1)} collective-permute-done((bf16[352,1024]{1,0:T(8,128)(2,1)S(1)}, bf16[352,1024]{1,0:T(8,128)(2,1)S(1)}, u32[]{:S(2)}, u32[]{:S(2)}) %collective-permute-start.11) | collective-permute-done | bytes 720928 | tf_op jit(solution)/shard_map/ppermute | solution.py:20
  216.2 15.1 %collective-permute-done.9 = bf16[352,1024]{1,0:T(8,128)(2,1)S(1)} collective-permute-done((bf16[352,1024]{1,0:T(8,128)(2,1)S(1)}, bf16[352,1024]{1,0:T(8,128)(2,1)S(1)}, u32[]{:S(2)}, u32[]{:S(2)}) %collective-permute-start.9) | collective-permute-done | bytes 720928 | tf_op jit(solution)/shard_map/ppermute | solution.py:20
  236.7 17.2 %shard_map.297 = (bf16[1408,1024]{1,0:T(8,128)(2,1)}, bf16[1408,1024]{1,0:T(8,128)(2,1)}, f32[1408,1024]{1,0:T(8,128)}, f32[1408,1024]{1,0:T(8,128)}, f32[1,1024]{1,0:T(1,128)S(1)}) custom-call(bf16[1408,1024]{1,0:T(8,128)(2,1)} %pad_maximum_fusion.2.second_ref, bf16[1408,1024]{1,0:T(8,128)(2,1)} %pad_maximum_fusion.3.grad_ref, ...), custom_call_target="tpu_custom_call" | custom-call | flops 11811160064 | bytes 27262976 | tf_op jit(solution)/shard_map/pallas_call | solution.py:269
  260.1 3.7 convolution_convert_fusion.1
  263.8 3.7 convolution_convert_fusion.2
  275.6 6.6 %copy.79 = bf16[1024,2048]{1,0:T(8,128)(2,1)} copy(bf16[1024,2048]{0,1:T(8,128)(2,1)} %pad_maximum_fusion) | data formatting | bytes 8388608
  285.4 5.1 %collective-permute-done.14 = bf16[352,1024]{1,0:T(8,128)(2,1)} collective-permute-done((bf16[352,1024]{1,0:T(8,128)(2,1)}, bf16[352,1024]{1,0:T(8,128)(2,1)}, u32[]{:S(2)}, u32[]{:S(2)}) %collective-permute-start.14) | collective-permute-done | bytes 720928 | tf_op jit(solution)/shard_map/ppermute | solution.py:20
  292.4 12.8 %collective-permute-done.18 = bf16[352,1024]{1,0:T(8,128)(2,1)S(1)} collective-permute-done((bf16[352,1024]{1,0:T(8,128)(2,1)S(1)}, bf16[352,1024]{1,0:T(8,128)(2,1)S(1)}, u32[]{:S(2)}, u32[]{:S(2)}) %collective-permute-start.18) | collective-permute-done | bytes 720928 | tf_op jit(solution)/shard_map/ppermute | solution.py:20
  314.5 22.8 %all-to-all-start.2 = ((bf16[8,352,128]{2,1,0:T(8,128)(2,1)}), bf16[8,352,128]{2,1,0:T(8,128)(2,1)}, u32[]{:S(2)}, u32[]{:S(2)}) async-start(bf16[8,352,128]{2,1,0:T(8,128)(2,1)} %collective-permute-done.19), calls=%async_computation.2 | async-start | bytes 1441792 | tf_op jit(solution)/shard_map/all_to_all | solution.py:93
  337.3 6.8 %collective-permute-done.15 = bf16[352,1024]{1,0:T(8,128)(2,1)} collective-permute-done((bf16[352,1024]{1,0:T(8,128)(2,1)}, bf16[352,1024]{1,0:T(8,128)(2,1)}, u32[]{:S(2)}, u32[]{:S(2)}) %collective-permute-start.15) | collective-permute-done | bytes 720928 | tf_op jit(solution)/shard_map/ppermute | solution.py:20
  346.7 9.3 %all-to-all-done.2 = bf16[8,352,128]{2,1,0:T(8,128)(2,1)} async-done(((bf16[8,352,128]{2,1,0:T(8,128)(2,1)}), bf16[8,352,128]{2,1,0:T(8,128)(2,1)}, u32[]{:S(2)}, u32[]{:S(2)}) %all-to-all-start.2) | async-done | bytes 720928 | tf_op jit(solution)/shard_map/all_to_all | solution.py:93
  363.6 23.0 %shard_map.298 = bf16[3,256,1408]{2,1,0:T(8,128)(2,1)} custom-call(bf16[256,1408]{1,0:T(8,128)(2,1)S(1)} %get-tuple-element.113.q_ref, bf16[256,1408]{1,0:T(8,128)(2,1)S(1)} %slice.433.k_ref, bf16[256,1408]{1,0:T(8,128)(2,1)S(1)} %get-tuple-element.112.v_ref, bf16[256,1408]{1,0:T(8,128)(2,1)S(1)} %convolution_convert_fusion.g_ref, ...), custom_call_target="tpu_custom_call" | custom-call | flops 8120172544 | bytes 7208960 | tf_op jit(solution)/shard_map/pallas_call | solution.py:212
  386.6 4.6 fusion.7
  393.3 4.0 convolution_convert_fusion.3
  407.8 8.6 %collective-permute-done.21 = bf16[352,1024]{1,0:T(8,128)(2,1)} collective-permute-done((bf16[352,1024]{1,0:T(8,128)(2,1)}, bf16[352,1024]{1,0:T(8,128)(2,1)}, u32[]{:S(2)}, u32[]{:S(2)}) %collective-permute-start.21) | collective-permute-done | bytes 720928 | tf_op jit(solution)/shard_map/ppermute | solution.py:20
  427.6 21.1 %collective-permute-done.23 = f32[1536]{0:T(1024)S(1)} collective-permute-done((f32[1536]{0:T(1024)S(1)}, f32[1536]{0:T(1024)S(1)}, u32[]{:S(2)}, u32[]{:S(2)}) %collective-permute-start.23) | collective-permute-done | bytes 6176 | tf_op jit(solution)/shard_map/ppermute | solution.py:20
  448.8 5.6 %all-to-all-start.3 = ((bf16[8,352,128]{2,1,0:T(8,128)(2,1)}), bf16[8,352,128]{2,1,0:T(8,128)(2,1)S(1)}, u32[]{:S(2)}, u32[]{:S(2)}) async-start(bf16[8,352,128]{2,1,0:T(8,128)(2,1)} %collective-permute-done.22), calls=%async_computation.3 | async-start | bytes 1441792 | tf_op jit(solution)/shard_map/all_to_all | solution.py:93
  460.9 20.6 %collective-permute-done.25 = f32[1536]{0:T(1024)S(1)} collective-permute-done((f32[1536]{0:T(1024)S(1)}, f32[1536]{0:T(1024)S(1)}, u32[]{:S(2)}, u32[]{:S(2)}) %collective-permute-start.25) | collective-permute-done | bytes 6176 | tf_op jit(solution)/shard_map/ppermute | solution.py:20
  (268 shorter events, 112.3 us)
Async XLA Ops:
  7.2 134.3 %all-gather.2.cloned.1.call-start = ((), (), s32[]{:S(2)}) async-start(), calls=%async_computation.6 | async-start | bytes 7077888 | tf_op jit(solution)/shard_map/all_gather | solution.py:387
  12.9 42.6 %all-to-all-start = ((bf16[8,352,128]{2,1,0:T(8,128)(2,1)}), bf16[8,352,128]{2,1,0:T(8,128)(2,1)S(1)}, u32[]{:S(2)}, u32[]{:S(2)}) async-start(bf16[8,352,128]{2,1,0:T(8,128)(2,1)} %bitcast.4), calls=%async_computation | async-start | bytes 1441792 | tf_op jit(solution)/shard_map/all_to_all | solution.py:75
  55.6 53.7 %all-to-all-start.1 = ((bf16[8,352,128]{2,1,0:T(8,128)(2,1)}), bf16[8,352,128]{2,1,0:T(8,128)(2,1)S(1)}, u32[]{:S(2)}, u32[]{:S(2)}) async-start(bf16[8,352,128]{2,1,0:T(8,128)(2,1)} %bitcast.7), calls=%async_computation.1 | async-start | bytes 1441792 | tf_op jit(solution)/shard_map/all_to_all | solution.py:75
  60.4 425.3 %reduce-scatter.9.cloned.1.call-start = ((), (), s32[]{:S(2)}) async-start(), calls=%async_computation.8 | async-start | bytes 4718592
  60.5 48.6 %collective-permute-start = (bf16[8,352,128]{2,1,0:T(8,128)(2,1)S(1)}, bf16[8,352,128]{2,1,0:T(8,128)(2,1)S(1)}, u32[]{:S(2)}, u32[]{:S(2)}) collective-permute-start(bf16[8,352,128]{2,1,0:T(8,128)(2,1)S(1)} %all-to-all-done), channel_id=1, source_target_pairs={{0,0},{1,16},{2,8},{3,24},{4,4},{5,20},{6,12},{7,28},{8,2},{9,18},... | collective-permute-start | bytes 2162696 | tf_op jit(solution)/shard_map/ppermute | solution.py:80
  61.3 33.7 %collective-permute-start.1 = (f32[1,8,128]{2,1,0:T(8,128)S(1)}, f32[1,8,128]{2,1,0:T(8,128)S(1)}, u32[]{:S(2)}, u32[]{:S(2)}) collective-permute-start(f32[1,8,128]{2,1,0:T(8,128)S(1)} %bitcast.153), channel_id=1, source_target_pairs={{0,1},{1,0},{2,3},{3,2},{4,5},{5,4},{6,7},{7,6},{8,9},{9,8},{10,11... | collective-permute-start | bytes 12296 | tf_op jit(solution)/shard_map/ppermute | solution.py:20
  95.0 9.2 %collective-permute-start.2 = (f32[2,8,128]{2,1,0:T(8,128)S(1)}, f32[2,8,128]{2,1,0:T(8,128)S(1)}, u32[]{:S(2)}, u32[]{:S(2)}) collective-permute-start(f32[2,8,128]{2,1,0:T(8,128)S(1)} %maximum_select_fusion.2), channel_id=1, source_target_pairs={{0,2},{1,3},{2,0},{3,1},{4,6},{5,7},{6,4},{7,5},{8,10},{9,11},{10,... | collective-permute-start | bytes 24584 | tf_op jit(solution)/shard_map/ppermute | solution.py:20
  110.6 17.3 %collective-permute-start.4 = (bf16[352,1024]{1,0:T(8,128)(2,1)S(1)}, bf16[352,1024]{1,0:T(8,128)(2,1)S(1)}, u32[]{:S(2)}, u32[]{:S(2)}) collective-permute-start(bf16[352,1024]{1,0:T(8,128)(2,1)S(1)} %add_convert_fusion.3), channel_id=1, source_target_pairs={{0,16},{8,24},{16,0},{24,8},{1,17},{9,25},{17,1},{25,9},{2,18},{10... | collective-permute-start | bytes 2162696 | tf_op jit(solution)/shard_map/ppermute | solution.py:20
  173.6 26.8 %collective-permute-start.8 = (bf16[352,1024]{1,0:T(8,128)(2,1)S(1)}, bf16[352,1024]{1,0:T(8,128)(2,1)S(1)}, u32[]{:S(2)}, u32[]{:S(2)}) collective-permute-start(bf16[352,1024]{1,0:T(8,128)(2,1)S(1)} %slice.432), channel_id=1, source_target_pairs={{0,16},{8,24},{16,0},{24,8},{1,17},{9,25},{17,1},{25,9},{2,18},{10... | collective-permute-start | bytes 2162696 | tf_op jit(solution)/shard_map/ppermute | solution.py:20
  173.9 42.0 %collective-permute-start.11 = (bf16[352,1024]{1,0:T(8,128)(2,1)S(1)}, bf16[352,1024]{1,0:T(8,128)(2,1)S(1)}, u32[]{:S(2)}, u32[]{:S(2)}) collective-permute-start(bf16[352,1024]{1,0:T(8,128)(2,1)S(1)} %fusion.1), channel_id=1, source_target_pairs={{0,16},{8,24},{16,0},{24,8},{1,17},{9,25},{17,1},{25,9},{2,18},{10... | collective-permute-start | bytes 2162696 | tf_op jit(solution)/shard_map/ppermute | solution.py:20
  201.6 29.7 %collective-permute-start.9 = (bf16[352,1024]{1,0:T(8,128)(2,1)S(1)}, bf16[352,1024]{1,0:T(8,128)(2,1)S(1)}, u32[]{:S(2)}, u32[]{:S(2)}) collective-permute-start(bf16[352,1024]{1,0:T(8,128)(2,1)S(1)} %add_convert_fusion.2), channel_id=1, source_target_pairs={{0,16},{8,24},{16,0},{24,8},{1,17},{9,25},{17,1},{25,9},{2,18},{10... | collective-permute-start | bytes 2162696 | tf_op jit(solution)/shard_map/ppermute | solution.py:20
  216.0 15.6 %collective-permute-start.12 = (bf16[704,1024]{1,0:T(8,128)(2,1)S(1)}, bf16[704,1024]{1,0:T(8,128)(2,1)S(1)}, u32[]{:S(2)}, u32[]{:S(2)}) collective-permute-start(bf16[704,1024]{1,0:T(8,128)(2,1)S(1)} %pad_maximum_fusion.8), channel_id=1, source_target_pairs={{0,8},{8,0},{16,24},{24,16},{1,9},{9,1},{17,25},{25,17},{2,10},{10... | collective-permute-start | bytes 4325384 | tf_op jit(solution)/shard_map/ppermute | solution.py:20
  256.1 11.5 %collective-permute-start.13 = (bf16[704,1024]{1,0:T(8,128)(2,1)S(1)}, bf16[704,1024]{1,0:T(8,128)(2,1)S(1)}, u32[]{:S(2)}, u32[]{:S(2)}) collective-permute-start(bf16[704,1024]{1,0:T(8,128)(2,1)S(1)} %slice.427), channel_id=1, source_target_pairs={{0,8},{8,0},{16,24},{24,16},{1,9},{9,1},{17,25},{25,17},{2,10},{10... | collective-permute-start | bytes 4325384 | tf_op jit(solution)/shard_map/ppermute | solution.py:20
  259.6 22.6 %collective-permute-start.17 = (bf16[704,1024]{1,0:T(8,128)(2,1)}, bf16[704,1024]{1,0:T(8,128)(2,1)}, u32[]{:S(2)}, u32[]{:S(2)}) collective-permute-start(bf16[704,1024]{1,0:T(8,128)(2,1)} %slice.426), channel_id=1, source_target_pairs={{0,8},{8,0},{16,24},{24,16},{1,9},{9,1},{17,25},{25,17},{2,10},{10... | collective-permute-start | bytes 4325384 | tf_op jit(solution)/shard_map/ppermute | solution.py:20
  270.8 19.7 %collective-permute-start.14 = (bf16[352,1024]{1,0:T(8,128)(2,1)}, bf16[352,1024]{1,0:T(8,128)(2,1)}, u32[]{:S(2)}, u32[]{:S(2)}) collective-permute-start(bf16[352,1024]{1,0:T(8,128)(2,1)} %slice.431), channel_id=1, source_target_pairs={{0,16},{8,24},{16,0},{24,8},{1,17},{9,25},{17,1},{25,9},{2,18},{10... | collective-permute-start | bytes 2162696 | tf_op jit(solution)/shard_map/ppermute | solution.py:20
  285.3 20.0 %collective-permute-start.18 = (bf16[352,1024]{1,0:T(8,128)(2,1)S(1)}, bf16[352,1024]{1,0:T(8,128)(2,1)S(1)}, u32[]{:S(2)}, u32[]{:S(2)}) collective-permute-start(bf16[352,1024]{1,0:T(8,128)(2,1)S(1)} %slice.430), channel_id=1, source_target_pairs={{0,16},{8,24},{16,0},{24,8},{1,17},{9,25},{17,1},{25,9},{2,18},{10... | collective-permute-start | bytes 2162696 | tf_op jit(solution)/shard_map/ppermute | solution.py:20
  308.5 6.0 %collective-permute-start.19 = (bf16[8,352,128]{2,1,0:T(8,128)(2,1)S(1)}, bf16[8,352,128]{2,1,0:T(8,128)(2,1)}, u32[]{:S(2)}, u32[]{:S(2)}) collective-permute-start(bf16[8,352,128]{2,1,0:T(8,128)(2,1)S(1)} %bitcast.128), channel_id=1, source_target_pairs={{0,0},{16,1},{8,2},{24,3},{4,4},{20,5},{12,6},{28,7},{2,8},{18,9},... | collective-permute-start | bytes 2162696 | tf_op jit(solution)/shard_map/ppermute | solution.py:87
  311.1 33.0 %collective-permute-start.15 = (bf16[352,1024]{1,0:T(8,128)(2,1)}, bf16[352,1024]{1,0:T(8,128)(2,1)}, u32[]{:S(2)}, u32[]{:S(2)}) collective-permute-start(bf16[352,1024]{1,0:T(8,128)(2,1)} %multiply_convert_fusion), channel_id=1, source_target_pairs={{0,16},{8,24},{16,0},{24,8},{1,17},{9,25},{17,1},{25,9},{2,18},{10... | collective-permute-start | bytes 2162696 | tf_op jit(solution)/shard_map/ppermute | solution.py:20
  314.5 41.6 %all-to-all-start.2 = ((bf16[8,352,128]{2,1,0:T(8,128)(2,1)}), bf16[8,352,128]{2,1,0:T(8,128)(2,1)}, u32[]{:S(2)}, u32[]{:S(2)}) async-start(bf16[8,352,128]{2,1,0:T(8,128)(2,1)} %collective-permute-done.19), calls=%async_computation.2 | async-start | bytes 1441792 | tf_op jit(solution)/shard_map/all_to_all | solution.py:93
  337.2 154.5 %reduce-scatter.7.cloned.1.call-start = ((), (), s32[]{:S(2)}) async-start(), calls=%async_computation.7 | async-start | bytes 2359296
  346.7 13.8 %collective-permute-start.16 = (bf16[704,1024]{1,0:T(8,128)(2,1)}, bf16[704,1024]{1,0:T(8,128)(2,1)}, u32[]{:S(2)}, u32[]{:S(2)}) collective-permute-start(bf16[704,1024]{1,0:T(8,128)(2,1)} %pad_maximum_fusion.9), channel_id=1, source_target_pairs={{0,8},{8,0},{16,24},{24,16},{1,9},{9,1},{17,25},{25,17},{2,10},{10... | collective-permute-start | bytes 4325384 | tf_op jit(solution)/shard_map/ppermute | solution.py:20
  391.5 5.8 %collective-permute-start.20 = (bf16[704,1024]{1,0:T(8,128)(2,1)S(1)}, bf16[704,1024]{1,0:T(8,128)(2,1)S(1)}, u32[]{:S(2)}, u32[]{:S(2)}) collective-permute-start(bf16[704,1024]{1,0:T(8,128)(2,1)S(1)} %slice.425), channel_id=1, source_target_pairs={{0,8},{8,0},{16,24},{24,16},{1,9},{9,1},{17,25},{25,17},{2,10},{10... | collective-permute-start | bytes 4325384 | tf_op jit(solution)/shard_map/ppermute | solution.py:20
  399.0 17.3 %collective-permute-start.21 = (bf16[352,1024]{1,0:T(8,128)(2,1)}, bf16[352,1024]{1,0:T(8,128)(2,1)}, u32[]{:S(2)}, u32[]{:S(2)}) collective-permute-start(bf16[352,1024]{1,0:T(8,128)(2,1)} %slice.429), channel_id=1, source_target_pairs={{0,16},{8,24},{16,0},{24,8},{1,17},{9,25},{17,1},{25,9},{2,18},{10... | collective-permute-start | bytes 2162696 | tf_op jit(solution)/shard_map/ppermute | solution.py:20
  418.8 7.6 %collective-permute-start.26 = (f32[4,8,128]{2,1,0:T(8,128)S(1)}, f32[4,8,128]{2,1,0:T(8,128)S(1)}, u32[]{:S(2)}, u32[]{:S(2)}) collective-permute-start(f32[4,8,128]{2,1,0:T(8,128)S(1)} %slice_select_fusion), channel_id=1, source_target_pairs={{0,4},{1,5},{2,6},{3,7},{4,0},{5,1},{6,2},{7,3},{8,12},{9,13},{10,... | collective-permute-start | bytes 49160 | tf_op jit(solution)/shard_map/ppermute | solution.py:20
  421.6 27.3 %collective-permute-start.22 = (bf16[8,352,128]{2,1,0:T(8,128)(2,1)S(1)}, bf16[8,352,128]{2,1,0:T(8,128)(2,1)}, u32[]{:S(2)}, u32[]{:S(2)}) collective-permute-start(bf16[8,352,128]{2,1,0:T(8,128)(2,1)S(1)} %bitcast_bitcast_fusion), channel_id=1, source_target_pairs={{0,0},{16,1},{8,2},{24,3},{4,4},{20,5},{12,6},{28,7},{2,8},{18,9},... | collective-permute-start | bytes 2162696 | tf_op jit(solution)/shard_map/ppermute | solution.py:87
  423.1 25.6 %collective-permute-start.23 = (f32[1536]{0:T(1024)S(1)}, f32[1536]{0:T(1024)S(1)}, u32[]{:S(2)}, u32[]{:S(2)}) collective-permute-start(f32[1536]{0:T(1024)S(1)} %pad_maximum_fusion.19), channel_id=1, source_target_pairs={{0,1},{1,0},{2,3},{3,2},{4,5},{5,4},{6,7},{7,6},{8,9},{9,8},{10,11... | collective-permute-start | bytes 18440 | tf_op jit(solution)/shard_map/ppermute | solution.py:20
  426.4 28.1 %collective-permute-start.27 = (f32[2,8,128]{2,1,0:T(8,128)S(1)}, f32[2,8,128]{2,1,0:T(8,128)S(1)}, u32[]{:S(2)}, u32[]{:S(2)}) collective-permute-start(f32[2,8,128]{2,1,0:T(8,128)S(1)} %slice_select_fusion.1), channel_id=1, source_target_pairs={{0,2},{1,3},{2,0},{3,1},{4,6},{5,7},{6,4},{7,5},{8,10},{9,11},{10,... | collective-permute-start | bytes 24584 | tf_op jit(solution)/shard_map/ppermute | solution.py:20
  448.8 7.8 %collective-permute-start.24 = (f32[1536]{0:T(1024)S(1)}, f32[1536]{0:T(1024)S(1)}, u32[]{:S(2)}, u32[]{:S(2)}) collective-permute-start(f32[1536]{0:T(1024)S(1)} %fusion.24), channel_id=1, source_target_pairs={{0,2},{1,3},{2,0},{3,1},{4,6},{5,7},{6,4},{7,5},{8,10},{9,11},{10,... | collective-permute-start | bytes 18440 | tf_op jit(solution)/shard_map/ppermute | solution.py:20
  448.8 40.2 %all-to-all-start.3 = ((bf16[8,352,128]{2,1,0:T(8,128)(2,1)}), bf16[8,352,128]{2,1,0:T(8,128)(2,1)S(1)}, u32[]{:S(2)}, u32[]{:S(2)}) async-start(bf16[8,352,128]{2,1,0:T(8,128)(2,1)} %collective-permute-done.22), calls=%async_computation.3 | async-start | bytes 1441792 | tf_op jit(solution)/shard_map/all_to_all | solution.py:93
  454.5 6.4 %collective-permute-start.28 = (f32[1,8,128]{2,1,0:T(8,128)S(1)}, f32[1,8,128]{2,1,0:T(8,128)S(1)}, u32[]{:S(2)}, u32[]{:S(2)}) collective-permute-start(f32[1,8,128]{2,1,0:T(8,128)S(1)} %slice_select_fusion.2), channel_id=1, source_target_pairs={{0,1},{1,0},{2,3},{3,2},{4,5},{5,4},{6,7},{7,6},{8,9},{9,8},{10,11... | collective-permute-start | bytes 12296 | tf_op jit(solution)/shard_map/ppermute | solution.py:20
  456.6 24.9 %collective-permute-start.25 = (f32[1536]{0:T(1024)S(1)}, f32[1536]{0:T(1024)S(1)}, u32[]{:S(2)}, u32[]{:S(2)}) collective-permute-start(f32[1536]{0:T(1024)S(1)} %add.203), channel_id=1, source_target_pairs={{0,4},{1,5},{2,6},{3,7},{4,0},{5,1},{6,2},{7,3},{8,12},{9,13},{10,... | collective-permute-start | bytes 18440 | tf_op jit(solution)/shard_map/ppermute | solution.py:20
  460.9 20.6 %collective-permute-start.29 = (f32[8,128]{1,0:T(8,128)S(1)}, f32[8,128]{1,0:T(8,128)S(1)}, u32[]{:S(2)}, u32[]{:S(2)}) collective-permute-start(f32[8,128]{1,0:T(8,128)S(1)} %add_bitcast_fusion), channel_id=1, source_target_pairs={{0,8},{8,0},{16,24},{24,16},{1,9},{9,1},{17,25},{25,17},{2,10},{10... | collective-permute-start | bytes 12296 | tf_op jit(solution)/shard_map/ppermute | solution.py:20
  (58 other events, 762.0 us)
Sparse Core Ops, SparseCore 0:
  11.7 129.6 all-gather.1
  282.3 100.7 reduce-scatter.8
  406.2 77.2 reduce-scatter.6

commit v3 on v2

v3 whole, which is shorter than its diff:
```python
import math

import jax
import jax.numpy as jnp
from jax import lax
from jax.experimental import pallas as pl
from jax.experimental.pallas import tpu as pltpu
from jax.sharding import PartitionSpec as P

D = 1024
HEAD_DIM = 64
SEQ = 1370
SCALE = HEAD_DIM ** (-0.5)
LOW = jnp.bfloat16
WIDE = jnp.float32


def swap(values, axis, bit):
    size = lax.axis_size(axis)
    return lax.ppermute(values, axis, [(k, k ^ bit) for k in range(size)])


def together(*values):
    return lax.optimization_barrier(values)


def gather_far(values):
    bit = lax.axis_size("gx") // 2
    while bit > 2:
        values = jnp.concatenate((values, swap(values, "gx", bit)), axis=0)
        bit //= 2
    return values, swap(values, "gx", 2)


def gather_step(values):
    return jnp.concatenate(gather_far(values), axis=0)


def gather_halves(values):
    near = gather_step(values)
    return near, swap(near, "gx", 1)


def slot_blocks(count):
    order = [0]
    bit = count // 2
    while bit:
        order = order + [k ^ bit for k in order]
        bit //= 2
    return order


def scatter_near(kept, sent):
    return kept + swap(sent, "gx", 1).astype(WIDE)


def scatter_last(partial):
    bit = 2
    while True:
        half = partial.shape[0] // 2
        received = swap(partial[half:].astype(LOW), "gx", bit)
        partial = partial[:half]
        bit *= 2
        if bit >= lax.axis_size("gx"):
            return partial, received
        partial = partial + received.astype(WIDE)


def scatter_far(partial):
    kept, received = scatter_last(partial)
    return kept + received.astype(WIDE)


def in_two(partial):
    half = partial.shape[0] // 2
    return partial[:half], partial[half:].astype(LOW)


def pieces(values, count):
    parts = []
    for _ in range(count):
        head = lax.reduce_precision(values, exponent_bits=8, mantissa_bits=7)
        parts.append(head.astype(LOW))
        values = values - head
    return parts


def reversed_bits(value, count):
    turned = 0
    while count > 1:
        turned = turned * 2 + value % 2
        value //= 2
        count //= 2
    return turned


def owner_pairs(nx, ny):
    return [
        (i * ny + h * nx + q, reversed_bits(q, nx) * ny + h * nx + reversed_bits(i, nx))
        for i in range(nx)
        for h in range(ny // nx)
        for q in range(nx)
    ]


def cut_rows(values, block):
    nx, ny = lax.axis_size("gx"), lax.axis_size("gy")
    images = values.reshape(ny // nx, SEQ, D // ny)
    images = jnp.pad(images, ((0, 0), (0, nx * block - SEQ), (0, 0)))
    parts = images.reshape(ny // nx, nx, block, D // ny)
    parts = jnp.stack([parts[:, reversed_bits(q, nx)] for q in range(nx)], axis=1)
    return parts.reshape(ny, block, D // ny)


def cross(parts, extra=None):
    if extra is None:
        return lax.all_to_all(parts, "gy", split_axis=0, concat_axis=0, tiled=True), None
    rows, more = parts.shape[1], extra.shape[1]
    parts = jnp.concatenate((parts, jnp.pad(extra, ((0, 0), (0, -more % 16), (0, 0)))), axis=1)
    parts = lax.all_to_all(parts, "gy", split_axis=0, concat_axis=0, tiled=True)
    return parts[:, :rows], parts[:, rows : rows + more]


def spread_lines(values):
    ny = lax.axis_size("gy")
    lines = jnp.concatenate([item.reshape(-1, D // ny) for item in pieces(values, 2)], axis=0)
    return jnp.broadcast_to(lines[None], (ny,) + lines.shape)


def split_lines(vectors):
    ny = lax.axis_size("gy")
    lines = jnp.concatenate(pieces(vectors, 2), axis=0)
    return lines.reshape(-1, ny, D // ny).transpose(1, 0, 2)


def sum_lines(lines):
    return jnp.sum(lines.astype(WIDE), axis=0).reshape(2, -1, lines.shape[2]).sum(axis=0)


def move_to_owner(parts):
    nx, ny = lax.axis_size("gx"), lax.axis_size("gy")
    return lax.ppermute(parts, ("gx", "gy"), owner_pairs(nx, ny))


def join_width(parts):
    return parts.transpose(1, 0, 2).reshape(parts.shape[1], D)


def to_owner(parts):
    return join_width(move_to_owner(parts))


def leave_owner(values):
    nx, ny = lax.axis_size("gx"), lax.axis_size("gy")
    parts = values.reshape(values.shape[0], ny, D // ny).transpose(1, 0, 2)
    return lax.ppermute(parts, ("gx", "gy"), [(b, a) for a, b in owner_pairs(nx, ny)])


def join_rows(parts, packed_shape):
    nx, ny = lax.axis_size("gx"), lax.axis_size("gy")
    block = parts.shape[1]
    parts = parts.reshape(ny // nx, nx, block, D // ny)
    parts = jnp.stack([parts[:, reversed_bits(q, nx)] for q in range(nx)], axis=1)
    return parts.reshape(ny // nx, nx * block, D // ny)[:, :SEQ].reshape(packed_shape)


def norm_forward(values, gain, shift):
    center = jnp.mean(values, axis=1, keepdims=True)
    spread = jnp.mean(values * values, axis=1, keepdims=True) - center * center
    rstd = lax.rsqrt(spread + 1e-06)
    normed = (values - center) * rstd
    return (normed * gain + shift).astype(LOW), normed, rstd


def norm_backward(grad, gain, normed, rstd):
    scaled = grad * gain
    total = jnp.mean(scaled, axis=1, keepdims=True)
    along = jnp.mean(scaled * normed, axis=1, keepdims=True)
    return rstd * (scaled - total - normed * along)


def times(left, right):
    return jnp.dot(left, right, preferred_element_type=WIDE)


def times_t(left, right):
    return lax.dot_general(left, right, (((1,), (1,)), ((), ())), preferred_element_type=WIDE)


def inner_rows(left, right):
    return lax.dot_general(left, right, (((0,), (0,)), ((), ())), preferred_element_type=WIDE)


def lane_blocks(size):
    return [(start, min(256, size - start)) for start in range(0, size, 256)]


def with_row(head, row):
    return jnp.concatenate((head, row), axis=0)


def attend_forward_body(q_ref, k_ref, v_ref, mask_ref, ones_ref, *refs):
    low_ref, wide_ref, log_ref = refs[-3:]
    keys = with_row(k_ref[...], mask_ref[...]).T
    query = with_row((q_ref[...].astype(WIDE) * SCALE).astype(LOW), ones_ref[...])
    values = with_row(v_ref[...], ones_ref[...])
    for start, size in lane_blocks(query.shape[1]):
        lanes = slice(start, start + size)
        scores = jnp.dot(keys, query[:, lanes], preferred_element_type=WIDE)
        peak = jnp.max(scores, axis=0, keepdims=True)
        raised = jnp.exp(scores - peak).astype(LOW)
        mixed = jnp.dot(values, raised, preferred_element_type=WIDE)
        total = mixed[HEAD_DIM : HEAD_DIM + 1]
        attended = mixed[:HEAD_DIM] / total
        wide_ref[:, lanes] = attended
        low_ref[:, lanes] = attended.astype(LOW)
        log_ref[0, :, lanes] = peak + jnp.log(total)


def attend_forward(query, keys, values, mask, ones, first_head, count, before=()):
    cols, rows = query.shape
    heads = cols // HEAD_DIM
    head = pl.BlockSpec((HEAD_DIM, rows), lambda h: (h + first_head, 0))
    shared = pl.BlockSpec((HEAD_DIM, rows), lambda h: (0, 0))
    return pl.pallas_call(
        attend_forward_body,
        grid=(count,),
        in_specs=[head, head, head, shared, shared] + [pl.BlockSpec(memory_space=pl.ANY)] * len(before),
        out_specs=[head, head, pl.BlockSpec((1, 1, rows), lambda h: (h + first_head, 0, 0))],
        out_shape=[
            jax.ShapeDtypeStruct((cols, rows), LOW),
            jax.ShapeDtypeStruct((cols, rows), WIDE),
            jax.ShapeDtypeStruct((heads, 1, rows), WIDE),
        ],
        input_output_aliases={5 + k: k for k in range(len(before))},
        compiler_params=pltpu.CompilerParams(vmem_limit_bytes=40 * 1024 * 1024),
        cost_estimate=pl.CostEstimate(
            flops=48 * count * rows * rows * HEAD_DIM,
            bytes_accessed=12 * count * HEAD_DIM * rows,
            transcendentals=count * rows * rows,
        ),
    )(query, keys, values, mask, ones, *before)


def attend_backward_body(
    q_ref, k_ref, v_ref, g_ref, wide_ref, log_ref, mask_ref, ones_ref, *refs
):
    out_ref = refs[-1]
    rows = q_ref.shape[1]
    keys_t = k_ref[...]
    keys = with_row(keys_t, mask_ref[...]).T
    query = with_row((q_ref[...].astype(WIDE) * SCALE).astype(LOW), ones_ref[...])
    values = with_row(v_ref[...], mask_ref[...]).T[:, :HEAD_DIM]
    both = with_row(q_ref[...], g_ref[...]).T
    grad_keys = jnp.zeros((rows, HEAD_DIM), WIDE)
    grad_values = jnp.zeros((rows, HEAD_DIM), WIDE)
    for start, size in lane_blocks(rows):
        lanes = slice(start, start + size)
        grad_out = g_ref[:, lanes]
        scores = jnp.dot(keys, query[:, lanes], preferred_element_type=WIDE)
        probs = jnp.exp(scores - log_ref[0, :, lanes])
        grad_probs = jnp.dot(values, grad_out, preferred_element_type=WIDE)
        along = jnp.sum(grad_out.astype(WIDE) * wide_ref[:, lanes], axis=0, keepdims=True)
        grad_scores = (probs * (grad_probs - along)).astype(LOW)
        grad_query = jnp.dot(keys_t, grad_scores, preferred_element_type=WIDE) * SCALE
        out_ref[0, :, lanes] = grad_query.astype(LOW)
        grad_keys += jnp.dot(
            grad_scores, both[lanes, :HEAD_DIM], preferred_element_type=WIDE
        )
        grad_values += jnp.dot(
            probs.astype(LOW), both[lanes, HEAD_DIM:], preferred_element_type=WIDE
        )
    joined = jnp.concatenate((grad_keys * SCALE, grad_values), axis=1).T
    out_ref[1] = joined[:HEAD_DIM].astype(LOW)
    out_ref[2] = joined[HEAD_DIM:].astype(LOW)


def attend_backward(
    query, keys, values, grad_out, wide, log_total, mask, ones, first_head, count, before=()
):
    cols, rows = query.shape
    head = pl.BlockSpec((HEAD_DIM, rows), lambda h: (h + first_head, 0))
    shared = pl.BlockSpec((HEAD_DIM, rows), lambda h: (0, 0))
    return pl.pallas_call(
        attend_backward_body,
        grid=(count,),
        in_specs=[
            head,
            head,
            head,
            head,
            head,
            pl.BlockSpec((1, 1, rows), lambda h: (h + first_head, 0, 0)),
            shared,
            shared,
        ]
        + [pl.BlockSpec(memory_space=pl.ANY)] * len(before),
        out_specs=pl.BlockSpec((3, HEAD_DIM, rows), lambda h: (0, h + first_head, 0)),
        out_shape=jax.ShapeDtypeStruct((3, cols, rows), LOW),
        input_output_aliases={8 + k: k for k in range(len(before))},
        compiler_params=pltpu.CompilerParams(vmem_limit_bytes=40 * 1024 * 1024),
        cost_estimate=pl.CostEstimate(
            flops=56 * count * rows * rows * HEAD_DIM,
            bytes_accessed=20 * count * HEAD_DIM * rows,
            transcendentals=count * rows * rows,
        ),
    )(query, keys, values, grad_out, wide, log_total, mask, ones, *before)


def forward_body(
    near_ref, far_ref, expand_ref, shrink_ref, bias_ref, hidden_ref, slope_ref, kept_ref, sent_ref
):
    def work(rows_ref, down_ref):
        preact = jnp.dot(rows_ref[...], expand_ref[...], preferred_element_type=WIDE)
        preact = preact + bias_ref[...]
        share = 0.5 * (1.0 + lax.erf(preact * 0.5**0.5))
        hidden = (preact * share).astype(LOW)
        hidden_ref[...] = hidden
        bell = jnp.exp(preact * preact * -0.5) * (0.5 / math.pi) ** 0.5
        slope_ref[...] = share + preact * bell
        down_ref[...] = times_t(hidden, shrink_ref[...]).astype(down_ref.dtype)

    @pl.when(pl.program_id(0) < 2)
    def _():
        work(far_ref, sent_ref)

    @pl.when(pl.program_id(0) >= 2)
    def _():
        work(near_ref, kept_ref)


def backward_body(
    near_ref, far_ref, expand_ref, shrink_ref, slope_ref, pre_ref, kept_ref, sent_ref, sum_ref
):
    def work(rows_ref, back_ref):
        grad_hidden = jnp.dot(rows_ref[...], shrink_ref[...], preferred_element_type=WIDE)
        grad_pre = (grad_hidden * slope_ref[...]).astype(LOW)
        pre_ref[...] = grad_pre
        back_ref[...] = times_t(grad_pre, expand_ref[...]).astype(back_ref.dtype)
        sums = jnp.sum(grad_pre.astype(WIDE), axis=0, keepdims=True)

        @pl.when(pl.program_id(0) == 0)
        def _():
            sum_ref[...] = sums

        @pl.when(pl.program_id(0) != 0)
        def _():
            sum_ref[...] += sums

    @pl.when(pl.program_id(0) < 2)
    def _():
        work(far_ref, sent_ref)

    @pl.when(pl.program_id(0) >= 2)
    def _():
        work(near_ref, kept_ref)


def hidden_specs(rows, width, cols):
    step = rows // 2
    near = pl.BlockSpec((step, width), lambda r: (jnp.maximum(r - 2, 0), 0))
    far = pl.BlockSpec((step, width), lambda r: (jnp.minimum(r, 1), 0))
    units = pl.BlockSpec((step, cols), lambda r: ((r + 2) % 4, 0))
    weight = pl.BlockSpec((width, cols), lambda r: (0, 0))
    line = pl.BlockSpec((1, cols), lambda r: (0, 0))
    return near, far, units, weight, line


def hidden_cost(rows, width, cols):
    return pl.CostEstimate(
        flops=16 * rows * cols * width,
        bytes_accessed=10 * rows * width + 12 * rows * cols + 4 * width * cols,
        transcendentals=4 * rows * cols,
    )


def hidden_forward(near_rows, far_rows, expand, shrink, bias):
    rows, width = near_rows.shape
    cols = expand.shape[1]
    near, far, units, weight, line = hidden_specs(rows, width, cols)
    return pl.pallas_call(
        forward_body,
        grid=(4,),
        in_specs=[near, far, weight, weight, line],
        out_specs=[units, units, near, far],
        out_shape=[
            jax.ShapeDtypeStruct((2 * rows, cols), LOW),
            jax.ShapeDtypeStruct((2 * rows, cols), WIDE),
            jax.ShapeDtypeStruct((rows, width), WIDE),
            jax.ShapeDtypeStruct((rows, width), LOW),
        ],
        compiler_params=pltpu.CompilerParams(vmem_limit_bytes=40 * 1024 * 1024),
        cost_estimate=hidden_cost(rows, width, cols),
    )(near_rows, far_rows, expand, shrink, bias)


def hidden_backward(near_rows, far_rows, expand, shrink, slope):
    rows, width = near_rows.shape
    cols = expand.shape[1]
    near, far, units, weight, line = hidden_specs(rows, width, cols)
    return pl.pallas_call(
        backward_body,
        grid=(4,),
        in_specs=[near, far, weight, weight, units],
        out_specs=[units, near, far, line],
        out_shape=[
            jax.ShapeDtypeStruct((2 * rows, cols), LOW),
            jax.ShapeDtypeStruct((rows, width), WIDE),
            jax.ShapeDtypeStruct((rows, width), LOW),
            jax.ShapeDtypeStruct((1, cols), WIDE),
        ],
        compiler_params=pltpu.CompilerParams(vmem_limit_bytes=40 * 1024 * 1024),
        cost_estimate=hidden_cost(rows, width, cols),
    )(near_rows, far_rows, expand, shrink, slope)


def unit_grads_body(
    gn_ref, gf_ref, sn_ref, sf_ref, hidden_ref, pre_ref, out_ref
):
    half = gn_ref.shape[0]

    def work(near_ref, far_ref, units_ref):
        total = inner_rows(near_ref[...], units_ref[:half])
        total += inner_rows(far_ref[...], units_ref[half:])
        out_ref[...] = total.astype(LOW)

    @pl.when(pl.program_id(0) < 4)
    def _():
        work(gn_ref, gf_ref, hidden_ref)

    @pl.when(pl.program_id(0) >= 4)
    def _():
        work(sn_ref, sf_ref, pre_ref)


def unit_grads(grad_near, grad_far, second_near, second_far, hidden, grad_pre):
    half, width = grad_near.shape
    rows, cols = hidden.shape
    tile = width // 4
    early = pl.BlockSpec((half, tile), lambda r: (0, jnp.minimum(r, 3)))
    late = pl.BlockSpec((half, tile), lambda r: (0, jnp.maximum(r - 4, 0)))
    whole = pl.BlockSpec((rows, cols), lambda r: (0, 0))
    return pl.pallas_call(
        unit_grads_body,
        grid=(8,),
        in_specs=[early, early, late, late, whole, whole],
        out_specs=pl.BlockSpec((tile, cols), lambda r: (r % 4, r // 4)),
        out_shape=jax.ShapeDtypeStruct((width, 2 * cols), LOW),
        compiler_params=pltpu.CompilerParams(vmem_limit_bytes=40 * 1024 * 1024),
        cost_estimate=pl.CostEstimate(
            flops=8 * rows * cols * width,
            bytes_accessed=4 * rows * (width + cols) + 4 * width * cols,
            transcendentals=0,
        ),
    )(grad_near, grad_far, second_near, second_far, hidden, grad_pre)


def head_grads_body(place_ref, first_ref, grad_ref, mixed_ref, attended_ref, kept_ref, sent_ref):
    cols = mixed_ref.shape[0]
    heads = times(mixed_ref[...], first_ref[...]).T
    tail = times(attended_ref[...], grad_ref[...]).T
    half = pl.num_programs(0) // 2

    @pl.when(pl.program_id(0) < half)
    def _():
        sent_ref[:, :cols] = heads.astype(LOW)
        sent_ref[:, cols:] = tail.astype(LOW)

    @pl.when(pl.program_id(0) >= half)
    def _():
        kept_ref[:, :cols] = heads
        kept_ref[:, cols:] = tail


def head_grads_of(first, grad, mixed, attended):
    rows, width = first.shape
    cols, more = mixed.shape[0], attended.shape[0]
    tile = 128
    tiles = width // tile
    bits = tiles.bit_length() - 1

    def block(r, place):
        slot = (r + tiles // 2) % tiles
        turned = slot * 0
        for k in range(bits):
            turned = turned * 2 + (slot // 2**k) % 2
        return turned ^ place[0]

    narrow = pl.BlockSpec((rows, tile), lambda r, place: (0, block(r, place)))
    return pl.pallas_call(
        head_grads_body,
        grid_spec=pltpu.PrefetchScalarGridSpec(
            num_scalar_prefetch=1,
            grid=(tiles,),
            in_specs=[
                narrow,
                narrow,
                pl.BlockSpec((cols, rows), lambda r, place: (0, 0)),
                pl.BlockSpec((more, rows), lambda r, place: (0, 0)),
            ],
            out_specs=[
                pl.BlockSpec(
                    (tile, cols + more), lambda r, place: (jnp.maximum(r - tiles // 2, 0), 0)
                ),
                pl.BlockSpec(
                    (tile, cols + more), lambda r, place: (jnp.minimum(r, tiles // 2 - 1), 0)
                ),
            ],
        ),
        out_shape=[
            jax.ShapeDtypeStruct((width // 2, cols + more), WIDE),
            jax.ShapeDtypeStruct((width // 2, cols + more), LOW),
        ],
        compiler_params=pltpu.CompilerParams(vmem_limit_bytes=40 * 1024 * 1024),
        cost_estimate=pl.CostEstimate(
            flops=4 * rows * (cols + more) * width,
            bytes_accessed=2 * rows * (2 * width + cols + more) + 3 * width * (cols + more),
            transcendentals=0,
        ),
    )(lax.axis_index("gy").astype(jnp.int32)[None], first, grad, mixed, attended)


def plain_head_grads(first, grad, mixed, attended):
    joined = jnp.concatenate((times(mixed, first).T, times(attended, grad).T), axis=1).astype(LOW)
    return lax.psum_scatter(joined, "gy", scatter_dimension=0, tiled=True).astype(WIDE)


def scatter_head_grads(first, grad, mixed, attended):
    ny = lax.axis_size("gy")
    if D // ny != 128:
        return plain_head_grads(first, grad, mixed, attended)
    kept, sent = head_grads_of(first, grad, mixed, attended)
    total = kept + swap(sent, "gy", 1).astype(WIDE)
    bit = 2
    while bit < ny:
        half = total.shape[0] // 2
        received = swap(total[half:].astype(LOW), "gy", bit)
        total = total[:half] + received.astype(WIDE)
        bit *= 2
    return total


def on_device(
    tokens,
    project_in,
    query_bias,
    value_bias,
    project_out,
    output_bias,
    attention_scale,
    first_norm_gain,
    first_norm_bias,
    second_norm_gain,
    second_norm_bias,
    expand_weight,
    expand_bias,
    shrink_weight,
    shrink_bias,
    feedforward_scale,
    cotangent,
):
    nx, ny = lax.axis_size("gx"), lax.axis_size("gy")
    head_cols = project_out.shape[0]
    hidden_cols = expand_weight.shape[1]
    packed_shape = tokens.shape
    block = -(-SEQ // (nx * 16)) * 16
    column = jnp.arange(block)
    mask = jnp.concatenate(
        [
            jnp.where((lax.axis_index("gx") ^ k) * block + column < SEQ, 0.0, -1e30)
            for k in slot_blocks(nx)
        ]
    )
    top = jnp.arange(HEAD_DIM)[:, None] == 0
    mask = jnp.where(top, mask[None], 0.0).astype(LOW)
    ones = jnp.where(top, jnp.ones((1, nx * block), WIDE), 0.0).astype(LOW)

    small = jnp.concatenate(
        pieces(
            jnp.stack(
                (
                    output_bias,
                    attention_scale,
                    first_norm_gain,
                    first_norm_bias,
                    second_norm_gain,
                    second_norm_bias,
                    shrink_bias,
                    feedforward_scale,
                )
            ),
            3,
        ),
        axis=0,
    )
    heads_weight = lax.all_gather(
        jnp.concatenate((project_in.reshape(-1, 3 * head_cols), project_out.T), axis=1),
        "gy",
        axis=0,
        tiled=True,
    )
    weight_in, weight_out = heads_weight[:, : 3 * head_cols], heads_weight[:, 3 * head_cols :]
    units_weight = jnp.concatenate((expand_weight, shrink_weight.T), axis=1)

    parts, small = cross(
        jnp.concatenate((cut_rows(tokens, block), cut_rows(cotangent, block)), axis=1),
        jnp.broadcast_to(small[None], (ny,) + small.shape),
    )
    parts, small, units_weight = together(parts, small, units_weight)
    units_weight = lax.all_gather(units_weight, "gy", axis=0, tiled=True)
    weight_expand, weight_shrink = units_weight[:, :hidden_cols], units_weight[:, hidden_cols:]
    small = small.astype(WIDE)
    small = small[:, :8] + (small[:, 8:16] + small[:, 16:])
    out_shift, attn_scale, gain_one, shift_one, gain_two, shift_two, shrink_shift, ff_scale = [
        small[:, k].reshape(D) for k in range(8)
    ]
    inputs = to_owner(parts[:, :block]).astype(WIDE)

    first, first_hat, first_rstd = norm_forward(inputs, gain_one, shift_one)
    first_own, first_far = gather_far(first)
    first_far, grad_parts = together(first_far, parts[:, block:])
    first_near = jnp.concatenate((first_own, first_far), axis=0)
    first_all = jnp.concatenate((first_near, swap(first_near, "gx", 1)), axis=0)
    grad_parts = move_to_owner(grad_parts)
    mixed = lax.dot_general(
        weight_in, first_all, (((0,), (1,)), ((), ())), preferred_element_type=WIDE
    )
    query = (mixed[:head_cols] + query_bias[:, None]).astype(LOW)
    keys = mixed[head_cols : 2 * head_cols].astype(LOW)
    values = (mixed[2 * head_cols :] + value_bias[:, None]).astype(LOW)
    split = head_cols // HEAD_DIM // 2
    half = attend_forward(query, keys, values, mask, ones, 0, split)
    *half, grad_parts = together(*half, grad_parts)
    grad = join_width(grad_parts).astype(WIDE)
    grad_b = grad * ff_scale
    grad_b_own, grad_b_other = gather_far(grad_b.astype(LOW))
    attended, attended_wide, log_total = attend_forward(
        query, keys, values, mask, ones, split, head_cols // HEAD_DIM - split, half
    )
    attended, grad_b_other = together(attended, grad_b_other)
    grad_b_near = jnp.concatenate((grad_b_own, grad_b_other), axis=0)
    grad_b_far = swap(grad_b_near, "gx", 1)

    kept, sent = in_two(inner_rows(attended, weight_out.T))
    branch_a = scatter_far(scatter_near(kept, sent)) + out_shift
    middle = inputs + attn_scale * branch_a
    second, second_hat, second_rstd = norm_forward(middle, gain_two, shift_two)
    second_near, second_far = gather_halves(second)
    hidden, slope, kept_b, sent_b = hidden_forward(
        second_near, second_far, weight_expand, weight_shrink, expand_bias[None]
    )
    branch_near = scatter_near(kept_b, sent_b)
    grad_pre, kept, sent, pre_sum = hidden_backward(
        grad_b_near, grad_b_far, weight_expand, weight_shrink, slope
    )
    wide_grads = unit_grads(grad_b_near, grad_b_far, second_near, second_far, hidden, grad_pre)
    grad_second, wide_grads = together(scatter_far(scatter_near(kept, sent)), wide_grads)
    wide_grads = lax.psum_scatter(wide_grads, "gy", scatter_dimension=0, tiled=True).astype(WIDE)

    grad_middle = grad + norm_backward(grad_second, gain_two, second_hat, second_rstd)
    grad_a = grad_middle * attn_scale
    grad_a_near, branch_near = together(gather_step(grad_a.astype(LOW)), branch_near)
    grad_a_all = jnp.concatenate((grad_a_near, swap(grad_a_near, "gx", 1)), axis=0)
    branch_kept, branch_far = scatter_last(branch_near)
    grad_attended = lax.dot_general(
        weight_out, grad_a_all, (((0,), (1,)), ((), ())), preferred_element_type=WIDE
    ).astype(LOW)
    half = attend_backward(
        query, keys, values, grad_attended, attended_wide, log_total, mask, ones, 0, split
    )
    half, branch_far = together(half, branch_far)
    branch_b = branch_kept + branch_far.astype(WIDE) + shrink_shift
    output_parts = leave_owner((middle + ff_scale * branch_b).astype(LOW))
    grad_mixed = attend_backward(
        query,
        keys,
        values,
        grad_attended,
        attended_wide,
        log_total,
        mask,
        ones,
        split,
        head_cols // HEAD_DIM - split,
        (half,),
    )
    grad_mixed, output_parts = together(grad_mixed, output_parts)
    early = jnp.stack(
        [
            jnp.sum(item, axis=0)
            for item in (grad_second * second_hat, grad_second, grad_b, grad * branch_b)
        ]
    )
    output_parts, lines = cross(
        output_parts, jnp.concatenate((split_lines(early), spread_lines(pre_sum[0])), axis=1)
    )
    block_output = join_rows(output_parts, packed_shape)
    early, pre_sum = sum_lines(lines[:, :8]), sum_lines(lines[:, 8:]).reshape(-1)

    joined = grad_mixed.reshape(3 * head_cols, nx * block)
    kept, sent = in_two(inner_rows(joined, weight_in.T))
    near, joined = together(scatter_near(kept, sent), joined)
    grad_first = scatter_far(near)
    head_grads = scatter_head_grads(first_all, grad_a_all, joined, attended)
    input_gradient = grad_middle + norm_backward(grad_first, gain_one, first_hat, first_rstd)
    input_parts = leave_owner(input_gradient.astype(LOW))
    late = jnp.stack(
        [
            jnp.sum(item, axis=0)
            for item in (grad_a, grad_middle * branch_a, grad_first * first_hat, grad_first)
        ]
    )
    head_sums = jnp.concatenate(
        (
            jnp.sum(grad_mixed[0].astype(WIDE), axis=1),
            jnp.sum(grad_mixed[2].astype(WIDE), axis=1),
        )
    )
    input_parts, lines = cross(
        input_parts, jnp.concatenate((split_lines(late), spread_lines(head_sums)), axis=1)
    )
    input_gradient = join_rows(input_parts, packed_shape).astype(WIDE)
    late, head_sums = sum_lines(lines[:, :8]), sum_lines(lines[:, 8:]).reshape(-1)
    sums = jnp.concatenate((late, early), axis=0)
    bit = 1
    while bit < nx:
        sums = sums + swap(sums, "gx", bit)
        bit *= 2
    return (
        block_output,
        input_gradient,
        head_grads[:, : 3 * head_cols].reshape(-1, 3, head_cols),
        head_sums[:head_cols],
        head_sums[head_cols:],
        head_grads[:, 3 * head_cols :].T,
        sums[0],
        sums[1],
        sums[2],
        sums[3],
        sums[4],
        sums[5],
        wide_grads[:, hidden_cols:],
        pre_sum,
        wide_grads[:, :hidden_cols].T,
        sums[6],
        sums[7],
    )


def solution(mesh):
    rows = P("gx", "gy", None)
    wide, heads = P("gy"), P("gx")
    placed = (
        rows, P("gy", None, "gx"), heads, heads, P("gx", "gy"), wide, wide, wide, wide, wide, wide,
        P("gy", "gx"), heads, P("gx", "gy"), wide, wide, rows,
    )
    results = (
        rows, rows, P("gy", None, "gx"), heads, heads, P("gx", "gy"), wide, wide, wide, wide, wide,
        wide, P("gy", "gx"), heads, P("gx", "gy"), wide, wide,
    )
    return jax.shard_map(
        on_device, mesh=mesh, in_specs=placed, out_specs=results, check_vma=False
    )
```

time: 511 us -> 442 us (0.86); the launches traced: 501 us -> 438 us
  waiting for transfers between devices: 233 us -> 185 us
  Pallas kernels: 60.7 us -> 83.4 us
  matrix products: 28.8 us -> 9.93 us
  starting transfers between devices: 88.9 us -> 76.2 us
  local copies, waits for them, and re-layouts: 41.9 us -> 34.6 us
    ppermute x27 -> x21, waiting for transfers between devices: 180 us -> 130 us  [swap(): return lax.ppermute(values, axis, [(k, k ^ bit) for k in range(size)])]
    pallas_call x3 -> x8, Pallas kernels: 60.7 us -> 83.4 us  [the longest x2 22.3 us: attend_backward(): pl.pallas_call(attend_backward_body, grid=(count,), in_specs=[head, head,...]
    all_to_all x4 -> x3, starting transfers between devices: 40.5 us -> 18.2 us  [cross(): parts = lax.all_to_all(parts, 'gy', split_axis=0, concat_axis=0, tiled=True)]
    dot_general x4 -> x2, matrix products: 14.5 us -> 4.44 us  [inner_rows(): lax.dot_general(left, right, (((0,), (0,)), ((), ())), preferred_element_...]
    ppermute x27 -> x21, starting transfers between devices: 43.4 us -> 52.4 us  [swap(): return lax.ppermute(values, axis, [(k, k ^ bit) for k in range(size)])]
    add x11, other arithmetic: 4.75 us -> 12.5 us  [the longest x4 7.81 us: scatter_near(): return kept + swap(sent, 'gx', 1).astype(WIDE)]
    all_gather x1 -> x2, waiting for transfers between devices: 8.61 us -> 16.4 us  [the longest x1 16.4 us: on_device(): lax.all_gather(jnp.concatenate((project_in.reshape(-1, 3 * head_cols), pr...]
    dot_general x2 -> x0, matrix products: 6.75 us -> none  [times_t(): lax.dot_general(left, right, (((1,), (1,)), ((), ())), preferred_element_...]
  transfers between devices with their start and end apart: 38 -> 31, of which waited for: 21 -> 19; matrix products, arithmetic and copies ran while one was open for 16% -> 13% of each run, Pallas kernels for 5% -> 17%
where the time goes in v3:
time: 442 us; the launch traced here: 438 us
  waiting for transfers between devices  185 us (42%)
  Pallas kernels  83.4 us (19%)
  starting transfers between devices  76.2 us (17%)
  local copies, waits for them, and re-layouts  34.6 us (8%)
  other arithmetic  33.9 us (8%)
  between operations  15.3 us (3%)
  matrix products  9.93 us (2%)
    ppermute x21, waiting for transfers between devices, swap(): return lax.ppermute(values, axis, [(k, k ^ bit) for k in range(size)])  130 us
    ppermute x21, starting transfers between devices, swap(): return lax.ppermute(values, axis, [(k, k ^ bit) for k in range(size)])  52.4 us
    all_to_all x3, waiting for transfers between devices, cross(): parts = lax.all_to_all(parts, 'gy', split_axis=0, concat_axis=0, tiled=True)  37.9 us
    pallas_call x2, Pallas kernels, attend_backward(): pl.pallas_call(attend_backward_body, grid=(count,), in_specs=[head, head,...  22.3 us
    pallas_call x2, Pallas kernels, attend_forward(): pl.pallas_call(attend_forward_body, grid=(count,), in_specs=[head, head,...  20.8 us
    all_to_all x3, starting transfers between devices, cross(): parts = lax.all_to_all(parts, 'gy', split_axis=0, concat_axis=0, tiled=True)  18.2 us
    unnamed x134, local copies, waits for them, and re-layouts  17 us
    all_gather x1, waiting for transfers between devices, on_device(): lax.all_gather(jnp.concatenate((project_in.reshape(-1, 3 * head_cols), pr...  16.4 us
  transfers between devices with their start and end apart: 31, of which 19 were waited for; matrix products, arithmetic and copies ran while one was open for 13% of the time, Pallas kernels for 17%

profile of v3, /device:TPU:0, one launch (start us, length us, event | category | flops | bytes accessed | tf_op | source)
XLA Modules:
  0.0 438.1 jit_solution(12684586022567993111)
XLA Ops:
  12.0 7.4 %all-to-all-start = ((bf16[8,736,128]{2,1,0:T(8,128)(2,1)}), bf16[8,736,128]{2,1,0:T(8,128)(2,1)S(1)}, u32[]{:S(2)}, u32[]{:S(2)}) async-start(bf16[8,736,128]{2,1,0:T(8,128)(2,1)} %fusion.1), calls=%async_computation | async-start | bytes 3014656 | tf_op jit(solution)/shard_map/all_to_all | solution.py:120
  20.6 34.4 %all-to-all-done = bf16[8,736,128]{2,1,0:T(8,128)(2,1)S(1)} async-done(((bf16[8,736,128]{2,1,0:T(8,128)(2,1)}), bf16[8,736,128]{2,1,0:T(8,128)(2,1)S(1)}, u32[]{:S(2)}, u32[]{:S(2)}) %all-to-all-start) | async-done | bytes 1507360 | tf_op jit(solution)/shard_map/all_to_all | solution.py:120
  58.3 23.9 %collective-permute-start.1 = (bf16[352,1024]{1,0:T(8,128)(2,1)S(1)}, bf16[352,1024]{1,0:T(8,128)(2,1)S(1)}, u32[]{:S(2)}, u32[]{:S(2)}) collective-permute-start(bf16[352,1024]{1,0:T(8,128)(2,1)S(1)} %add_convert_fusion.3), channel_id=1, source_target_pairs={{0,16},{8,24},{16,0},{24,8},{1,17},{9,25},{17,1},{25,9},{2,18},{10... | collective-permute-start | bytes 2162696 | tf_op jit(solution)/shard_map/ppermute | solution.py:20
  82.2 11.4 %collective-permute-done.1 = bf16[352,1024]{1,0:T(8,128)(2,1)S(1)} collective-permute-done((bf16[352,1024]{1,0:T(8,128)(2,1)S(1)}, bf16[352,1024]{1,0:T(8,128)(2,1)S(1)}, u32[]{:S(2)}, u32[]{:S(2)}) %collective-permute-start.1) | collective-permute-done | bytes 720928 | tf_op jit(solution)/shard_map/ppermute | solution.py:20
  97.3 16.4 %all-gather.3.cloned.1.call-done = bf16[1024,1024]{0,1:T(8,128)(2,1)} async-done(((bf16[128,1024]{0,1:T(8,128)(2,1)}), bf16[1024,1024]{0,1:T(8,128)(2,1)}) %all-gather.3.cloned.1.call-update) | async-done | bytes 2097168 | tf_op jit(solution)/shard_map/all_gather | solution.py:596
  113.7 4.5 %fusion.12 = f32[768,1408]{1,0:T(8,128)S(1)} fusion(bf16[1024,1024]{0,1:T(8,128)(2,1)} %all-gather.3.cloned.1.call-done, bf16[704,1024]{1,0:T(8,128)(2,1)} %collective-permute-done.2, bf16[352,1024]{1,0:T(8,128)(2,1)S(1)} %collective-permute-done.1, bf16[352,1024]{1,0:T(8,128)(2,1)S(1)} %add_convert_fusion.3), kind=kOutput, calls=%fused_computation.60 | convolution fusion | flops 2223243264 | bytes 8781824 | tf_op jit(solution)/shard_map/dot_general | solution.py:625
  119.2 10.1 %shard_map.296 = (bf16[256,1408]{1,0:T(8,128)(2,1)S(1)}, f32[256,1408]{1,0:T(8,128)S(1)}, f32[4,1,1408]{2,1,0:T(1,128)S(1)}) custom-call(bf16[256,1408]{1,0:T(8,128)(2,1)S(1)} %get-tuple-element.180.q_ref, bf16[256,1408]{1,0:T(8,128)(2,1)S(1)} %slice.480.k_ref, bf16[256,1408]{1,0:T(8,128)(2,1)S(1)} %get-tuple-element.179.v_ref, ...), custom_call_target="tpu_custom_call" | custom-call | flops 12180258816 | bytes 2162688 | tf_op jit(solution)/shard_map/pallas_call | solution.py:225
  129.6 10.7 %shard_map.297 = (bf16[256,1408]{1,0:T(8,128)(2,1)S(1)}, f32[256,1408]{1,0:T(8,128)S(1)}, f32[4,1,1408]{2,1,0:T(1,128)S(1)}) custom-call(bf16[256,1408]{1,0:T(8,128)(2,1)S(1)} %get-tuple-element.180.q_ref, bf16[256,1408]{1,0:T(8,128)(2,1)S(1)} %slice.480.k_ref, ...), custom_call_target="tpu_custom_call", output_to_operand_aliasing={{0}: (5, {}), {1}: (6, {}), {2}: (7, {})} | custom-call | flops 12180258816 | bytes 2162688 | tf_op jit(solution)/shard_map/pallas_call | solution.py:225
  140.3 6.3 %collective-permute-done.4 = bf16[352,1024]{1,0:T(8,128)(2,1)S(1)} collective-permute-done((bf16[352,1024]{1,0:T(8,128)(2,1)S(1)}, bf16[352,1024]{1,0:T(8,128)(2,1)S(1)}, u32[]{:S(2)}, u32[]{:S(2)}) %collective-permute-start.4) | collective-permute-done | bytes 720928 | tf_op jit(solution)/shard_map/ppermute | solution.py:20
  149.0 3.2 collective-permute-done.5
  153.3 17.9 %collective-permute-done.6 = bf16[352,1024]{1,0:T(8,128)(2,1)S(1)} collective-permute-done((bf16[352,1024]{1,0:T(8,128)(2,1)S(1)}, bf16[352,1024]{1,0:T(8,128)(2,1)S(1)}, u32[]{:S(2)}, u32[]{:S(2)}) %collective-permute-start.6) | collective-permute-done | bytes 720928 | tf_op jit(solution)/shard_map/ppermute | solution.py:20
  173.1 16.8 %collective-permute-done.8 = bf16[352,1024]{1,0:T(8,128)(2,1)S(1)} collective-permute-done((bf16[352,1024]{1,0:T(8,128)(2,1)S(1)}, bf16[352,1024]{1,0:T(8,128)(2,1)S(1)}, u32[]{:S(2)}, u32[]{:S(2)}) %collective-permute-start.8) | collective-permute-done | bytes 720928 | tf_op jit(solution)/shard_map/ppermute | solution.py:20
  191.9 2.8 fusion.39
  197.2 9.3 %shard_map.298 = (bf16[1408,1024]{1,0:T(8,128)(2,1)S(1)}, f32[1408,1024]{1,0:T(8,128)}, f32[704,1024]{1,0:T(8,128)S(1)}, bf16[704,1024]{1,0:T(8,128)(2,1)}) custom-call(bf16[704,1024]{1,0:T(8,128)(2,1)S(1)} %copy-done.5, bf16[704,1024]{1,0:T(8,128)(2,1)S(1)} %copy-done.17, bf16[1024,1024]{1,0:T(8,128)(2,1)S(1)} %get-tuple-element.182.expand_ref, ...), custom_call_target="tpu_custom_call" | custom-call | flops 11811160064 | bytes 20054016 | tf_op jit(solution)/shard_map/pallas_call | solution.py:381
  206.4 8.7 %shard_map.299 = (bf16[1408,1024]{1,0:T(8,128)(2,1)S(1)}, f32[704,1024]{1,0:T(8,128)S(1)}, bf16[704,1024]{1,0:T(8,128)(2,1)S(1)}, f32[1,1024]{1,0:T(1,128)S(1)}) custom-call(bf16[704,1024]{1,0:T(8,128)(2,1)} %pad_maximum_fusion.2.near_ref.gn_ref, bf16[704,1024]{1,0:T(8,128)(2,1)} %collective-permute-done.7.far_ref.gf_ref, ...), custom_call_target="tpu_custom_call" | custom-call | flops 11811160064 | bytes 20054016 | tf_op jit(solution)/shard_map/pallas_call | solution.py:401
  222.8 11.1 %shard_map.300 = bf16[1024,2048]{1,0:T(8,128)(2,1)} custom-call(bf16[704,1024]{1,0:T(8,128)(2,1)} %pad_maximum_fusion.2.near_ref.gn_ref, bf16[704,1024]{1,0:T(8,128)(2,1)} %collective-permute-done.7.far_ref.gf_ref, bf16[704,1024]{1,0:T(8,128)(2,1)S(1)} %copy-done.5, bf16[704,1024]{1,0:T(8,128)(2,1)S(1)} %copy-done.17, ...), custom_call_target="tpu_custom_call" | custom-call | flops 11811160064 | bytes 15728640 | tf_op jit(solution)/shard_map/pallas_call | solution.py:443
  233.9 5.0 %collective-permute-done.11 = bf16[352,1024]{1,0:T(8,128)(2,1)} collective-permute-done((bf16[352,1024]{1,0:T(8,128)(2,1)}, bf16[352,1024]{1,0:T(8,128)(2,1)}, u32[]{:S(2)}, u32[]{:S(2)}) %collective-permute-start.11) | collective-permute-done | bytes 720928 | tf_op jit(solution)/shard_map/ppermute | solution.py:20
  244.1 3.4 convert_add_fusion
  247.6 13.8 %collective-permute-done.12 = bf16[352,1024]{1,0:T(8,128)(2,1)S(1)} collective-permute-done((bf16[352,1024]{1,0:T(8,128)(2,1)S(1)}, bf16[352,1024]{1,0:T(8,128)(2,1)S(1)}, u32[]{:S(2)}, u32[]{:S(2)}) %collective-permute-start.12) | collective-permute-done | bytes 720928 | tf_op jit(solution)/shard_map/ppermute | solution.py:20
  268.2 11.0 %shard_map.301.refs_0_ = bf16[3,256,1408]{2,1,0:T(8,128)(2,1)S(1)} custom-call(bf16[256,1408]{1,0:T(8,128)(2,1)S(1)} %copy-done.15, bf16[256,1408]{1,0:T(8,128)(2,1)S(1)} %copy-done.11, bf16[256,1408]{1,0:T(8,128)(2,1)S(1)} %copy-done.13, bf16[256,1408]{1,0:T(8,128)(2,1)S(1)} %convolution_convert_fusion.g_ref, f32[256,1408]{1,0:T(8,128)S(1)} %copy-done.22, ...), custom_call_target="tpu_custom_call" | custom-call | flops 14210301952 | bytes 3604480 | tf_op jit(solution)/shard_map/pallas_call | solution.py:284
  283.0 11.3 %shard_map.302 = bf16[3,256,1408]{2,1,0:T(8,128)(2,1)S(1)} custom-call(bf16[256,1408]{1,0:T(8,128)(2,1)S(1)} %copy-done.15, bf16[256,1408]{1,0:T(8,128)(2,1)S(1)} %copy-done.11, bf16[256,1408]{1,0:T(8,128)(2,1)S(1)} %copy-done.13, bf16[256,1408]{1,0:T(8,128)(2,1)S(1)} %convolution_convert_fusion.g_ref, ...), custom_call_target="tpu_custom_call", output_to_operand_aliasing={{}: (8, {})} | custom-call | flops 14210301952 | bytes 3604480 | tf_op jit(solution)/shard_map/pallas_call | solution.py:284
  299.7 17.8 %collective-permute-start.17 = (bf16[704,1024]{1,0:T(8,128)(2,1)}, bf16[704,1024]{1,0:T(8,128)(2,1)}, u32[]{:S(2)}, u32[]{:S(2)}) collective-permute-start(bf16[704,1024]{1,0:T(8,128)(2,1)} %slice.474), channel_id=1, source_target_pairs={{0,8},{8,0},{16,24},{24,16},{1,9},{9,1},{17,25},{25,17},{2,10},{10... | collective-permute-start | bytes 4325384 | tf_op jit(solution)/shard_map/ppermute | solution.py:20
  320.9 5.3 %all-to-all-start.1 = ((bf16[8,384,128]{2,1,0:T(8,128)(2,1)}), bf16[8,384,128]{2,1,0:T(8,128)(2,1)}, u32[]{:S(2)}, u32[]{:S(2)}) async-start(bf16[8,384,128]{2,1,0:T(8,128)(2,1)} %pad_maximum_fusion.5), calls=%async_computation.1 | async-start | bytes 1572864 | tf_op jit(solution)/shard_map/all_to_all | solution.py:120
  326.3 3.1 slice_add_fusion
  330.7 11.2 %shard_map.303 = (f32[512,1024]{1,0:T(8,128)S(1)}, bf16[512,1024]{1,0:T(8,128)(2,1)}) custom-call(s32[1]{0:T(128)} %bitcast.47.place_ref, bf16[1408,1024]{1,0:T(8,128)(2,1)S(1)} %pad_maximum_fusion.first_ref, bf16[1408,1024]{1,0:T(8,128)(2,1)S(1)} %copy-done.9, bf16[768,1408]{1,0:T(8,128)(2,1)S(1)} %bitcast.138, bf16[256,1408]{1,0:T(8,128)(2,1)S(1)} %copy-done.3), custom_call_target="tpu_custom_call" | custom-call | flops 5905580032 | bytes 11796480 | tf_op jit(solution)/shard_map/pallas_call | solution.py:490
  343.9 3.9 collective-permute-done.18
  352.8 3.5 all-to-all-done.1
  357.5 19.2 %collective-permute-done.20 = bf16[512,1024]{1,0:T(8,128)(2,1)} collective-permute-done((bf16[512,1024]{1,0:T(8,128)(2,1)}, bf16[512,1024]{1,0:T(8,128)(2,1)}, u32[]{:S(2)}, u32[]{:S(2)}) %collective-permute-start.20) | collective-permute-done | bytes 1048608 | tf_op jit(solution)/shard_map/ppermute | solution.py:20
  379.7 2.7 collective-permute-start.21
  383.4 5.5 %all-to-all-start.2 = ((bf16[8,368,128]{2,1,0:T(8,128)(2,1)}), bf16[8,368,128]{2,1,0:T(8,128)(2,1)S(1)}, u32[]{:S(2)}, u32[]{:S(2)}) async-start(bf16[8,368,128]{2,1,0:T(8,128)(2,1)} %pad_maximum_fusion.6), calls=%async_computation.2 | async-start | bytes 1507328 | tf_op jit(solution)/shard_map/all_to_all | solution.py:120
  389.1 6.0 %collective-permute-done.21 = bf16[256,1024]{1,0:T(8,128)(2,1)} collective-permute-done((bf16[256,1024]{1,0:T(8,128)(2,1)S(1)}, bf16[256,1024]{1,0:T(8,128)(2,1)}, u32[]{:S(2)}, u32[]{:S(2)}) %collective-permute-start.21) | collective-permute-done | bytes 524320 | tf_op jit(solution)/shard_map/ppermute | solution.py:20
  401.2 19.5 %collective-permute-done.22 = bf16[128,1024]{1,0:T(8,128)(2,1)S(1)} collective-permute-done((bf16[128,1024]{1,0:T(8,128)(2,1)S(1)}, bf16[128,1024]{1,0:T(8,128)(2,1)S(1)}, u32[]{:S(2)}, u32[]{:S(2)}) %collective-permute-start.22) | collective-permute-done | bytes 262176 | tf_op jit(solution)/shard_map/ppermute | solution.py:20
  (293 shorter events, 85.8 us)
Async XLA Ops:
  12.0 43.0 %all-to-all-start = ((bf16[8,736,128]{2,1,0:T(8,128)(2,1)}), bf16[8,736,128]{2,1,0:T(8,128)(2,1)S(1)}, u32[]{:S(2)}, u32[]{:S(2)}) async-start(bf16[8,736,128]{2,1,0:T(8,128)(2,1)} %fusion.1), calls=%async_computation | async-start | bytes 3014656 | tf_op jit(solution)/shard_map/all_to_all | solution.py:120
  19.4 94.3 %all-gather.3.cloned.1.call-start = ((), (), s32[]{:S(2)}) async-start(), calls=%async_computation.4 | async-start | bytes 2359296 | tf_op jit(solution)/shard_map/all_gather | solution.py:596
  56.0 1.6 collective-permute-start
  57.5 134.4 %all-gather.5.cloned.1.call-start = ((), (), s32[]{:S(2)}) async-start(), calls=%async_computation.5 | async-start | bytes 4718592 | tf_op jit(solution)/shard_map/all_gather | solution.py:610
  57.6 113.6 %copy-start.26 = (bf16[8,352,128]{2,1,0:T(8,128)(2,1)}, bf16[8,352,128]{2,1,0:T(8,128)(2,1)S(1)}, u32[]{:S(2)}) copy-start(bf16[8,352,128]{2,1,0:T(8,128)(2,1)S(1)} %collective-permute-done) | copy-start | bytes 2162692
  58.3 35.3 %collective-permute-start.1 = (bf16[352,1024]{1,0:T(8,128)(2,1)S(1)}, bf16[352,1024]{1,0:T(8,128)(2,1)S(1)}, u32[]{:S(2)}, u32[]{:S(2)}) collective-permute-start(bf16[352,1024]{1,0:T(8,128)(2,1)S(1)} %add_convert_fusion.3), channel_id=1, source_target_pairs={{0,16},{8,24},{16,0},{24,8},{1,17},{9,25},{17,1},{25,9},{2,18},{10... | collective-permute-start | bytes 2162696 | tf_op jit(solution)/shard_map/ppermute | solution.py:20
  95.0 18.7 %collective-permute-start.2 = (bf16[704,1024]{1,0:T(8,128)(2,1)}, bf16[704,1024]{1,0:T(8,128)(2,1)}, u32[]{:S(2)}, u32[]{:S(2)}) collective-permute-start(bf16[704,1024]{1,0:T(8,128)(2,1)} %pad_maximum_fusion.1), channel_id=1, source_target_pairs={{0,8},{8,0},{16,24},{24,16},{1,9},{9,1},{17,25},{25,17},{2,10},{10... | collective-permute-start | bytes 4325384 | tf_op jit(solution)/shard_map/ppermute | solution.py:20
  95.2 333.0 %reduce-scatter.2.cloned.1.call-start = ((), (), s32[]{:S(2)}) async-start(), calls=%async_computation.6 | async-start | bytes 4718592 | tf_op jit(solution)/shard_map/reduce_scatter | solution.py:658
  95.3 34.1 %collective-permute-start.3 = (bf16[8,352,128]{2,1,0:T(8,128)(2,1)}, bf16[8,352,128]{2,1,0:T(8,128)(2,1)S(1)}, u32[]{:S(2)}, u32[]{:S(2)}) collective-permute-start(bf16[8,352,128]{2,1,0:T(8,128)(2,1)} %get-tuple-element.60), channel_id=1, source_target_pairs={{0,0},{1,16},{2,8},{3,24},{4,4},{5,20},{6,12},{7,28},{8,2},{9,18},... | collective-permute-start | bytes 2162696 | tf_op jit(solution)/shard_map/ppermute | solution.py:142
  129.5 17.1 %collective-permute-start.4 = (bf16[352,1024]{1,0:T(8,128)(2,1)S(1)}, bf16[352,1024]{1,0:T(8,128)(2,1)S(1)}, u32[]{:S(2)}, u32[]{:S(2)}) collective-permute-start(bf16[352,1024]{1,0:T(8,128)(2,1)S(1)} %fusion.4), channel_id=1, source_target_pairs={{0,16},{8,24},{16,0},{24,8},{1,17},{9,25},{17,1},{25,9},{2,18},{10... | collective-permute-start | bytes 2162696 | tf_op jit(solution)/shard_map/ppermute | solution.py:20
  148.9 3.3 collective-permute-start.5
  152.9 18.2 %collective-permute-start.6 = (bf16[352,1024]{1,0:T(8,128)(2,1)S(1)}, bf16[352,1024]{1,0:T(8,128)(2,1)S(1)}, u32[]{:S(2)}, u32[]{:S(2)}) collective-permute-start(bf16[352,1024]{1,0:T(8,128)(2,1)S(1)} %slice.479), channel_id=1, source_target_pairs={{0,16},{8,24},{16,0},{24,8},{1,17},{9,25},{17,1},{25,9},{2,18},{10... | collective-permute-start | bytes 2162696 | tf_op jit(solution)/shard_map/ppermute | solution.py:20
  172.4 17.5 %collective-permute-start.8 = (bf16[352,1024]{1,0:T(8,128)(2,1)S(1)}, bf16[352,1024]{1,0:T(8,128)(2,1)S(1)}, u32[]{:S(2)}, u32[]{:S(2)}) collective-permute-start(bf16[352,1024]{1,0:T(8,128)(2,1)S(1)} %add_convert_fusion.2), channel_id=1, source_target_pairs={{0,16},{8,24},{16,0},{24,8},{1,17},{9,25},{17,1},{25,9},{2,18},{10... | collective-permute-start | bytes 2162696 | tf_op jit(solution)/shard_map/ppermute | solution.py:20
  190.0 4.6 %collective-permute-start.9 = (bf16[704,1024]{1,0:T(8,128)(2,1)S(1)}, bf16[704,1024]{1,0:T(8,128)(2,1)S(1)}, u32[]{:S(2)}, u32[]{:S(2)}) collective-permute-start(bf16[704,1024]{1,0:T(8,128)(2,1)S(1)} %pad_maximum_fusion.3.near_ref.sn_ref), channel_id=1, source_target_pairs={{0,8},{8,0},{16,24},{24,16},{1,9},{9,1},{17,25},{25,17},{2,10},{10... | collective-permute-start | bytes 4325384 | tf_op jit(solution)/shard_map/ppermute | solution.py:20
  191.6 14.8 %collective-permute-start.7 = (bf16[704,1024]{1,0:T(8,128)(2,1)}, bf16[704,1024]{1,0:T(8,128)(2,1)}, u32[]{:S(2)}, u32[]{:S(2)}) collective-permute-start(bf16[704,1024]{1,0:T(8,128)(2,1)} %pad_maximum_fusion.2.near_ref.gn_ref), channel_id=1, source_target_pairs={{0,8},{8,0},{16,24},{24,16},{1,9},{9,1},{17,25},{25,17},{2,10},{10... | collective-permute-start | bytes 4325384 | tf_op jit(solution)/shard_map/ppermute | solution.py:20
  215.2 3.3 collective-permute-start.10
  215.5 28.6 %collective-permute-start.13 = (bf16[704,1024]{1,0:T(8,128)(2,1)}, bf16[704,1024]{1,0:T(8,128)(2,1)}, u32[]{:S(2)}, u32[]{:S(2)}) collective-permute-start(bf16[704,1024]{1,0:T(8,128)(2,1)} %get-tuple-element.76), channel_id=1, source_target_pairs={{0,8},{8,0},{16,24},{24,16},{1,9},{9,1},{17,25},{25,17},{2,10},{10... | collective-permute-start | bytes 4325384 | tf_op jit(solution)/shard_map/ppermute | solution.py:20
  220.3 18.6 %collective-permute-start.11 = (bf16[352,1024]{1,0:T(8,128)(2,1)}, bf16[352,1024]{1,0:T(8,128)(2,1)}, u32[]{:S(2)}, u32[]{:S(2)}) collective-permute-start(bf16[352,1024]{1,0:T(8,128)(2,1)} %slice.478), channel_id=1, source_target_pairs={{0,16},{8,24},{16,0},{24,8},{1,17},{9,25},{17,1},{25,9},{2,18},{10... | collective-permute-start | bytes 2162696 | tf_op jit(solution)/shard_map/ppermute | solution.py:20
  243.8 17.6 %collective-permute-start.12 = (bf16[352,1024]{1,0:T(8,128)(2,1)S(1)}, bf16[352,1024]{1,0:T(8,128)(2,1)S(1)}, u32[]{:S(2)}, u32[]{:S(2)}) collective-permute-start(bf16[352,1024]{1,0:T(8,128)(2,1)S(1)} %multiply_convert_fusion), channel_id=1, source_target_pairs={{0,16},{8,24},{16,0},{24,8},{1,17},{9,25},{17,1},{25,9},{2,18},{10... | collective-permute-start | bytes 2162696 | tf_op jit(solution)/shard_map/ppermute | solution.py:20
  261.5 3.3 collective-permute-start.14
  263.0 18.6 %collective-permute-start.15 = (bf16[352,1024]{1,0:T(8,128)(2,1)S(1)}, bf16[352,1024]{1,0:T(8,128)(2,1)S(1)}, u32[]{:S(2)}, u32[]{:S(2)}) collective-permute-start(bf16[352,1024]{1,0:T(8,128)(2,1)S(1)} %slice.477), channel_id=1, source_target_pairs={{0,16},{8,24},{16,0},{24,8},{1,17},{9,25},{17,1},{25,9},{2,18},{10... | collective-permute-start | bytes 2162696 | tf_op jit(solution)/shard_map/ppermute | solution.py:20
  282.3 12.0 %collective-permute-start.16 = (bf16[8,352,128]{2,1,0:T(8,128)(2,1)S(1)}, bf16[8,352,128]{2,1,0:T(8,128)(2,1)S(1)}, u32[]{:S(2)}, u32[]{:S(2)}) collective-permute-start(bf16[8,352,128]{2,1,0:T(8,128)(2,1)S(1)} %bitcast.152), channel_id=1, source_target_pairs={{0,0},{16,1},{8,2},{24,3},{4,4},{20,5},{12,6},{28,7},{2,8},{18,9},... | collective-permute-start | bytes 2162696 | tf_op jit(solution)/shard_map/ppermute | solution.py:156
  299.7 26.5 %collective-permute-start.17 = (bf16[704,1024]{1,0:T(8,128)(2,1)}, bf16[704,1024]{1,0:T(8,128)(2,1)}, u32[]{:S(2)}, u32[]{:S(2)}) collective-permute-start(bf16[704,1024]{1,0:T(8,128)(2,1)} %slice.474), channel_id=1, source_target_pairs={{0,8},{8,0},{16,24},{24,16},{1,9},{9,1},{17,25},{25,17},{2,10},{10... | collective-permute-start | bytes 4325384 | tf_op jit(solution)/shard_map/ppermute | solution.py:20
  320.9 35.4 %all-to-all-start.1 = ((bf16[8,384,128]{2,1,0:T(8,128)(2,1)}), bf16[8,384,128]{2,1,0:T(8,128)(2,1)}, u32[]{:S(2)}, u32[]{:S(2)}) async-start(bf16[8,384,128]{2,1,0:T(8,128)(2,1)} %pad_maximum_fusion.5), calls=%async_computation.1 | async-start | bytes 1572864 | tf_op jit(solution)/shard_map/all_to_all | solution.py:120
  329.5 18.3 %collective-permute-start.18 = (bf16[352,1024]{1,0:T(8,128)(2,1)S(1)}, bf16[352,1024]{1,0:T(8,128)(2,1)S(1)}, u32[]{:S(2)}, u32[]{:S(2)}) collective-permute-start(bf16[352,1024]{1,0:T(8,128)(2,1)S(1)} %slice.476), channel_id=1, source_target_pairs={{0,16},{8,24},{16,0},{24,8},{1,17},{9,25},{17,1},{25,9},{2,18},{10... | collective-permute-start | bytes 2162696 | tf_op jit(solution)/shard_map/ppermute | solution.py:20
  342.0 34.7 %collective-permute-start.20 = (bf16[512,1024]{1,0:T(8,128)(2,1)}, bf16[512,1024]{1,0:T(8,128)(2,1)}, u32[]{:S(2)}, u32[]{:S(2)}) collective-permute-start(bf16[512,1024]{1,0:T(8,128)(2,1)} %get-tuple-element.89), channel_id=1, source_target_pairs={{0,1},{1,0},{2,3},{3,2},{4,5},{5,4},{6,7},{7,6},{8,9},{9,8},{10,11... | collective-permute-start | bytes 3145736 | tf_op jit(solution)/shard_map/ppermute | solution.py:20
  350.2 32.3 %collective-permute-start.19 = (bf16[8,352,128]{2,1,0:T(8,128)(2,1)}, bf16[8,352,128]{2,1,0:T(8,128)(2,1)S(1)}, u32[]{:S(2)}, u32[]{:S(2)}) collective-permute-start(bf16[8,352,128]{2,1,0:T(8,128)(2,1)} %bitcast_bitcast_fusion), channel_id=1, source_target_pairs={{0,0},{16,1},{8,2},{24,3},{4,4},{20,5},{12,6},{28,7},{2,8},{18,9},... | collective-permute-start | bytes 2162696 | tf_op jit(solution)/shard_map/ppermute | solution.py:156
  379.7 15.3 %collective-permute-start.21 = (bf16[256,1024]{1,0:T(8,128)(2,1)S(1)}, bf16[256,1024]{1,0:T(8,128)(2,1)}, u32[]{:S(2)}, u32[]{:S(2)}) collective-permute-start(bf16[256,1024]{1,0:T(8,128)(2,1)S(1)} %slice.481), channel_id=1, source_target_pairs={{0,2},{1,3},{2,0},{3,1},{4,6},{5,7},{6,4},{7,5},{8,10},{9,11},{10,... | collective-permute-start | bytes 1572872 | tf_op jit(solution)/shard_map/ppermute | solution.py:20
  383.4 39.3 %all-to-all-start.2 = ((bf16[8,368,128]{2,1,0:T(8,128)(2,1)}), bf16[8,368,128]{2,1,0:T(8,128)(2,1)S(1)}, u32[]{:S(2)}, u32[]{:S(2)}) async-start(bf16[8,368,128]{2,1,0:T(8,128)(2,1)} %pad_maximum_fusion.6), calls=%async_computation.2 | async-start | bytes 1507328 | tf_op jit(solution)/shard_map/all_to_all | solution.py:120
  396.3 24.4 %collective-permute-start.22 = (bf16[128,1024]{1,0:T(8,128)(2,1)S(1)}, bf16[128,1024]{1,0:T(8,128)(2,1)S(1)}, u32[]{:S(2)}, u32[]{:S(2)}) collective-permute-start(bf16[128,1024]{1,0:T(8,128)(2,1)S(1)} %slice.482), channel_id=1, source_target_pairs={{0,4},{1,5},{2,6},{3,7},{4,0},{5,1},{6,2},{7,3},{8,12},{9,13},{10,... | collective-permute-start | bytes 786440 | tf_op jit(solution)/shard_map/ppermute | solution.py:20
  422.7 1.2 collective-permute-start.23
  424.0 3.7 collective-permute-start.24
  (63 other events, 373.1 us)
Sparse Core Ops, SparseCore 0:
  57.6 56.0 all-gather.2
  116.4 73.8 all-gather.4
  261.7 105.0 reduce-scatter.1

commit v4 on v3

--- a/solution.py
+++ b/solution.py
@@ -71,9 +71,9 @@
     return kept + received.astype(WIDE)
 
 
-def in_two(partial):
-    half = partial.shape[0] // 2
-    return partial[:half], partial[half:].astype(LOW)
+def scatter_step(total, bit):
+    half = total.shape[0] // 2
+    return total[:half], swap(total[half:].astype(LOW), "gy", bit)
 
 
 def pieces(values, count):
@@ -85,40 +85,44 @@
     return parts
 
 
-def reversed_bits(value, count):
-    turned = 0
-    while count > 1:
-        turned = turned * 2 + value % 2
-        value //= 2
-        count //= 2
-    return turned
-
-
-def owner_pairs(nx, ny):
-    return [
-        (i * ny + h * nx + q, reversed_bits(q, nx) * ny + h * nx + reversed_bits(i, nx))
-        for i in range(nx)
-        for h in range(ny // nx)
-        for q in range(nx)
-    ]
-
-
-def cut_rows(values, block):
+def spread_images(values, block):
     nx, ny = lax.axis_size("gx"), lax.axis_size("gy")
     images = values.reshape(ny // nx, SEQ, D // ny)
     images = jnp.pad(images, ((0, 0), (0, nx * block - SEQ), (0, 0)))
-    parts = images.reshape(ny // nx, nx, block, D // ny)
-    parts = jnp.stack([parts[:, reversed_bits(q, nx)] for q in range(nx)], axis=1)
-    return parts.reshape(ny, block, D // ny)
-
-
-def cross(parts, extra=None):
-    if extra is None:
-        return lax.all_to_all(parts, "gy", split_axis=0, concat_axis=0, tiled=True), None
-    rows, more = parts.shape[1], extra.shape[1]
-    parts = jnp.concatenate((parts, jnp.pad(extra, ((0, 0), (0, -more % 16), (0, 0)))), axis=1)
-    parts = lax.all_to_all(parts, "gy", split_axis=0, concat_axis=0, tiled=True)
-    return parts[:, :rows], parts[:, rows : rows + more]
+    return images.reshape(ny // nx, nx, block, D // ny).transpose(1, 0, 2, 3)
+
+
+def to_rows(parts):
+    parts = lax.all_to_all(parts, "gx", split_axis=0, concat_axis=0, tiled=True)
+    return parts.reshape((-1,) + parts.shape[2:])
+
+
+def to_images(parts):
+    nx, ny = lax.axis_size("gx"), lax.axis_size("gy")
+    parts = parts.reshape((nx, ny // nx) + parts.shape[1:])
+    return lax.all_to_all(parts, "gx", split_axis=0, concat_axis=0, tiled=True)
+
+
+def join_images(parts, packed_shape):
+    nx, per, block, width = parts.shape
+    parts = parts.transpose(1, 0, 2, 3).reshape(per, nx * block, width)
+    return parts[:, :SEQ].reshape(packed_shape)
+
+
+def over_rows(sums):
+    bit = 1
+    while bit < lax.axis_size("gx"):
+        sums = sums + swap(sums, "gx", bit)
+        bit *= 2
+    return sums
+
+
+def cross(parts, *extra):
+    if extra:
+        rows = sum(item.shape[1] for item in extra)
+        space = jnp.zeros((parts.shape[0], -rows % 16, parts.shape[2]), LOW)
+        parts = jnp.concatenate((parts, *extra, space), axis=1)
+    return lax.all_to_all(parts, "gy", split_axis=0, concat_axis=0, tiled=True)
 
 
 def spread_lines(values):
@@ -137,31 +141,27 @@
     return jnp.sum(lines.astype(WIDE), axis=0).reshape(2, -1, lines.shape[2]).sum(axis=0)
 
 
-def move_to_owner(parts):
-    nx, ny = lax.axis_size("gx"), lax.axis_size("gy")
-    return lax.ppermute(parts, ("gx", "gy"), owner_pairs(nx, ny))
-
-
 def join_width(parts):
     return parts.transpose(1, 0, 2).reshape(parts.shape[1], D)
 
 
-def to_owner(parts):
-    return join_width(move_to_owner(parts))
-
-
-def leave_owner(values):
-    nx, ny = lax.axis_size("gx"), lax.axis_size("gy")
-    parts = values.reshape(values.shape[0], ny, D // ny).transpose(1, 0, 2)
-    return lax.ppermute(parts, ("gx", "gy"), [(b, a) for a, b in owner_pairs(nx, ny)])
-
-
-def join_rows(parts, packed_shape):
-    nx, ny = lax.axis_size("gx"), lax.axis_size("gy")
-    block = parts.shape[1]
-    parts = parts.reshape(ny // nx, nx, block, D // ny)
-    parts = jnp.stack([parts[:, reversed_bits(q, nx)] for q in range(nx)], axis=1)
-    return parts.reshape(ny // nx, nx * block, D // ny)[:, :SEQ].reshape(packed_shape)
+def cut_width(values):
+    ny = lax.axis_size("gy")
+    return values.reshape(values.shape[0], ny, D // ny).transpose(1, 0, 2)
+
+
+def gather_weight(weight):
+    place = lax.axis_index("gy")
+    rows, cols = weight.shape
+    weight = weight[None]
+    bit = lax.axis_size("gy") // 2
+    while bit:
+        other = swap(weight, "gy", bit)
+        upper = (place & bit) != 0
+        low, high = jnp.where(upper, other, weight), jnp.where(upper, weight, other)
+        weight = jnp.stack((low, high), axis=1).reshape(-1, rows, cols)
+        bit //= 2
+    return weight.reshape(-1, cols)
 
 
 def norm_forward(values, gain, shift):
@@ -361,9 +361,10 @@
     near = pl.BlockSpec((step, width), lambda r: (jnp.maximum(r - 2, 0), 0))
     far = pl.BlockSpec((step, width), lambda r: (jnp.minimum(r, 1), 0))
     units = pl.BlockSpec((step, cols), lambda r: ((r + 2) % 4, 0))
-    weight = pl.BlockSpec((width, cols), lambda r: (0, 0))
+    expand = pl.BlockSpec((width, cols), lambda r: (0, 0))
+    shrink = pl.BlockSpec((width, cols), lambda r: (0, 1))
     line = pl.BlockSpec((1, cols), lambda r: (0, 0))
-    return near, far, units, weight, line
+    return near, far, units, expand, shrink, line
 
 
 def hidden_cost(rows, width, cols):
@@ -374,14 +375,14 @@
     )
 
 
-def hidden_forward(near_rows, far_rows, expand, shrink, bias):
+def hidden_forward(near_rows, far_rows, weights, bias):
     rows, width = near_rows.shape
-    cols = expand.shape[1]
-    near, far, units, weight, line = hidden_specs(rows, width, cols)
+    cols = weights.shape[1] // 2
+    near, far, units, expand, shrink, line = hidden_specs(rows, width, cols)
     return pl.pallas_call(
         forward_body,
         grid=(4,),
-        in_specs=[near, far, weight, weight, line],
+        in_specs=[near, far, expand, shrink, line],
         out_specs=[units, units, near, far],
         out_shape=[
             jax.ShapeDtypeStruct((2 * rows, cols), LOW),
@@ -391,17 +392,17 @@
         ],
         compiler_params=pltpu.CompilerParams(vmem_limit_bytes=40 * 1024 * 1024),
         cost_estimate=hidden_cost(rows, width, cols),
-    )(near_rows, far_rows, expand, shrink, bias)
-
-
-def hidden_backward(near_rows, far_rows, expand, shrink, slope):
+    )(near_rows, far_rows, weights, weights, bias)
+
+
+def hidden_backward(near_rows, far_rows, weights, slope):
     rows, width = near_rows.shape
-    cols = expand.shape[1]
-    near, far, units, weight, line = hidden_specs(rows, width, cols)
+    cols = weights.shape[1] // 2
+    near, far, units, expand, shrink, line = hidden_specs(rows, width, cols)
     return pl.pallas_call(
         backward_body,
         grid=(4,),
-        in_specs=[near, far, weight, weight, units],
+        in_specs=[near, far, expand, shrink, units],
         out_specs=[units, near, far, line],
         out_shape=[
             jax.ShapeDtypeStruct((2 * rows, cols), LOW),
@@ -411,7 +412,24 @@
         ],
         compiler_params=pltpu.CompilerParams(vmem_limit_bytes=40 * 1024 * 1024),
         cost_estimate=hidden_cost(rows, width, cols),
-    )(near_rows, far_rows, expand, shrink, slope)
+    )(near_rows, far_rows, weights, weights, slope)
+
+
+def turned_slot(slot, count):
+    turned = slot * 0
+    while count > 1:
+        turned = turned * 2 + slot % 2
+        slot = slot // 2
+        count //= 2
+    return turned
+
+
+def far_first(total, tiles):
+    order = jnp.array([turned_slot(slot, tiles) for slot in range(tiles)])
+    parts = total.reshape(tiles, -1, total.shape[1])
+    parts = jnp.take(parts, order ^ lax.axis_index("gy"), axis=0).reshape(total.shape)
+    half = total.shape[0] // 2
+    return parts[:half], parts[half:].astype(LOW)
 
 
 def unit_grads_body(
@@ -455,89 +473,103 @@
     )(grad_near, grad_far, second_near, second_far, hidden, grad_pre)
 
 
-def head_grads_body(place_ref, first_ref, grad_ref, mixed_ref, attended_ref, kept_ref, sent_ref):
+def project_body(rows_ref, weight_ref, kept_ref, sent_ref, turned_ref):
+    @pl.when(pl.program_id(0) == 0)
+    def _():
+        turned_ref[...] = rows_ref[...].T
+
+    total = times_t(turned_ref[...], weight_ref[...])
+    half = kept_ref.shape[0]
+    kept_ref[...] = total[:half]
+    sent_ref[...] = total[half:].astype(LOW)
+
+
+def project_rows(values, weight):
+    cols, rows = values.shape
+    width = weight.shape[0]
+    tile = width // 4
+    return pl.pallas_call(
+        project_body,
+        grid=(4,),
+        in_specs=[
+            pl.BlockSpec((cols, rows), lambda t: (0, 0)),
+            pl.BlockSpec((tile, cols), lambda t: (t, 0)),
+        ],
+        out_specs=[
+            pl.BlockSpec((rows // 2, tile), lambda t: (0, t)),
+            pl.BlockSpec((rows // 2, tile), lambda t: (0, t)),
+        ],
+        out_shape=[
+            jax.ShapeDtypeStruct((rows // 2, width), WIDE),
+            jax.ShapeDtypeStruct((rows // 2, width), LOW),
+        ],
+        scratch_shapes=[pltpu.VMEM((rows, cols), LOW)],
+        compiler_params=pltpu.CompilerParams(vmem_limit_bytes=40 * 1024 * 1024),
+        cost_estimate=pl.CostEstimate(
+            flops=2 * rows * cols * width,
+            bytes_accessed=2 * rows * cols + 2 * width * cols + 3 * rows * width,
+            transcendentals=0,
+        ),
+    )(values, weight)
+
+
+def head_grads_body(place_ref, fn_ref, ff_ref, gn_ref, gf_ref, mixed_ref, attended_ref, out_ref):
     cols = mixed_ref.shape[0]
-    heads = times(mixed_ref[...], first_ref[...]).T
-    tail = times(attended_ref[...], grad_ref[...]).T
-    half = pl.num_programs(0) // 2
-
-    @pl.when(pl.program_id(0) < half)
-    def _():
-        sent_ref[:, :cols] = heads.astype(LOW)
-        sent_ref[:, cols:] = tail.astype(LOW)
-
-    @pl.when(pl.program_id(0) >= half)
-    def _():
-        kept_ref[:, :cols] = heads
-        kept_ref[:, cols:] = tail
-
-
-def head_grads_of(first, grad, mixed, attended):
-    rows, width = first.shape
+    first = jnp.concatenate((fn_ref[...], ff_ref[...]), axis=0)
+    grad = jnp.concatenate((gn_ref[...], gf_ref[...]), axis=0)
+    out_ref[:, :cols] = times(mixed_ref[...], first).T.astype(out_ref.dtype)
+    out_ref[:, cols:] = times(attended_ref[...], grad).T.astype(out_ref.dtype)
+
+
+def head_grads_of(first_near, first_far, grad_near, grad_far, mixed, attended, upper):
+    half, width = first_near.shape
+    rows = 2 * half
     cols, more = mixed.shape[0], attended.shape[0]
-    tile = 128
-    tiles = width // tile
-    bits = tiles.bit_length() - 1
+    tiles = lax.axis_size("gy")
+    tile = width // tiles
+    dtype = LOW if upper else WIDE
+    if tile % 128:
+        first = jnp.concatenate((first_near, first_far), axis=0)
+        grad = jnp.concatenate((grad_near, grad_far), axis=0)
+        total = jnp.concatenate((times(mixed, first).T, times(attended, grad).T), axis=1)
+        return far_first(total, tiles)[1 if upper else 0].astype(dtype)
+    start = tiles // 2 if upper else 0
 
     def block(r, place):
-        slot = (r + tiles // 2) % tiles
-        turned = slot * 0
-        for k in range(bits):
-            turned = turned * 2 + (slot // 2**k) % 2
-        return turned ^ place[0]
-
-    narrow = pl.BlockSpec((rows, tile), lambda r, place: (0, block(r, place)))
+        return turned_slot(r + start, tiles) ^ place[0]
+
+    narrow = pl.BlockSpec((half, tile), lambda r, place: (0, block(r, place)))
     return pl.pallas_call(
         head_grads_body,
         grid_spec=pltpu.PrefetchScalarGridSpec(
             num_scalar_prefetch=1,
-            grid=(tiles,),
+            grid=(tiles // 2,),
             in_specs=[
+                narrow,
+                narrow,
                 narrow,
                 narrow,
                 pl.BlockSpec((cols, rows), lambda r, place: (0, 0)),
                 pl.BlockSpec((more, rows), lambda r, place: (0, 0)),
             ],
-            out_specs=[
-                pl.BlockSpec(
-                    (tile, cols + more), lambda r, place: (jnp.maximum(r - tiles // 2, 0), 0)
-                ),
-                pl.BlockSpec(
-                    (tile, cols + more), lambda r, place: (jnp.minimum(r, tiles // 2 - 1), 0)
-                ),
-            ],
+            out_specs=pl.BlockSpec((tile, cols + more), lambda r, place: (r, 0)),
         ),
-        out_shape=[
-            jax.ShapeDtypeStruct((width // 2, cols + more), WIDE),
-            jax.ShapeDtypeStruct((width // 2, cols + more), LOW),
-        ],
+        out_shape=jax.ShapeDtypeStruct((width // 2, cols + more), dtype),
         compiler_params=pltpu.CompilerParams(vmem_limit_bytes=40 * 1024 * 1024),
         cost_estimate=pl.CostEstimate(
-            flops=4 * rows * (cols + more) * width,
-            bytes_accessed=2 * rows * (2 * width + cols + more) + 3 * width * (cols + more),
+            flops=2 * rows * (cols + more) * width,
+            bytes_accessed=2 * rows * (width + cols + more) + 2 * width * (cols + more),
             transcendentals=0,
         ),
-    )(lax.axis_index("gy").astype(jnp.int32)[None], first, grad, mixed, attended)
-
-
-def plain_head_grads(first, grad, mixed, attended):
-    joined = jnp.concatenate((times(mixed, first).T, times(attended, grad).T), axis=1).astype(LOW)
-    return lax.psum_scatter(joined, "gy", scatter_dimension=0, tiled=True).astype(WIDE)
-
-
-def scatter_head_grads(first, grad, mixed, attended):
-    ny = lax.axis_size("gy")
-    if D // ny != 128:
-        return plain_head_grads(first, grad, mixed, attended)
-    kept, sent = head_grads_of(first, grad, mixed, attended)
-    total = kept + swap(sent, "gy", 1).astype(WIDE)
-    bit = 2
-    while bit < ny:
-        half = total.shape[0] // 2
-        received = swap(total[half:].astype(LOW), "gy", bit)
-        total = total[:half] + received.astype(WIDE)
-        bit *= 2
-    return total
+    )(
+        lax.axis_index("gy").astype(jnp.int32)[None],
+        first_near,
+        first_far,
+        grad_near,
+        grad_far,
+        mixed,
+        attended,
+    )
 
 
 def on_device(
@@ -593,84 +625,81 @@
         ),
         axis=0,
     )
-    heads_weight = lax.all_gather(
-        jnp.concatenate((project_in.reshape(-1, 3 * head_cols), project_out.T), axis=1),
-        "gy",
-        axis=0,
-        tiled=True,
-    )
-    weight_in, weight_out = heads_weight[:, : 3 * head_cols], heads_weight[:, 3 * head_cols :]
+    weight_in = lax.all_gather(project_in.reshape(-1, 3 * head_cols), "gy", axis=0, tiled=True)
     units_weight = jnp.concatenate((expand_weight, shrink_weight.T), axis=1)
 
-    parts, small = cross(
-        jnp.concatenate((cut_rows(tokens, block), cut_rows(cotangent, block)), axis=1),
-        jnp.broadcast_to(small[None], (ny,) + small.shape),
-    )
-    parts, small, units_weight = together(parts, small, units_weight)
+    parts = to_rows(
+        jnp.concatenate((spread_images(tokens, block), spread_images(cotangent, block)), axis=2)
+    )
+    input_parts = cross(parts[:, :block], jnp.broadcast_to(small[None], (ny,) + small.shape))
+    input_parts, grad_parts, units_weight, weight_out = together(
+        input_parts, parts[:, block:], units_weight, project_out.T
+    )
+    input_parts, small = input_parts[:, :block], input_parts[:, block : block + 24]
+    grad_parts = cross(grad_parts)
+    weight_out = gather_weight(weight_out)
     units_weight = lax.all_gather(units_weight, "gy", axis=0, tiled=True)
-    weight_expand, weight_shrink = units_weight[:, :hidden_cols], units_weight[:, hidden_cols:]
     small = small.astype(WIDE)
     small = small[:, :8] + (small[:, 8:16] + small[:, 16:])
     out_shift, attn_scale, gain_one, shift_one, gain_two, shift_two, shrink_shift, ff_scale = [
         small[:, k].reshape(D) for k in range(8)
     ]
-    inputs = to_owner(parts[:, :block]).astype(WIDE)
+    inputs = join_width(input_parts).astype(WIDE)
 
     first, first_hat, first_rstd = norm_forward(inputs, gain_one, shift_one)
-    first_own, first_far = gather_far(first)
-    first_far, grad_parts = together(first_far, parts[:, block:])
-    first_near = jnp.concatenate((first_own, first_far), axis=0)
-    first_all = jnp.concatenate((first_near, swap(first_near, "gx", 1)), axis=0)
-    grad_parts = move_to_owner(grad_parts)
+    first_near = gather_step(first)
+    first_other = swap(first_near, "gx", 1)
+    first_all = jnp.concatenate((first_near, first_other), axis=0)
     mixed = lax.dot_general(
         weight_in, first_all, (((0,), (1,)), ((), ())), preferred_element_type=WIDE
     )
     query = (mixed[:head_cols] + query_bias[:, None]).astype(LOW)
     keys = mixed[head_cols : 2 * head_cols].astype(LOW)
     values = (mixed[2 * head_cols :] + value_bias[:, None]).astype(LOW)
-    split = head_cols // HEAD_DIM // 2
-    half = attend_forward(query, keys, values, mask, ones, 0, split)
+    heads = head_cols // HEAD_DIM
+    half = attend_forward(query, keys, values, mask, ones, 0, heads // 2)
     *half, grad_parts = together(*half, grad_parts)
     grad = join_width(grad_parts).astype(WIDE)
     grad_b = grad * ff_scale
     grad_b_own, grad_b_other = gather_far(grad_b.astype(LOW))
     attended, attended_wide, log_total = attend_forward(
-        query, keys, values, mask, ones, split, head_cols // HEAD_DIM - split, half
+        query, keys, values, mask, ones, heads // 2, heads - heads // 2, half
     )
     attended, grad_b_other = together(attended, grad_b_other)
     grad_b_near = jnp.concatenate((grad_b_own, grad_b_other), axis=0)
     grad_b_far = swap(grad_b_near, "gx", 1)
 
-    kept, sent = in_two(inner_rows(attended, weight_out.T))
+    kept, sent = project_rows(attended, weight_out)
     branch_a = scatter_far(scatter_near(kept, sent)) + out_shift
     middle = inputs + attn_scale * branch_a
     second, second_hat, second_rstd = norm_forward(middle, gain_two, shift_two)
     second_near, second_far = gather_halves(second)
     hidden, slope, kept_b, sent_b = hidden_forward(
-        second_near, second_far, weight_expand, weight_shrink, expand_bias[None]
-    )
-    branch_near = scatter_near(kept_b, sent_b)
-    grad_pre, kept, sent, pre_sum = hidden_backward(
-        grad_b_near, grad_b_far, weight_expand, weight_shrink, slope
-    )
+        second_near, second_far, units_weight, expand_bias[None]
+    )
+    grad_pre, kept, sent, pre_sum = hidden_backward(grad_b_near, grad_b_far, units_weight, slope)
     wide_grads = unit_grads(grad_b_near, grad_b_far, second_near, second_far, hidden, grad_pre)
-    grad_second, wide_grads = together(scatter_far(scatter_near(kept, sent)), wide_grads)
-    wide_grads = lax.psum_scatter(wide_grads, "gy", scatter_dimension=0, tiled=True).astype(WIDE)
+    grad_second, received = scatter_last(scatter_near(kept, sent))
+    received, wide_grads = together(received, wide_grads)
+    grad_second = grad_second + received.astype(WIDE)
+    wide_grads = lax.psum_scatter(wide_grads, "gy", scatter_dimension=0, tiled=True)
 
     grad_middle = grad + norm_backward(grad_second, gain_two, second_hat, second_rstd)
     grad_a = grad_middle * attn_scale
-    grad_a_near, branch_near = together(gather_step(grad_a.astype(LOW)), branch_near)
-    grad_a_all = jnp.concatenate((grad_a_near, swap(grad_a_near, "gx", 1)), axis=0)
+    grad_a_own, grad_a_other = gather_far(grad_a.astype(LOW))
+    branch_near = scatter_near(kept_b, sent_b)
+    grad_a_other, branch_near = together(grad_a_other, branch_near)
+    grad_a_near = jnp.concatenate((grad_a_own, grad_a_other), axis=0)
+    grad_a_other = swap(grad_a_near, "gx", 1)
+    grad_a_all = jnp.concatenate((grad_a_near, grad_a_other), axis=0)
     branch_kept, branch_far = scatter_last(branch_near)
     grad_attended = lax.dot_general(
         weight_out, grad_a_all, (((0,), (1,)), ((), ())), preferred_element_type=WIDE
     ).astype(LOW)
     half = attend_backward(
-        query, keys, values, grad_attended, attended_wide, log_total, mask, ones, 0, split
+        query, keys, values, grad_attended, attended_wide, log_total, mask, ones, 0, heads // 2
     )
     half, branch_far = together(half, branch_far)
-    branch_b = branch_kept + branch_far.astype(WIDE) + shrink_shift
-    output_parts = leave_owner((middle + ff_scale * branch_b).astype(LOW))
     grad_mixed = attend_backward(
         query,
         keys,
@@ -680,52 +709,65 @@
         log_total,
         mask,
         ones,
-        split,
-        head_cols // HEAD_DIM - split,
+        heads // 2,
+        heads - heads // 2,
         (half,),
     )
-    grad_mixed, output_parts = together(grad_mixed, output_parts)
-    early = jnp.stack(
+    branch_b = branch_kept + branch_far.astype(WIDE) + shrink_shift
+    output_parts = cut_width((middle + ff_scale * branch_b).astype(LOW))
+    joined = grad_mixed.reshape(3 * head_cols, nx * block)
+    kept, sent = project_rows(joined, weight_in)
+    shares = (first_near, first_other, grad_a_near, grad_a_other, joined, attended)
+    received, head_sent, output_parts = together(
+        swap(sent, "gx", 1), head_grads_of(*shares, True), output_parts
+    )
+    grad_first, received = scatter_last(kept + received.astype(WIDE))
+    received, head_other, head_kept, wide_grads = together(
+        received, swap(head_sent, "gy", 1), head_grads_of(*shares, False), wide_grads
+    )
+    grad_first = grad_first + received.astype(WIDE)
+    wide_grads = wide_grads.astype(WIDE)
+    head_kept, head_other = scatter_step(head_kept + head_other.astype(WIDE), 2)
+    input_gradient = grad_middle + norm_backward(grad_first, gain_one, first_hat, first_rstd)
+    sums = jnp.stack(
         [
             jnp.sum(item, axis=0)
-            for item in (grad_second * second_hat, grad_second, grad_b, grad * branch_b)
+            for item in (
+                grad_a,
+                grad_middle * branch_a,
+                grad_first * first_hat,
+                grad_first,
+                grad_second * second_hat,
+                grad_second,
+                grad_b,
+                grad * branch_b,
+            )
         ]
     )
-    output_parts, lines = cross(
-        output_parts, jnp.concatenate((split_lines(early), spread_lines(pre_sum[0])), axis=1)
-    )
-    block_output = join_rows(output_parts, packed_shape)
-    early, pre_sum = sum_lines(lines[:, :8]), sum_lines(lines[:, 8:]).reshape(-1)
-
-    joined = grad_mixed.reshape(3 * head_cols, nx * block)
-    kept, sent = in_two(inner_rows(joined, weight_in.T))
-    near, joined = together(scatter_near(kept, sent), joined)
-    grad_first = scatter_far(near)
-    head_grads = scatter_head_grads(first_all, grad_a_all, joined, attended)
-    input_gradient = grad_middle + norm_backward(grad_first, gain_one, first_hat, first_rstd)
-    input_parts = leave_owner(input_gradient.astype(LOW))
-    late = jnp.stack(
-        [
-            jnp.sum(item, axis=0)
-            for item in (grad_a, grad_middle * branch_a, grad_first * first_hat, grad_first)
-        ]
-    )
-    head_sums = jnp.concatenate(
+    image_sums = jnp.concatenate(
         (
             jnp.sum(grad_mixed[0].astype(WIDE), axis=1),
             jnp.sum(grad_mixed[2].astype(WIDE), axis=1),
+            pre_sum[0],
         )
     )
-    input_parts, lines = cross(
-        input_parts, jnp.concatenate((split_lines(late), spread_lines(head_sums)), axis=1)
-    )
-    input_gradient = join_rows(input_parts, packed_shape).astype(WIDE)
-    late, head_sums = sum_lines(lines[:, :8]), sum_lines(lines[:, 8:]).reshape(-1)
-    sums = jnp.concatenate((late, early), axis=0)
-    bit = 1
-    while bit < nx:
-        sums = sums + swap(sums, "gx", bit)
+    input_parts = cut_width(input_gradient.astype(LOW))
+    input_parts, output_parts = together(input_parts, cross(output_parts))
+    input_parts = cross(input_parts, split_lines(sums), spread_lines(image_sums))
+    input_parts, head_other = together(input_parts, head_other)
+    head_grads = head_kept + head_other.astype(WIDE)
+    bit = 4
+    while bit < ny:
+        head_kept, head_other = scatter_step(head_grads, bit)
+        head_grads = head_kept + head_other.astype(WIDE)
         bit *= 2
+    both = to_images(jnp.concatenate((input_parts[:, :block], output_parts), axis=1))
+    block_output = join_images(both[:, :, block:], packed_shape)
+    input_gradient = join_images(both[:, :, :block], packed_shape).astype(WIDE)
+    sums = over_rows(sum_lines(input_parts[:, block : block + 16]))
+    lines = 2 * image_sums.shape[0] * ny // D
+    image_sums = sum_lines(input_parts[:, block + 16 : block + 16 + lines]).reshape(-1)
+    head_sums, pre_sum = image_sums[: 2 * head_cols], image_sums[2 * head_cols :]
     return (
         block_output,
         input_gradient,

time: 442 us -> 427 us (0.966)
  starting transfers between devices: 76.2 us -> 47.4 us
  waiting for transfers between devices: 185 us -> 194 us
  Pallas kernels: 83.4 us -> 90 us
    ppermute x21 -> x24, starting transfers between devices: 52.4 us -> 15.6 us  [swap(): return lax.ppermute(values, axis, [(k, k ^ bit) for k in range(size)])]
    all_gather x1, waiting for transfers between devices: 16.4 us -> 0.02 us  [on_device(): lax.all_gather(project_in.reshape(-1, 3 * head_cols), 'gy', axis=0, tiled...]
    all_to_all x3 -> x6, starting transfers between devices: 18.2 us -> 31.6 us  [the longest x4 23.7 us: cross(): return lax.all_to_all(parts, 'gy', split_axis=0, concat_axis=0, tiled=True)]
    ppermute x21 -> x24, waiting for transfers between devices: 130 us -> 143 us  [swap(): return lax.ppermute(values, axis, [(k, k ^ bit) for k in range(size)])]
    all_to_all x3 -> x6, waiting for transfers between devices: 37.9 us -> 50.1 us  [the longest x4 31.5 us: cross(): return lax.all_to_all(parts, 'gy', split_axis=0, concat_axis=0, tiled=True)]
    reduce_sum x3 -> x5, other arithmetic: 1.84 us -> 12.4 us  [on_device(): jnp.sum(item, axis=0)]
    pallas_call x2 -> x4, Pallas kernels: 18 us -> 24.8 us  [the longest x1 9.83 us: hidden_forward(): pl.pallas_call(forward_body, grid=(4,), in_specs=[near, far, expand, shri...]
    ppermute x4 -> x0, starting transfers between devices: 5.45 us -> none  [the longest x2 2.73 us: move_to_owner(): return lax.ppermute(parts, ('gx', 'gy'), owner_pairs(nx, ny))]
  transfers between devices with their start and end apart: 31 -> 33, of which waited for: 19 -> 21; matrix products, arithmetic and copies ran while one was open for 13% -> 12% of each run, Pallas kernels for 17% -> 19%
where the time goes in v4:
time: 427 us; the launch traced here: 420 us
  waiting for transfers between devices  194 us (45%)
  Pallas kernels  90 us (21%)
  starting transfers between devices  47.4 us (11%)
  other arithmetic  36.7 us (9%)
  local copies, waits for them, and re-layouts  31.3 us (7%)
  between operations  15.3 us (4%)
  matrix products  5.87 us (1%)
    ppermute x24, waiting for transfers between devices, swap(): return lax.ppermute(values, axis, [(k, k ^ bit) for k in range(size)])  143 us
    all_to_all x4, waiting for transfers between devices, cross(): return lax.all_to_all(parts, 'gy', split_axis=0, concat_axis=0, tiled=True)  31.5 us
    all_to_all x4, starting transfers between devices, cross(): return lax.all_to_all(parts, 'gy', split_axis=0, concat_axis=0, tiled=True)  23.7 us
    pallas_call x2, Pallas kernels, attend_backward(): pl.pallas_call(attend_backward_body, grid=(count,), in_specs=[head, head,...  22.3 us
    pallas_call x2, Pallas kernels, attend_forward(): pl.pallas_call(attend_forward_body, grid=(count,), in_specs=[head, head,...  20.5 us
    all_to_all x1, waiting for transfers between devices, to_rows(): parts = lax.all_to_all(parts, 'gx', split_axis=0, concat_axis=0, tiled=True)  18.6 us
    unnamed x124, local copies, waits for them, and re-layouts  16.6 us
    ppermute x24, starting transfers between devices, swap(): return lax.ppermute(values, axis, [(k, k ^ bit) for k in range(size)])  15.6 us
  transfers between devices with their start and end apart: 33, of which 21 were waited for; matrix products, arithmetic and copies ran while one was open for 12% of the time, Pallas kernels for 19%

profile of v4, /device:TPU:0, one launch (start us, length us, event | category | flops | bytes accessed | tf_op | source)
XLA Modules:
  0.0 420.4 jit_solution(16537147455578039527)
XLA Ops:
  10.2 4.4 %all-to-all-start = ((bf16[4,2,704,128]{3,2,1,0:T(8,128)(2,1)}), bf16[4,2,704,128]{3,2,1,0:T(8,128)(2,1)S(1)}, u32[]{:S(2)}, u32[]{:S(2)}) async-start(bf16[4,2,704,128]{3,2,1,0:T(8,128)(2,1)} %pad_maximum_fusion), calls=%async_computation | async-start | bytes 2883584 | tf_op jit(solution)/shard_map/all_to_all | solution.py:96
  14.7 18.6 %all-to-all-done = bf16[4,2,704,128]{3,2,1,0:T(8,128)(2,1)S(1)} async-done(((bf16[4,2,704,128]{3,2,1,0:T(8,128)(2,1)}), bf16[4,2,704,128]{3,2,1,0:T(8,128)(2,1)S(1)}, u32[]{:S(2)}, u32[]{:S(2)}) %all-to-all-start) | async-done | bytes 1441824 | tf_op jit(solution)/shard_map/all_to_all | solution.py:96
  35.2 6.7 %all-to-all-start.1 = ((bf16[8,384,128]{2,1,0:T(8,128)(2,1)}), bf16[8,384,128]{2,1,0:T(8,128)(2,1)S(1)}, u32[]{:S(2)}, u32[]{:S(2)}) async-start(bf16[8,384,128]{2,1,0:T(8,128)(2,1)} %pad_maximum_fusion.7), calls=%async_computation.1 | async-start | bytes 1572864 | tf_op jit(solution)/shard_map/all_to_all | solution.py:125
  44.1 22.5 %all-to-all-done.1 = bf16[8,384,128]{2,1,0:T(8,128)(2,1)S(1)} async-done(((bf16[8,384,128]{2,1,0:T(8,128)(2,1)}), bf16[8,384,128]{2,1,0:T(8,128)(2,1)S(1)}, u32[]{:S(2)}, u32[]{:S(2)}) %all-to-all-start.1) | async-done | bytes 786464 | tf_op jit(solution)/shard_map/all_to_all | solution.py:125
  68.4 5.2 %collective-permute-done.3 = bf16[1,128,256]{2,1,0:T(8,128)(2,1)S(1)} collective-permute-done((bf16[1,128,256]{2,1,0:T(8,128)(2,1)S(1)}, bf16[1,128,256]{2,1,0:T(8,128)(2,1)S(1)}, u32[]{:S(2)}, u32[]{:S(2)}) %collective-permute-start.3) | collective-permute-done | bytes 65568 | tf_op jit(solution)/shard_map/ppermute | solution.py:20
  73.7 9.3 %collective-permute-done = bf16[352,1024]{1,0:T(8,128)(2,1)} collective-permute-done((bf16[352,1024]{1,0:T(8,128)(2,1)S(1)}, bf16[352,1024]{1,0:T(8,128)(2,1)}, u32[]{:S(2)}, u32[]{:S(2)}) %collective-permute-start) | collective-permute-done | bytes 720928 | tf_op jit(solution)/shard_map/ppermute | solution.py:20
  87.5 4.2 %all-to-all-start.2 = ((bf16[8,352,128]{2,1,0:T(8,128)(2,1)}), bf16[8,352,128]{2,1,0:T(8,128)(2,1)}, u32[]{:S(2)}, u32[]{:S(2)}) async-start(bf16[8,352,128]{2,1,0:T(8,128)(2,1)} %get-tuple-element.66), calls=%async_computation.2 | async-start | bytes 1441792 | tf_op jit(solution)/shard_map/all_to_all | solution.py:125
  94.5 4.8 %convolution_bitcast_fusion = f32[768,1408]{1,0:T(8,128)S(1)} fusion(bf16[1024,768]{1,0:T(8,128)(2,1)} %all-gather.3.cloned.1.call-done.weight_ref, bf16[704,1024]{1,0:T(8,128)(2,1)} %collective-permute-done.1.ff_ref, bf16[352,1024]{1,0:T(8,128)(2,1)} %collective-permute-done, bf16[352,1024]{1,0:T(8,128)(2,1)S(1)} %add_convert_fusion.3), kind=kOutput, calls=%fused_computation | convolution fusion | flops 2223243264 | bytes 8781824 | tf_op jit(solution)/shard_map/dot_general | solution.py:653
  99.9 10.3 %shard_map.296 = (bf16[256,1408]{1,0:T(8,128)(2,1)S(1)}, f32[256,1408]{1,0:T(8,128)S(1)}, f32[4,1,1408]{2,1,0:T(1,128)S(1)}) custom-call(bf16[256,1408]{1,0:T(8,128)(2,1)S(1)} %get-tuple-element.211.q_ref, bf16[256,1408]{1,0:T(8,128)(2,1)S(1)} %slice.361.k_ref, bf16[256,1408]{1,0:T(8,128)(2,1)S(1)} %get-tuple-element.210.v_ref, ...), custom_call_target="tpu_custom_call" | custom-call | flops 12180258816 | bytes 2162688 | tf_op jit(solution)/shard_map/pallas_call | solution.py:225
  112.2 8.0 %all-to-all-done.2 = bf16[8,352,128]{2,1,0:T(8,128)(2,1)} async-done(((bf16[8,352,128]{2,1,0:T(8,128)(2,1)}), bf16[8,352,128]{2,1,0:T(8,128)(2,1)}, u32[]{:S(2)}, u32[]{:S(2)}) %all-to-all-start.2) | async-done | bytes 720928 | tf_op jit(solution)/shard_map/all_to_all | solution.py:125
  123.0 10.1 %shard_map.297 = (bf16[256,1408]{1,0:T(8,128)(2,1)S(1)}, f32[256,1408]{1,0:T(8,128)S(1)}, f32[4,1,1408]{2,1,0:T(1,128)S(1)}) custom-call(bf16[256,1408]{1,0:T(8,128)(2,1)S(1)} %get-tuple-element.211.q_ref, bf16[256,1408]{1,0:T(8,128)(2,1)S(1)} %slice.361.k_ref, ...), custom_call_target="tpu_custom_call", output_to_operand_aliasing={{0}: (5, {}), {1}: (6, {}), {2}: (7, {})} | custom-call | flops 12180258816 | bytes 2162688 | tf_op jit(solution)/shard_map/pallas_call | solution.py:225
  142.7 17.9 %collective-permute-done.7 = bf16[352,1024]{1,0:T(8,128)(2,1)S(1)} collective-permute-done((bf16[352,1024]{1,0:T(8,128)(2,1)S(1)}, bf16[352,1024]{1,0:T(8,128)(2,1)S(1)}, u32[]{:S(2)}, u32[]{:S(2)}) %collective-permute-start.7) | collective-permute-done | bytes 720928 | tf_op jit(solution)/shard_map/ppermute | solution.py:20
  162.1 17.2 %collective-permute-done.9 = bf16[352,1024]{1,0:T(8,128)(2,1)S(1)} collective-permute-done((bf16[352,1024]{1,0:T(8,128)(2,1)S(1)}, bf16[352,1024]{1,0:T(8,128)(2,1)S(1)}, u32[]{:S(2)}, u32[]{:S(2)}) %collective-permute-start.9) | collective-permute-done | bytes 720928 | tf_op jit(solution)/shard_map/ppermute | solution.py:20
  188.8 9.8 %shard_map.299 = (bf16[1408,1024]{1,0:T(8,128)(2,1)S(1)}, f32[1408,1024]{1,0:T(8,128)}, f32[704,1024]{1,0:T(8,128)S(1)}, bf16[704,1024]{1,0:T(8,128)(2,1)}) custom-call(bf16[704,1024]{1,0:T(8,128)(2,1)S(1)} %copy-done.3, bf16[704,1024]{1,0:T(8,128)(2,1)S(1)} %copy-done.19, bf16[1024,2048]{1,0:T(8,128)(2,1)S(1)} %copy-done.15, ...), custom_call_target="tpu_custom_call" | custom-call | flops 11811160064 | bytes 20054016 | tf_op jit(solution)/shard_map/pallas_call | solution.py:382
  198.6 8.8 %shard_map.300 = (bf16[1408,1024]{1,0:T(8,128)(2,1)S(1)}, f32[704,1024]{1,0:T(8,128)S(1)}, bf16[704,1024]{1,0:T(8,128)(2,1)S(1)}, f32[1,1024]{1,0:T(1,128)S(1)}) custom-call(bf16[704,1024]{1,0:T(8,128)(2,1)} %pad_maximum_fusion.2.near_ref.gn_ref, bf16[704,1024]{1,0:T(8,128)(2,1)} %collective-permute-done.8.far_ref.gf_ref, bf16[1024,2048]{1,0:T(8,128)(2,1)S(1)} %copy-done.16, ...), custom_call_target="tpu_custom_call" | custom-call | flops 11811160064 | bytes 20054016 | tf_op jit(solution)/shard_map/pallas_call | solution.py:402
  215.2 11.4 %shard_map.301 = bf16[1024,2048]{1,0:T(8,128)(2,1)} custom-call(bf16[704,1024]{1,0:T(8,128)(2,1)} %pad_maximum_fusion.2.near_ref.gn_ref, bf16[704,1024]{1,0:T(8,128)(2,1)} %collective-permute-done.8.far_ref.gf_ref, bf16[704,1024]{1,0:T(8,128)(2,1)S(1)} %copy-done.4, bf16[704,1024]{1,0:T(8,128)(2,1)S(1)} %copy-done.20, ...), custom_call_target="tpu_custom_call" | custom-call | flops 11811160064 | bytes 15728640 | tf_op jit(solution)/shard_map/pallas_call | solution.py:461
  226.6 6.5 %collective-permute-done.12 = bf16[352,1024]{1,0:T(8,128)(2,1)} collective-permute-done((bf16[352,1024]{1,0:T(8,128)(2,1)}, bf16[352,1024]{1,0:T(8,128)(2,1)}, u32[]{:S(2)}, u32[]{:S(2)}) %collective-permute-start.12) | collective-permute-done | bytes 720928 | tf_op jit(solution)/shard_map/ppermute | solution.py:20
  235.9 3.9 multiply_reduce_fusion.2
  242.3 15.1 %collective-permute-done.13 = bf16[352,1024]{1,0:T(8,128)(2,1)S(1)} collective-permute-done((bf16[352,1024]{1,0:T(8,128)(2,1)S(1)}, bf16[352,1024]{1,0:T(8,128)(2,1)S(1)}, u32[]{:S(2)}, u32[]{:S(2)}) %collective-permute-start.13) | collective-permute-done | bytes 720928 | tf_op jit(solution)/shard_map/ppermute | solution.py:20
  261.9 11.1 %shard_map.302.refs_0_ = bf16[3,256,1408]{2,1,0:T(8,128)(2,1)S(1)} custom-call(bf16[256,1408]{1,0:T(8,128)(2,1)S(1)} %copy-done.10, bf16[256,1408]{1,0:T(8,128)(2,1)S(1)} %copy-done.6, bf16[256,1408]{1,0:T(8,128)(2,1)S(1)} %copy-done.8, bf16[256,1408]{1,0:T(8,128)(2,1)S(1)} %fusion.11.g_ref, f32[256,1408]{1,0:T(8,128)S(1)} %copy-done.29, ...), custom_call_target="tpu_custom_call" | custom-call | flops 14210301952 | bytes 3604480 | tf_op jit(solution)/shard_map/pallas_call | solution.py:284
  276.4 11.2 %shard_map.303 = bf16[3,256,1408]{2,1,0:T(8,128)(2,1)S(1)} custom-call(bf16[256,1408]{1,0:T(8,128)(2,1)S(1)} %copy-done.10, bf16[256,1408]{1,0:T(8,128)(2,1)S(1)} %copy-done.6, bf16[256,1408]{1,0:T(8,128)(2,1)S(1)} %copy-done.8, bf16[256,1408]{1,0:T(8,128)(2,1)S(1)} %fusion.11.g_ref, f32[256,1408]{1,0:T(8,128)S(1)} %copy-done.29, ...), custom_call_target="tpu_custom_call", output_to_operand_aliasing={{}: (8, {})} | custom-call | flops 14210301952 | bytes 3604480 | tf_op jit(solution)/shard_map/pallas_call | solution.py:284
  287.6 4.0 shard_map.304
  295.1 5.5 %shard_map.305 = bf16[512,1024]{1,0:T(8,128)(2,1)S(1)} custom-call(s32[1]{0:T(128)} %bitcast.39.place_ref, bf16[704,1024]{1,0:T(8,128)(2,1)S(1)} %copy-done.1, bf16[704,1024]{1,0:T(8,128)(2,1)} %collective-permute-done.1.ff_ref, bf16[704,1024]{1,0:T(8,128)(2,1)S(1)} %pad_maximum_fusion.4.gn_ref, bf16[704,1024]{1,0:T(8,128)(2,1)S(1)} %collective-permute-done.15.gf_ref, ...), custom_call_target="tpu_custom_call" | custom-call | flops 2952790016 | bytes 7864320 | tf_op jit(solution)/shard_map/pallas_call | solution.py:542
  305.7 5.6 %shard_map.306 = f32[512,1024]{1,0:T(8,128)S(1)} custom-call(s32[1]{0:T(128)} %bitcast.39.place_ref, bf16[704,1024]{1,0:T(8,128)(2,1)S(1)} %copy-done.1, bf16[704,1024]{1,0:T(8,128)(2,1)} %collective-permute-done.1.ff_ref, bf16[704,1024]{1,0:T(8,128)(2,1)S(1)} %pad_maximum_fusion.4.gn_ref, bf16[704,1024]{1,0:T(8,128)(2,1)S(1)} %collective-permute-done.15.gf_ref, ...), custom_call_target="tpu_custom_call" | custom-call | flops 2952790016 | bytes 7864320 | tf_op jit(solution)/shard_map/pallas_call | solution.py:542
  311.3 6.1 %all-to-all-start.3 = ((bf16[8,352,128]{2,1,0:T(8,128)(2,1)}), bf16[8,352,128]{2,1,0:T(8,128)(2,1)}, u32[]{:S(2)}, u32[]{:S(2)}) async-start(bf16[8,352,128]{2,1,0:T(8,128)(2,1)} %bitcast.179), calls=%async_computation.4 | async-start | bytes 1441792 | tf_op jit(solution)/shard_map/all_to_all | solution.py:125
  317.5 4.8 %collective-permute-done.18 = bf16[352,1024]{1,0:T(8,128)(2,1)} collective-permute-done((bf16[352,1024]{1,0:T(8,128)(2,1)}, bf16[352,1024]{1,0:T(8,128)(2,1)}, u32[]{:S(2)}, u32[]{:S(2)}) %collective-permute-start.18) | collective-permute-done | bytes 720928 | tf_op jit(solution)/shard_map/ppermute | solution.py:20
  322.3 13.9 %collective-permute-done.19 = bf16[512,1024]{1,0:T(8,128)(2,1)} collective-permute-done((bf16[512,1024]{1,0:T(8,128)(2,1)S(1)}, bf16[512,1024]{1,0:T(8,128)(2,1)}, u32[]{:S(2)}, u32[]{:S(2)}) %collective-permute-start.19) | collective-permute-done | bytes 1048608 | tf_op jit(solution)/shard_map/ppermute | solution.py:20
  338.9 3.5 bitcast_bitcast_fusion
  345.6 6.7 %all-to-all-start.4 = ((bf16[8,400,128]{2,1,0:T(8,128)(2,1)}), bf16[8,400,128]{2,1,0:T(8,128)(2,1)S(1)}, u32[]{:S(2)}, u32[]{:S(2)}) async-start(bf16[8,400,128]{2,1,0:T(8,128)(2,1)} %pad_maximum_fusion.6), calls=%async_computation.5 | async-start | bytes 1638400 | tf_op jit(solution)/shard_map/all_to_all | solution.py:125
  358.9 19.7 %collective-permute-done.20 = bf16[256,1024]{1,0:T(8,128)(2,1)} collective-permute-done((bf16[256,1024]{1,0:T(8,128)(2,1)}, bf16[256,1024]{1,0:T(8,128)(2,1)}, u32[]{:S(2)}, u32[]{:S(2)}) %collective-permute-start.20) | collective-permute-done | bytes 524320 | tf_op jit(solution)/shard_map/ppermute | solution.py:20
  385.0 3.5 all-to-all-start.5
  391.8 15.6 %collective-permute-done.23 = f32[8,128]{1,0:T(8,128)S(1)} collective-permute-done((f32[8,128]{1,0:T(8,128)S(1)}, f32[8,128]{1,0:T(8,128)S(1)}, u32[]{:S(2)}, u32[]{:S(2)}) %collective-permute-start.23) | collective-permute-done | bytes 4128 | tf_op jit(solution)/shard_map/ppermute | solution.py:20
  (275 shorter events, 99.0 us)
Async XLA Ops:
  10.2 23.1 %all-to-all-start = ((bf16[4,2,704,128]{3,2,1,0:T(8,128)(2,1)}), bf16[4,2,704,128]{3,2,1,0:T(8,128)(2,1)S(1)}, u32[]{:S(2)}, u32[]{:S(2)}) async-start(bf16[4,2,704,128]{3,2,1,0:T(8,128)(2,1)} %pad_maximum_fusion), calls=%async_computation | async-start | bytes 2883584 | tf_op jit(solution)/shard_map/all_to_all | solution.py:96
  35.2 31.4 %all-to-all-start.1 = ((bf16[8,384,128]{2,1,0:T(8,128)(2,1)}), bf16[8,384,128]{2,1,0:T(8,128)(2,1)S(1)}, u32[]{:S(2)}, u32[]{:S(2)}) async-start(bf16[8,384,128]{2,1,0:T(8,128)(2,1)} %pad_maximum_fusion.7), calls=%async_computation.1 | async-start | bytes 1572864 | tf_op jit(solution)/shard_map/all_to_all | solution.py:125
  41.9 52.7 %all-gather.3.cloned.1.call-start = ((), (), s32[]{:S(2)}) async-start(), calls=%async_computation.7 | async-start | bytes 1769472 | tf_op jit(solution)/shard_map/all_gather | solution.py:628
  67.3 15.8 %collective-permute-start = (bf16[352,1024]{1,0:T(8,128)(2,1)S(1)}, bf16[352,1024]{1,0:T(8,128)(2,1)}, u32[]{:S(2)}, u32[]{:S(2)}) collective-permute-start(bf16[352,1024]{1,0:T(8,128)(2,1)S(1)} %add_convert_fusion.3), channel_id=1, source_target_pairs={{0,16},{8,24},{16,0},{24,8},{1,17},{9,25},{17,1},{25,9},{2,18},{10... | collective-permute-start | bytes 2162696 | tf_op jit(solution)/shard_map/ppermute | solution.py:20
  68.4 5.2 %collective-permute-start.3 = (bf16[1,128,256]{2,1,0:T(8,128)(2,1)S(1)}, bf16[1,128,256]{2,1,0:T(8,128)(2,1)S(1)}, u32[]{:S(2)}, u32[]{:S(2)}) collective-permute-start(bf16[1,128,256]{2,1,0:T(8,128)(2,1)S(1)} %bitcast.188), channel_id=1, source_target_pairs={{0,4},{1,5},{2,6},{3,7},{4,0},{5,1},{6,2},{7,3},{8,12},{9,13},{10,... | collective-permute-start | bytes 196616 | tf_op jit(solution)/shard_map/ppermute | solution.py:20
  73.7 10.9 %collective-permute-start.4 = (bf16[2,128,256]{2,1,0:T(8,128)(2,1)S(1)}, bf16[2,128,256]{2,1,0:T(8,128)(2,1)S(1)}, u32[]{:S(2)}, u32[]{:S(2)}) collective-permute-start(bf16[2,128,256]{2,1,0:T(8,128)(2,1)S(1)} %maximum_bitcast_fusion), channel_id=1, source_target_pairs={{0,2},{1,3},{2,0},{3,1},{4,6},{5,7},{6,4},{7,5},{8,10},{9,11},{10,... | collective-permute-start | bytes 393224 | tf_op jit(solution)/shard_map/ppermute | solution.py:20
  84.3 10.2 %collective-permute-start.1 = (bf16[704,1024]{1,0:T(8,128)(2,1)S(1)}, bf16[704,1024]{1,0:T(8,128)(2,1)}, u32[]{:S(2)}, u32[]{:S(2)}) collective-permute-start(bf16[704,1024]{1,0:T(8,128)(2,1)S(1)} %pad_maximum_fusion.1.fn_ref), channel_id=1, source_target_pairs={{0,8},{8,0},{16,24},{24,16},{1,9},{9,1},{17,25},{25,17},{2,10},{10... | collective-permute-start | bytes 4325384 | tf_op jit(solution)/shard_map/ppermute | solution.py:20
  84.6 9.7 %collective-permute-start.5 = (bf16[4,128,256]{2,1,0:T(8,128)(2,1)S(1)}, bf16[4,128,256]{2,1,0:T(8,128)(2,1)S(1)}, u32[]{:S(2)}, u32[]{:S(2)}) collective-permute-start(bf16[4,128,256]{2,1,0:T(8,128)(2,1)S(1)} %bitcast.185), channel_id=1, source_target_pairs={{0,1},{1,0},{2,3},{3,2},{4,5},{5,4},{6,7},{7,6},{8,9},{9,8},{10,11... | collective-permute-start | bytes 786440 | tf_op jit(solution)/shard_map/ppermute | solution.py:20
  87.5 32.7 %all-to-all-start.2 = ((bf16[8,352,128]{2,1,0:T(8,128)(2,1)}), bf16[8,352,128]{2,1,0:T(8,128)(2,1)}, u32[]{:S(2)}, u32[]{:S(2)}) async-start(bf16[8,352,128]{2,1,0:T(8,128)(2,1)} %get-tuple-element.66), calls=%async_computation.2 | async-start | bytes 1441792 | tf_op jit(solution)/shard_map/all_to_all | solution.py:125
  91.7 92.1 %all-gather.5.cloned.1.call-start = ((), (), s32[]{:S(2)}) async-start(), calls=%async_computation.8 | async-start | bytes 4718592 | tf_op jit(solution)/shard_map/all_gather | solution.py:641
  92.5 243.7 %reduce-scatter.2.cloned.1.call-start = ((), (), s32[]{:S(2)}) async-start(), calls=%async_computation.9 | async-start | bytes 4718592 | tf_op jit(solution)/shard_map/reduce_scatter | solution.py:685
  121.5 14.6 %collective-permute-start.2 = (bf16[352,1024]{1,0:T(8,128)(2,1)S(1)}, bf16[352,1024]{1,0:T(8,128)(2,1)S(1)}, u32[]{:S(2)}, u32[]{:S(2)}) collective-permute-start(bf16[352,1024]{1,0:T(8,128)(2,1)S(1)} %fusion.16), channel_id=1, source_target_pairs={{0,16},{8,24},{16,0},{24,8},{1,17},{9,25},{17,1},{25,9},{2,18},{10... | collective-permute-start | bytes 2162696 | tf_op jit(solution)/shard_map/ppermute | solution.py:20
  138.2 3.3 collective-permute-start.6
  142.3 18.2 %collective-permute-start.7 = (bf16[352,1024]{1,0:T(8,128)(2,1)S(1)}, bf16[352,1024]{1,0:T(8,128)(2,1)S(1)}, u32[]{:S(2)}, u32[]{:S(2)}) collective-permute-start(bf16[352,1024]{1,0:T(8,128)(2,1)S(1)} %slice.360), channel_id=1, source_target_pairs={{0,16},{8,24},{16,0},{24,8},{1,17},{9,25},{17,1},{25,9},{2,18},{10... | collective-permute-start | bytes 2162696 | tf_op jit(solution)/shard_map/ppermute | solution.py:20
  161.8 17.5 %collective-permute-start.9 = (bf16[352,1024]{1,0:T(8,128)(2,1)S(1)}, bf16[352,1024]{1,0:T(8,128)(2,1)S(1)}, u32[]{:S(2)}, u32[]{:S(2)}) collective-permute-start(bf16[352,1024]{1,0:T(8,128)(2,1)S(1)} %add_convert_fusion.2), channel_id=1, source_target_pairs={{0,16},{8,24},{16,0},{24,8},{1,17},{9,25},{17,1},{25,9},{2,18},{10... | collective-permute-start | bytes 2162696 | tf_op jit(solution)/shard_map/ppermute | solution.py:20
  179.5 3.3 collective-permute-start.10
  181.0 17.6 %collective-permute-start.8 = (bf16[704,1024]{1,0:T(8,128)(2,1)}, bf16[704,1024]{1,0:T(8,128)(2,1)}, u32[]{:S(2)}, u32[]{:S(2)}) collective-permute-start(bf16[704,1024]{1,0:T(8,128)(2,1)} %pad_maximum_fusion.2.near_ref.gn_ref), channel_id=1, source_target_pairs={{0,8},{8,0},{16,24},{24,16},{1,9},{9,1},{17,25},{25,17},{2,10},{10... | collective-permute-start | bytes 4325384 | tf_op jit(solution)/shard_map/ppermute | solution.py:20
  207.4 4.0 collective-permute-start.11
  207.6 32.8 %collective-permute-start.14 = (bf16[704,1024]{1,0:T(8,128)(2,1)}, bf16[704,1024]{1,0:T(8,128)(2,1)}, u32[]{:S(2)}, u32[]{:S(2)}) collective-permute-start(bf16[704,1024]{1,0:T(8,128)(2,1)} %get-tuple-element.85), channel_id=1, source_target_pairs={{0,8},{8,0},{16,24},{24,16},{1,9},{9,1},{17,25},{25,17},{2,10},{10... | collective-permute-start | bytes 4325384 | tf_op jit(solution)/shard_map/ppermute | solution.py:20
  214.6 18.5 %collective-permute-start.12 = (bf16[352,1024]{1,0:T(8,128)(2,1)}, bf16[352,1024]{1,0:T(8,128)(2,1)}, u32[]{:S(2)}, u32[]{:S(2)}) collective-permute-start(bf16[352,1024]{1,0:T(8,128)(2,1)} %slice.359), channel_id=1, source_target_pairs={{0,16},{8,24},{16,0},{24,8},{1,17},{9,25},{17,1},{25,9},{2,18},{10... | collective-permute-start | bytes 2162696 | tf_op jit(solution)/shard_map/ppermute | solution.py:20
  240.0 17.4 %collective-permute-start.13 = (bf16[352,1024]{1,0:T(8,128)(2,1)S(1)}, bf16[352,1024]{1,0:T(8,128)(2,1)S(1)}, u32[]{:S(2)}, u32[]{:S(2)}) collective-permute-start(bf16[352,1024]{1,0:T(8,128)(2,1)S(1)} %multiply_convert_fusion), channel_id=1, source_target_pairs={{0,16},{8,24},{16,0},{24,8},{1,17},{9,25},{17,1},{25,9},{2,18},{10... | collective-permute-start | bytes 2162696 | tf_op jit(solution)/shard_map/ppermute | solution.py:20
  257.8 18.6 %collective-permute-start.16 = (bf16[352,1024]{1,0:T(8,128)(2,1)S(1)}, bf16[352,1024]{1,0:T(8,128)(2,1)S(1)}, u32[]{:S(2)}, u32[]{:S(2)}) collective-permute-start(bf16[352,1024]{1,0:T(8,128)(2,1)S(1)} %slice.358), channel_id=1, source_target_pairs={{0,16},{8,24},{16,0},{24,8},{1,17},{9,25},{17,1},{25,9},{2,18},{10... | collective-permute-start | bytes 2162696 | tf_op jit(solution)/shard_map/ppermute | solution.py:20
  291.7 8.9 %collective-permute-start.17 = (bf16[704,1024]{1,0:T(8,128)(2,1)S(1)}, bf16[704,1024]{1,0:T(8,128)(2,1)S(1)}, u32[]{:S(2)}, u32[]{:S(2)}) collective-permute-start(bf16[704,1024]{1,0:T(8,128)(2,1)S(1)} %get-tuple-element.92), channel_id=1, source_target_pairs={{0,8},{8,0},{16,24},{24,16},{1,9},{9,1},{17,25},{25,17},{2,10},{10... | collective-permute-start | bytes 4325384 | tf_op jit(solution)/shard_map/ppermute | solution.py:20
  300.6 35.6 %collective-permute-start.19 = (bf16[512,1024]{1,0:T(8,128)(2,1)S(1)}, bf16[512,1024]{1,0:T(8,128)(2,1)}, u32[]{:S(2)}, u32[]{:S(2)}) collective-permute-start(bf16[512,1024]{1,0:T(8,128)(2,1)S(1)} %shard_map.305), channel_id=1, source_target_pairs={{0,1},{1,0},{2,3},{3,2},{4,5},{5,4},{6,7},{7,6},{8,9},{9,8},{10,11... | collective-permute-start | bytes 3145736 | tf_op jit(solution)/shard_map/ppermute | solution.py:20
  303.7 18.6 %collective-permute-start.18 = (bf16[352,1024]{1,0:T(8,128)(2,1)}, bf16[352,1024]{1,0:T(8,128)(2,1)}, u32[]{:S(2)}, u32[]{:S(2)}) collective-permute-start(bf16[352,1024]{1,0:T(8,128)(2,1)} %slice.357), channel_id=1, source_target_pairs={{0,16},{8,24},{16,0},{24,8},{1,17},{9,25},{17,1},{25,9},{2,18},{10... | collective-permute-start | bytes 2162696 | tf_op jit(solution)/shard_map/ppermute | solution.py:20
  311.3 32.1 %all-to-all-start.3 = ((bf16[8,352,128]{2,1,0:T(8,128)(2,1)}), bf16[8,352,128]{2,1,0:T(8,128)(2,1)}, u32[]{:S(2)}, u32[]{:S(2)}) async-start(bf16[8,352,128]{2,1,0:T(8,128)(2,1)} %bitcast.179), calls=%async_computation.4 | async-start | bytes 1441792 | tf_op jit(solution)/shard_map/all_to_all | solution.py:125
  345.6 33.0 %all-to-all-start.4 = ((bf16[8,400,128]{2,1,0:T(8,128)(2,1)}), bf16[8,400,128]{2,1,0:T(8,128)(2,1)S(1)}, u32[]{:S(2)}, u32[]{:S(2)}) async-start(bf16[8,400,128]{2,1,0:T(8,128)(2,1)} %pad_maximum_fusion.6), calls=%async_computation.5 | async-start | bytes 1638400 | tf_op jit(solution)/shard_map/all_to_all | solution.py:125
  354.9 23.7 %collective-permute-start.20 = (bf16[256,1024]{1,0:T(8,128)(2,1)}, bf16[256,1024]{1,0:T(8,128)(2,1)}, u32[]{:S(2)}, u32[]{:S(2)}) collective-permute-start(bf16[256,1024]{1,0:T(8,128)(2,1)} %slice.362), channel_id=1, source_target_pairs={{0,2},{1,3},{2,0},{3,1},{4,6},{5,7},{6,4},{7,5},{8,10},{9,11},{10,... | collective-permute-start | bytes 1572872 | tf_op jit(solution)/shard_map/ppermute | solution.py:20
  378.7 10.5 %collective-permute-start.22 = (f32[8,128]{1,0:T(8,128)S(1)}, f32[8,128]{1,0:T(8,128)S(1)}, u32[]{:S(2)}, u32[]{:S(2)}) collective-permute-start(f32[8,128]{1,0:T(8,128)S(1)} %bitcast_reduce_fusion), channel_id=1, source_target_pairs={{0,8},{8,0},{16,24},{24,16},{1,9},{9,1},{17,25},{25,17},{2,10},{10... | collective-permute-start | bytes 12296 | tf_op jit(solution)/shard_map/ppermute | solution.py:20
  380.0 27.8 %collective-permute-start.21 = (bf16[128,1024]{1,0:T(8,128)(2,1)S(1)}, bf16[128,1024]{1,0:T(8,128)(2,1)S(1)}, u32[]{:S(2)}, u32[]{:S(2)}) collective-permute-start(bf16[128,1024]{1,0:T(8,128)(2,1)S(1)} %slice.363), channel_id=1, source_target_pairs={{0,4},{1,5},{2,6},{3,7},{4,0},{5,1},{6,2},{7,3},{8,12},{9,13},{10,... | collective-permute-start | bytes 786440 | tf_op jit(solution)/shard_map/ppermute | solution.py:20
  385.0 24.8 %all-to-all-start.5 = ((bf16[4,2,704,128]{3,2,1,0:T(8,128)(2,1)}), bf16[4,2,704,128]{3,2,1,0:T(8,128)(2,1)S(1)}, u32[]{:S(2)}, u32[]{:S(2)}) async-start(bf16[4,2,704,128]{3,2,1,0:T(8,128)(2,1)} %bitcast.55), calls=%async_computation.6 | async-start | bytes 2883584 | tf_op jit(solution)/shard_map/all_to_all | solution.py:103
  389.2 18.1 %collective-permute-start.23 = (f32[8,128]{1,0:T(8,128)S(1)}, f32[8,128]{1,0:T(8,128)S(1)}, u32[]{:S(2)}, u32[]{:S(2)}) collective-permute-start(f32[8,128]{1,0:T(8,128)S(1)} %add.202), channel_id=1, source_target_pairs={{0,16},{8,24},{16,0},{24,8},{1,17},{9,25},{17,1},{25,9},{2,18},{10... | collective-permute-start | bytes 12296 | tf_op jit(solution)/shard_map/ppermute | solution.py:20
  (59 other events, 420.9 us)
Sparse Core Ops, SparseCore 0:
  45.5 45.6 all-gather.2
  95.3 75.8 all-gather.4
  236.0 99.5 reduce-scatter.1

commit v5 on v4

--- a/solution.py
+++ b/solution.py
@@ -101,6 +101,22 @@
     nx, ny = lax.axis_size("gx"), lax.axis_size("gy")
     parts = parts.reshape((nx, ny // nx) + parts.shape[1:])
     return lax.all_to_all(parts, "gx", split_axis=0, concat_axis=0, tiled=True)
+
+
+def trade_images(parts):
+    nx, ny = lax.axis_size("gx"), lax.axis_size("gy")
+    place = lax.axis_index("gx")
+    shape = (nx, ny // nx) + parts.shape[1:]
+    bit = 1
+    while bit < nx:
+        pair = parts.reshape((nx // (2 * bit), 2, bit) + shape[1:])
+        upper = (place & bit) != 0
+        mine = jnp.where(upper, pair[:, 1], pair[:, 0])
+        theirs = swap(jnp.where(upper, pair[:, 0], pair[:, 1]), "gx", bit)
+        low, high = jnp.where(upper, theirs, mine), jnp.where(upper, mine, theirs)
+        parts = jnp.stack((low, high), axis=1).reshape(shape)
+        bit *= 2
+    return parts
 
 
 def join_images(parts, packed_shape):
@@ -761,9 +777,8 @@
         head_kept, head_other = scatter_step(head_grads, bit)
         head_grads = head_kept + head_other.astype(WIDE)
         bit *= 2
-    both = to_images(jnp.concatenate((input_parts[:, :block], output_parts), axis=1))
-    block_output = join_images(both[:, :, block:], packed_shape)
-    input_gradient = join_images(both[:, :, :block], packed_shape).astype(WIDE)
+    block_output = join_images(trade_images(output_parts), packed_shape)
+    input_gradient = join_images(to_images(input_parts[:, :block]), packed_shape).astype(WIDE)
     sums = over_rows(sum_lines(input_parts[:, block : block + 16]))
     lines = 2 * image_sums.shape[0] * ny // D
     image_sums = sum_lines(input_parts[:, block + 16 : block + 16 + lines]).reshape(-1)

time: 427 us -> 422 us (0.988)
  waiting for transfers between devices: 194 us -> 176 us
  other arithmetic: 36.7 us -> 43.1 us
  local copies, waits for them, and re-layouts: 31.3 us -> 37.5 us
    ppermute x24 -> x26, waiting for transfers between devices: 143 us -> 120 us  [swap(): return lax.ppermute(values, axis, [(k, k ^ bit) for k in range(size)])]
    unnamed x124 -> x138, local copies, waits for them, and re-layouts: 16.6 us -> 19.7 us
    ppermute x24 -> x26, starting transfers between devices: 15.6 us -> 15.7 us  [swap(): return lax.ppermute(values, axis, [(k, k ^ bit) for k in range(size)])]
  transfers between devices with their start and end apart: 33 -> 35, of which waited for: 21 -> 23; matrix products, arithmetic and copies ran while one was open for 12% -> 14% of each run, Pallas kernels for 19% -> 20%
where the time goes in v5:
time: 422 us; the launch traced here: 415 us
  waiting for transfers between devices  176 us (42%)
  Pallas kernels  91.3 us (22%)
  starting transfers between devices  46.2 us (11%)
  other arithmetic  43.1 us (10%)
  local copies, waits for them, and re-layouts  37.5 us (9%)
  between operations  15.3 us (4%)
  matrix products  5.85 us (1%)
    ppermute x26, waiting for transfers between devices, swap(): return lax.ppermute(values, axis, [(k, k ^ bit) for k in range(size)])  120 us
    all_to_all x4, waiting for transfers between devices, cross(): return lax.all_to_all(parts, 'gy', split_axis=0, concat_axis=0, tiled=True)  31.7 us
    all_to_all x4, starting transfers between devices, cross(): return lax.all_to_all(parts, 'gy', split_axis=0, concat_axis=0, tiled=True)  22.5 us
    pallas_call x2, Pallas kernels, attend_backward(): pl.pallas_call(attend_backward_body, grid=(count,), in_specs=[head, head,...  22.3 us
    pallas_call x2, Pallas kernels, attend_forward(): pl.pallas_call(attend_forward_body, grid=(count,), in_specs=[head, head,...  20.5 us
    unnamed x138, local copies, waits for them, and re-layouts  19.7 us
    all_to_all x1, waiting for transfers between devices, to_rows(): parts = lax.all_to_all(parts, 'gx', split_axis=0, concat_axis=0, tiled=True)  18.6 us
    ppermute x26, starting transfers between devices, swap(): return lax.ppermute(values, axis, [(k, k ^ bit) for k in range(size)])  15.7 us
  transfers between devices with their start and end apart: 35, of which 23 were waited for; matrix products, arithmetic and copies ran while one was open for 14% of the time, Pallas kernels for 20%

profile of v5, /device:TPU:0, one launch (start us, length us, event | category | flops | bytes accessed | tf_op | source)
XLA Modules:
  0.0 414.9 jit_solution(17244620322135370243)
XLA Ops:
  10.2 4.4 %all-to-all-start = ((bf16[4,2,704,128]{3,2,1,0:T(8,128)(2,1)}), bf16[4,2,704,128]{3,2,1,0:T(8,128)(2,1)S(1)}, u32[]{:S(2)}, u32[]{:S(2)}) async-start(bf16[4,2,704,128]{3,2,1,0:T(8,128)(2,1)} %pad_maximum_fusion), calls=%async_computation | async-start | bytes 2883584 | tf_op jit(solution)/shard_map/all_to_all | solution.py:96
  14.7 18.6 %all-to-all-done = bf16[4,2,704,128]{3,2,1,0:T(8,128)(2,1)S(1)} async-done(((bf16[4,2,704,128]{3,2,1,0:T(8,128)(2,1)}), bf16[4,2,704,128]{3,2,1,0:T(8,128)(2,1)S(1)}, u32[]{:S(2)}, u32[]{:S(2)}) %all-to-all-start) | async-done | bytes 1441824 | tf_op jit(solution)/shard_map/all_to_all | solution.py:96
  35.2 6.7 %all-to-all-start.1 = ((bf16[8,384,128]{2,1,0:T(8,128)(2,1)}), bf16[8,384,128]{2,1,0:T(8,128)(2,1)S(1)}, u32[]{:S(2)}, u32[]{:S(2)}) async-start(bf16[8,384,128]{2,1,0:T(8,128)(2,1)} %pad_maximum_fusion.6), calls=%async_computation.1 | async-start | bytes 1572864 | tf_op jit(solution)/shard_map/all_to_all | solution.py:141
  44.1 22.5 %all-to-all-done.1 = bf16[8,384,128]{2,1,0:T(8,128)(2,1)S(1)} async-done(((bf16[8,384,128]{2,1,0:T(8,128)(2,1)}), bf16[8,384,128]{2,1,0:T(8,128)(2,1)S(1)}, u32[]{:S(2)}, u32[]{:S(2)}) %all-to-all-start.1) | async-done | bytes 786464 | tf_op jit(solution)/shard_map/all_to_all | solution.py:141
  68.4 5.2 %collective-permute-done.3 = bf16[1,128,256]{2,1,0:T(8,128)(2,1)S(1)} collective-permute-done((bf16[1,128,256]{2,1,0:T(8,128)(2,1)S(1)}, bf16[1,128,256]{2,1,0:T(8,128)(2,1)S(1)}, u32[]{:S(2)}, u32[]{:S(2)}) %collective-permute-start.3) | collective-permute-done | bytes 65568 | tf_op jit(solution)/shard_map/ppermute | solution.py:20
  73.7 9.3 %collective-permute-done = bf16[352,1024]{1,0:T(8,128)(2,1)} collective-permute-done((bf16[352,1024]{1,0:T(8,128)(2,1)S(1)}, bf16[352,1024]{1,0:T(8,128)(2,1)}, u32[]{:S(2)}, u32[]{:S(2)}) %collective-permute-start) | collective-permute-done | bytes 720928 | tf_op jit(solution)/shard_map/ppermute | solution.py:20
  87.5 4.2 %all-to-all-start.2 = ((bf16[8,352,128]{2,1,0:T(8,128)(2,1)}), bf16[8,352,128]{2,1,0:T(8,128)(2,1)}, u32[]{:S(2)}, u32[]{:S(2)}) async-start(bf16[8,352,128]{2,1,0:T(8,128)(2,1)} %get-tuple-element.66), calls=%async_computation.2 | async-start | bytes 1441792 | tf_op jit(solution)/shard_map/all_to_all | solution.py:141
  94.5 4.8 %convolution_bitcast_fusion = f32[768,1408]{1,0:T(8,128)S(1)} fusion(bf16[1024,768]{1,0:T(8,128)(2,1)} %all-gather.3.cloned.1.call-done.weight_ref, bf16[704,1024]{1,0:T(8,128)(2,1)} %collective-permute-done.1.ff_ref, bf16[352,1024]{1,0:T(8,128)(2,1)} %collective-permute-done, bf16[352,1024]{1,0:T(8,128)(2,1)S(1)} %add_convert_fusion.3), kind=kOutput, calls=%fused_computation | convolution fusion | flops 2223243264 | bytes 8781824 | tf_op jit(solution)/shard_map/dot_general | solution.py:669
  99.8 10.3 %shard_map.296 = (bf16[256,1408]{1,0:T(8,128)(2,1)S(1)}, f32[256,1408]{1,0:T(8,128)S(1)}, f32[4,1,1408]{2,1,0:T(1,128)S(1)}) custom-call(bf16[256,1408]{1,0:T(8,128)(2,1)S(1)} %get-tuple-element.211.q_ref, bf16[256,1408]{1,0:T(8,128)(2,1)S(1)} %slice.399.k_ref, bf16[256,1408]{1,0:T(8,128)(2,1)S(1)} %get-tuple-element.210.v_ref, ...), custom_call_target="tpu_custom_call" | custom-call | flops 12180258816 | bytes 2162688 | tf_op jit(solution)/shard_map/pallas_call | solution.py:241
  112.2 8.0 %all-to-all-done.2 = bf16[8,352,128]{2,1,0:T(8,128)(2,1)} async-done(((bf16[8,352,128]{2,1,0:T(8,128)(2,1)}), bf16[8,352,128]{2,1,0:T(8,128)(2,1)}, u32[]{:S(2)}, u32[]{:S(2)}) %all-to-all-start.2) | async-done | bytes 720928 | tf_op jit(solution)/shard_map/all_to_all | solution.py:141
  123.0 10.1 %shard_map.297 = (bf16[256,1408]{1,0:T(8,128)(2,1)S(1)}, f32[256,1408]{1,0:T(8,128)S(1)}, f32[4,1,1408]{2,1,0:T(1,128)S(1)}) custom-call(bf16[256,1408]{1,0:T(8,128)(2,1)S(1)} %get-tuple-element.211.q_ref, bf16[256,1408]{1,0:T(8,128)(2,1)S(1)} %slice.399.k_ref, ...), custom_call_target="tpu_custom_call", output_to_operand_aliasing={{0}: (5, {}), {1}: (6, {}), {2}: (7, {})} | custom-call | flops 12180258816 | bytes 2162688 | tf_op jit(solution)/shard_map/pallas_call | solution.py:241
  142.7 17.9 %collective-permute-done.7 = bf16[352,1024]{1,0:T(8,128)(2,1)S(1)} collective-permute-done((bf16[352,1024]{1,0:T(8,128)(2,1)S(1)}, bf16[352,1024]{1,0:T(8,128)(2,1)S(1)}, u32[]{:S(2)}, u32[]{:S(2)}) %collective-permute-start.7) | collective-permute-done | bytes 720928 | tf_op jit(solution)/shard_map/ppermute | solution.py:20
  162.1 17.2 %collective-permute-done.9 = bf16[352,1024]{1,0:T(8,128)(2,1)S(1)} collective-permute-done((bf16[352,1024]{1,0:T(8,128)(2,1)S(1)}, bf16[352,1024]{1,0:T(8,128)(2,1)S(1)}, u32[]{:S(2)}, u32[]{:S(2)}) %collective-permute-start.9) | collective-permute-done | bytes 720928 | tf_op jit(solution)/shard_map/ppermute | solution.py:20
  188.7 9.8 %shard_map.299 = (bf16[1408,1024]{1,0:T(8,128)(2,1)S(1)}, f32[1408,1024]{1,0:T(8,128)}, f32[704,1024]{1,0:T(8,128)S(1)}, bf16[704,1024]{1,0:T(8,128)(2,1)}) custom-call(bf16[704,1024]{1,0:T(8,128)(2,1)S(1)} %copy-done.5, bf16[704,1024]{1,0:T(8,128)(2,1)S(1)} %copy-done.25, bf16[1024,2048]{1,0:T(8,128)(2,1)S(1)} %copy-done.19, ...), custom_call_target="tpu_custom_call" | custom-call | flops 11811160064 | bytes 20054016 | tf_op jit(solution)/shard_map/pallas_call | solution.py:398
  198.6 8.8 %shard_map.300 = (bf16[1408,1024]{1,0:T(8,128)(2,1)S(1)}, f32[704,1024]{1,0:T(8,128)S(1)}, bf16[704,1024]{1,0:T(8,128)(2,1)S(1)}, f32[1,1024]{1,0:T(1,128)S(1)}) custom-call(bf16[704,1024]{1,0:T(8,128)(2,1)} %pad_maximum_fusion.2.near_ref.gn_ref, bf16[704,1024]{1,0:T(8,128)(2,1)} %collective-permute-done.8.far_ref.gf_ref, bf16[1024,2048]{1,0:T(8,128)(2,1)S(1)} %copy-done.20, ...), custom_call_target="tpu_custom_call" | custom-call | flops 11811160064 | bytes 20054016 | tf_op jit(solution)/shard_map/pallas_call | solution.py:418
  215.3 11.4 %shard_map.301 = bf16[1024,2048]{1,0:T(8,128)(2,1)} custom-call(bf16[704,1024]{1,0:T(8,128)(2,1)} %pad_maximum_fusion.2.near_ref.gn_ref, bf16[704,1024]{1,0:T(8,128)(2,1)} %collective-permute-done.8.far_ref.gf_ref, bf16[704,1024]{1,0:T(8,128)(2,1)S(1)} %copy-done.6, bf16[704,1024]{1,0:T(8,128)(2,1)S(1)} %copy-done.26, ...), custom_call_target="tpu_custom_call" | custom-call | flops 11811160064 | bytes 15728640 | tf_op jit(solution)/shard_map/pallas_call | solution.py:477
  226.7 6.4 %collective-permute-done.12 = bf16[352,1024]{1,0:T(8,128)(2,1)} collective-permute-done((bf16[352,1024]{1,0:T(8,128)(2,1)}, bf16[352,1024]{1,0:T(8,128)(2,1)}, u32[]{:S(2)}, u32[]{:S(2)}) %collective-permute-start.12) | collective-permute-done | bytes 720928 | tf_op jit(solution)/shard_map/ppermute | solution.py:20
  235.9 3.9 multiply_reduce_fusion.2
  242.2 15.2 %collective-permute-done.13 = bf16[352,1024]{1,0:T(8,128)(2,1)S(1)} collective-permute-done((bf16[352,1024]{1,0:T(8,128)(2,1)S(1)}, bf16[352,1024]{1,0:T(8,128)(2,1)S(1)}, u32[]{:S(2)}, u32[]{:S(2)}) %collective-permute-start.13) | collective-permute-done | bytes 720928 | tf_op jit(solution)/shard_map/ppermute | solution.py:20
  262.0 11.1 %shard_map.302.refs_0_ = bf16[3,256,1408]{2,1,0:T(8,128)(2,1)S(1)} custom-call(bf16[256,1408]{1,0:T(8,128)(2,1)S(1)} %copy-done.14, bf16[256,1408]{1,0:T(8,128)(2,1)S(1)} %copy-done.10, bf16[256,1408]{1,0:T(8,128)(2,1)S(1)} %copy-done.12, bf16[256,1408]{1,0:T(8,128)(2,1)S(1)} %fusion.11.g_ref, f32[256,1408]{1,0:T(8,128)S(1)} %copy-done.35, ...), custom_call_target="tpu_custom_call" | custom-call | flops 14210301952 | bytes 3604480 | tf_op jit(solution)/shard_map/pallas_call | solution.py:300
  273.1 4.4 %collective-permute-done.16 = bf16[352,1024]{1,0:T(8,128)(2,1)S(1)} collective-permute-done((bf16[352,1024]{1,0:T(8,128)(2,1)S(1)}, bf16[352,1024]{1,0:T(8,128)(2,1)S(1)}, u32[]{:S(2)}, u32[]{:S(2)}) %collective-permute-start.16) | collective-permute-done | bytes 720928 | tf_op jit(solution)/shard_map/ppermute | solution.py:20
  277.6 11.2 %shard_map.303 = bf16[3,256,1408]{2,1,0:T(8,128)(2,1)S(1)} custom-call(bf16[256,1408]{1,0:T(8,128)(2,1)S(1)} %copy-done.14, bf16[256,1408]{1,0:T(8,128)(2,1)S(1)} %copy-done.10, bf16[256,1408]{1,0:T(8,128)(2,1)S(1)} %copy-done.12, bf16[256,1408]{1,0:T(8,128)(2,1)S(1)} %fusion.11.g_ref, f32[256,1408]{1,0:T(8,128)S(1)} %copy-done.35, ...), custom_call_target="tpu_custom_call", output_to_operand_aliasing={{}: (8, {})} | custom-call | flops 14210301952 | bytes 3604480 | tf_op jit(solution)/shard_map/pallas_call | solution.py:300
  288.8 4.6 %shard_map.304 = (f32[704,1024]{1,0:T(8,128)S(1)}, bf16[704,1024]{1,0:T(8,128)(2,1)}) custom-call(bf16[768,1408]{1,0:T(8,128)(2,1)S(1)} %bitcast.231, bf16[1024,768]{1,0:T(8,128)(2,1)S(1)} %copy-done.21), custom_call_target="tpu_custom_call" | custom-call | flops 2214592512 | bytes 8060928 | tf_op jit(solution)/shard_map/pallas_call | solution.py:507
  299.4 6.2 %shard_map.305 = bf16[512,1024]{1,0:T(8,128)(2,1)} custom-call(s32[1]{0:T(128)} %bitcast.39.place_ref, bf16[704,1024]{1,0:T(8,128)(2,1)S(1)} %copy-done.1, bf16[704,1024]{1,0:T(8,128)(2,1)} %collective-permute-done.1.ff_ref, bf16[704,1024]{1,0:T(8,128)(2,1)S(1)} %copy-done.3, bf16[704,1024]{1,0:T(8,128)(2,1)S(1)} %copy-done.23, ...), custom_call_target="tpu_custom_call" | custom-call | flops 2952790016 | bytes 7864320 | tf_op jit(solution)/shard_map/pallas_call | solution.py:558
  314.5 5.6 %shard_map.306 = f32[512,1024]{1,0:T(8,128)S(1)} custom-call(s32[1]{0:T(128)} %bitcast.39.place_ref, bf16[704,1024]{1,0:T(8,128)(2,1)S(1)} %copy-done.1, bf16[704,1024]{1,0:T(8,128)(2,1)} %collective-permute-done.1.ff_ref, bf16[704,1024]{1,0:T(8,128)(2,1)S(1)} %copy-done.3, bf16[704,1024]{1,0:T(8,128)(2,1)S(1)} %copy-done.23, ...), custom_call_target="tpu_custom_call" | custom-call | flops 2952790016 | bytes 7864320 | tf_op jit(solution)/shard_map/pallas_call | solution.py:558
  320.1 6.3 %all-to-all-start.3 = ((bf16[8,352,128]{2,1,0:T(8,128)(2,1)}), bf16[8,352,128]{2,1,0:T(8,128)(2,1)}, u32[]{:S(2)}, u32[]{:S(2)}) async-start(bf16[8,352,128]{2,1,0:T(8,128)(2,1)} %bitcast.239), calls=%async_computation.4 | async-start | bytes 1441792 | tf_op jit(solution)/shard_map/all_to_all | solution.py:141
  326.5 4.8 %collective-permute-done.18 = bf16[352,1024]{1,0:T(8,128)(2,1)} collective-permute-done((bf16[352,1024]{1,0:T(8,128)(2,1)}, bf16[352,1024]{1,0:T(8,128)(2,1)}, u32[]{:S(2)}, u32[]{:S(2)}) %collective-permute-start.18) | collective-permute-done | bytes 720928 | tf_op jit(solution)/shard_map/ppermute | solution.py:20
  331.3 7.2 %collective-permute-done.19 = bf16[512,1024]{1,0:T(8,128)(2,1)} collective-permute-done((bf16[512,1024]{1,0:T(8,128)(2,1)}, bf16[512,1024]{1,0:T(8,128)(2,1)}, u32[]{:S(2)}, u32[]{:S(2)}) %collective-permute-start.19) | collective-permute-done | bytes 1048608 | tf_op jit(solution)/shard_map/ppermute | solution.py:20
  348.2 5.2 %all-to-all-start.4 = ((bf16[8,400,128]{2,1,0:T(8,128)(2,1)}), bf16[8,400,128]{2,1,0:T(8,128)(2,1)}, u32[]{:S(2)}, u32[]{:S(2)}) async-start(bf16[8,400,128]{2,1,0:T(8,128)(2,1)} %pad_maximum_fusion.5), calls=%async_computation.5 | async-start | bytes 1638400 | tf_op jit(solution)/shard_map/all_to_all | solution.py:141
  368.6 12.7 %collective-permute-done.22 = bf16[256,1024]{1,0:T(8,128)(2,1)} collective-permute-done((bf16[256,1024]{1,0:T(8,128)(2,1)}, bf16[256,1024]{1,0:T(8,128)(2,1)}, u32[]{:S(2)}, u32[]{:S(2)}) %collective-permute-start.22) | collective-permute-done | bytes 524320 | tf_op jit(solution)/shard_map/ppermute | solution.py:20
  395.2 4.3 %collective-permute-done.23 = bf16[128,1024]{1,0:T(8,128)(2,1)S(1)} collective-permute-done((bf16[128,1024]{1,0:T(8,128)(2,1)S(1)}, bf16[128,1024]{1,0:T(8,128)(2,1)S(1)}, u32[]{:S(2)}, u32[]{:S(2)}) %collective-permute-start.23) | collective-permute-done | bytes 262176 | tf_op jit(solution)/shard_map/ppermute | solution.py:20
  401.5 4.1 all-to-all-done.5
  (299 shorter events, 117.0 us)
Async XLA Ops:
  10.2 23.1 %all-to-all-start = ((bf16[4,2,704,128]{3,2,1,0:T(8,128)(2,1)}), bf16[4,2,704,128]{3,2,1,0:T(8,128)(2,1)S(1)}, u32[]{:S(2)}, u32[]{:S(2)}) async-start(bf16[4,2,704,128]{3,2,1,0:T(8,128)(2,1)} %pad_maximum_fusion), calls=%async_computation | async-start | bytes 2883584 | tf_op jit(solution)/shard_map/all_to_all | solution.py:96
  35.2 31.4 %all-to-all-start.1 = ((bf16[8,384,128]{2,1,0:T(8,128)(2,1)}), bf16[8,384,128]{2,1,0:T(8,128)(2,1)S(1)}, u32[]{:S(2)}, u32[]{:S(2)}) async-start(bf16[8,384,128]{2,1,0:T(8,128)(2,1)} %pad_maximum_fusion.6), calls=%async_computation.1 | async-start | bytes 1572864 | tf_op jit(solution)/shard_map/all_to_all | solution.py:141
  41.9 52.7 %all-gather.3.cloned.1.call-start = ((), (), s32[]{:S(2)}) async-start(), calls=%async_computation.7 | async-start | bytes 1769472 | tf_op jit(solution)/shard_map/all_gather | solution.py:644
  67.3 15.8 %collective-permute-start = (bf16[352,1024]{1,0:T(8,128)(2,1)S(1)}, bf16[352,1024]{1,0:T(8,128)(2,1)}, u32[]{:S(2)}, u32[]{:S(2)}) collective-permute-start(bf16[352,1024]{1,0:T(8,128)(2,1)S(1)} %add_convert_fusion.3), channel_id=1, source_target_pairs={{0,16},{8,24},{16,0},{24,8},{1,17},{9,25},{17,1},{25,9},{2,18},{10... | collective-permute-start | bytes 2162696 | tf_op jit(solution)/shard_map/ppermute | solution.py:20
  68.4 5.2 %collective-permute-start.3 = (bf16[1,128,256]{2,1,0:T(8,128)(2,1)S(1)}, bf16[1,128,256]{2,1,0:T(8,128)(2,1)S(1)}, u32[]{:S(2)}, u32[]{:S(2)}) collective-permute-start(bf16[1,128,256]{2,1,0:T(8,128)(2,1)S(1)} %bitcast.249), channel_id=1, source_target_pairs={{0,4},{1,5},{2,6},{3,7},{4,0},{5,1},{6,2},{7,3},{8,12},{9,13},{10,... | collective-permute-start | bytes 196616 | tf_op jit(solution)/shard_map/ppermute | solution.py:20
  73.7 10.8 %collective-permute-start.4 = (bf16[2,128,256]{2,1,0:T(8,128)(2,1)S(1)}, bf16[2,128,256]{2,1,0:T(8,128)(2,1)S(1)}, u32[]{:S(2)}, u32[]{:S(2)}) collective-permute-start(bf16[2,128,256]{2,1,0:T(8,128)(2,1)S(1)} %maximum_bitcast_fusion.1), channel_id=1, source_target_pairs={{0,2},{1,3},{2,0},{3,1},{4,6},{5,7},{6,4},{7,5},{8,10},{9,11},{10,... | collective-permute-start | bytes 393224 | tf_op jit(solution)/shard_map/ppermute | solution.py:20
  84.3 10.2 %collective-permute-start.1 = (bf16[704,1024]{1,0:T(8,128)(2,1)S(1)}, bf16[704,1024]{1,0:T(8,128)(2,1)}, u32[]{:S(2)}, u32[]{:S(2)}) collective-permute-start(bf16[704,1024]{1,0:T(8,128)(2,1)S(1)} %pad_maximum_fusion.1.fn_ref), channel_id=1, source_target_pairs={{0,8},{8,0},{16,24},{24,16},{1,9},{9,1},{17,25},{25,17},{2,10},{10... | collective-permute-start | bytes 4325384 | tf_op jit(solution)/shard_map/ppermute | solution.py:20
  84.6 9.7 %collective-permute-start.5 = (bf16[4,128,256]{2,1,0:T(8,128)(2,1)S(1)}, bf16[4,128,256]{2,1,0:T(8,128)(2,1)S(1)}, u32[]{:S(2)}, u32[]{:S(2)}) collective-permute-start(bf16[4,128,256]{2,1,0:T(8,128)(2,1)S(1)} %bitcast.246), channel_id=1, source_target_pairs={{0,1},{1,0},{2,3},{3,2},{4,5},{5,4},{6,7},{7,6},{8,9},{9,8},{10,11... | collective-permute-start | bytes 786440 | tf_op jit(solution)/shard_map/ppermute | solution.py:20
  87.5 32.7 %all-to-all-start.2 = ((bf16[8,352,128]{2,1,0:T(8,128)(2,1)}), bf16[8,352,128]{2,1,0:T(8,128)(2,1)}, u32[]{:S(2)}, u32[]{:S(2)}) async-start(bf16[8,352,128]{2,1,0:T(8,128)(2,1)} %get-tuple-element.66), calls=%async_computation.2 | async-start | bytes 1441792 | tf_op jit(solution)/shard_map/all_to_all | solution.py:141
  91.7 92.1 %all-gather.5.cloned.1.call-start = ((), (), s32[]{:S(2)}) async-start(), calls=%async_computation.8 | async-start | bytes 4718592 | tf_op jit(solution)/shard_map/all_gather | solution.py:657
  92.5 246.0 %reduce-scatter.2.cloned.1.call-start = ((), (), s32[]{:S(2)}) async-start(), calls=%async_computation.9 | async-start | bytes 4718592 | tf_op jit(solution)/shard_map/reduce_scatter | solution.py:701
  121.5 14.6 %collective-permute-start.2 = (bf16[352,1024]{1,0:T(8,128)(2,1)S(1)}, bf16[352,1024]{1,0:T(8,128)(2,1)S(1)}, u32[]{:S(2)}, u32[]{:S(2)}) collective-permute-start(bf16[352,1024]{1,0:T(8,128)(2,1)S(1)} %fusion.16), channel_id=1, source_target_pairs={{0,16},{8,24},{16,0},{24,8},{1,17},{9,25},{17,1},{25,9},{2,18},{10... | collective-permute-start | bytes 2162696 | tf_op jit(solution)/shard_map/ppermute | solution.py:20
  142.3 18.2 %collective-permute-start.7 = (bf16[352,1024]{1,0:T(8,128)(2,1)S(1)}, bf16[352,1024]{1,0:T(8,128)(2,1)S(1)}, u32[]{:S(2)}, u32[]{:S(2)}) collective-permute-start(bf16[352,1024]{1,0:T(8,128)(2,1)S(1)} %slice.398), channel_id=1, source_target_pairs={{0,16},{8,24},{16,0},{24,8},{1,17},{9,25},{17,1},{25,9},{2,18},{10... | collective-permute-start | bytes 2162696 | tf_op jit(solution)/shard_map/ppermute | solution.py:20
  161.7 17.5 %collective-permute-start.9 = (bf16[352,1024]{1,0:T(8,128)(2,1)S(1)}, bf16[352,1024]{1,0:T(8,128)(2,1)S(1)}, u32[]{:S(2)}, u32[]{:S(2)}) collective-permute-start(bf16[352,1024]{1,0:T(8,128)(2,1)S(1)} %add_convert_fusion.2), channel_id=1, source_target_pairs={{0,16},{8,24},{16,0},{24,8},{1,17},{9,25},{17,1},{25,9},{2,18},{10... | collective-permute-start | bytes 2162696 | tf_op jit(solution)/shard_map/ppermute | solution.py:20
  181.0 17.6 %collective-permute-start.8 = (bf16[704,1024]{1,0:T(8,128)(2,1)}, bf16[704,1024]{1,0:T(8,128)(2,1)}, u32[]{:S(2)}, u32[]{:S(2)}) collective-permute-start(bf16[704,1024]{1,0:T(8,128)(2,1)} %pad_maximum_fusion.2.near_ref.gn_ref), channel_id=1, source_target_pairs={{0,8},{8,0},{16,24},{24,16},{1,9},{9,1},{17,25},{25,17},{2,10},{10... | collective-permute-start | bytes 4325384 | tf_op jit(solution)/shard_map/ppermute | solution.py:20
  207.4 4.0 collective-permute-start.11
  207.6 32.8 %collective-permute-start.14 = (bf16[704,1024]{1,0:T(8,128)(2,1)}, bf16[704,1024]{1,0:T(8,128)(2,1)}, u32[]{:S(2)}, u32[]{:S(2)}) collective-permute-start(bf16[704,1024]{1,0:T(8,128)(2,1)} %get-tuple-element.85), channel_id=1, source_target_pairs={{0,8},{8,0},{16,24},{24,16},{1,9},{9,1},{17,25},{25,17},{2,10},{10... | collective-permute-start | bytes 4325384 | tf_op jit(solution)/shard_map/ppermute | solution.py:20
  214.6 18.5 %collective-permute-start.12 = (bf16[352,1024]{1,0:T(8,128)(2,1)}, bf16[352,1024]{1,0:T(8,128)(2,1)}, u32[]{:S(2)}, u32[]{:S(2)}) collective-permute-start(bf16[352,1024]{1,0:T(8,128)(2,1)} %slice.397), channel_id=1, source_target_pairs={{0,16},{8,24},{16,0},{24,8},{1,17},{9,25},{17,1},{25,9},{2,18},{10... | collective-permute-start | bytes 2162696 | tf_op jit(solution)/shard_map/ppermute | solution.py:20
  240.0 17.4 %collective-permute-start.13 = (bf16[352,1024]{1,0:T(8,128)(2,1)S(1)}, bf16[352,1024]{1,0:T(8,128)(2,1)S(1)}, u32[]{:S(2)}, u32[]{:S(2)}) collective-permute-start(bf16[352,1024]{1,0:T(8,128)(2,1)S(1)} %multiply_convert_fusion), channel_id=1, source_target_pairs={{0,16},{8,24},{16,0},{24,8},{1,17},{9,25},{17,1},{25,9},{2,18},{10... | collective-permute-start | bytes 2162696 | tf_op jit(solution)/shard_map/ppermute | solution.py:20
  259.0 18.6 %collective-permute-start.16 = (bf16[352,1024]{1,0:T(8,128)(2,1)S(1)}, bf16[352,1024]{1,0:T(8,128)(2,1)S(1)}, u32[]{:S(2)}, u32[]{:S(2)}) collective-permute-start(bf16[352,1024]{1,0:T(8,128)(2,1)S(1)} %slice.396), channel_id=1, source_target_pairs={{0,16},{8,24},{16,0},{24,8},{1,17},{9,25},{17,1},{25,9},{2,18},{10... | collective-permute-start | bytes 2162696 | tf_op jit(solution)/shard_map/ppermute | solution.py:20
  293.5 12.1 %collective-permute-start.17 = (bf16[704,1024]{1,0:T(8,128)(2,1)}, bf16[704,1024]{1,0:T(8,128)(2,1)}, u32[]{:S(2)}, u32[]{:S(2)}) collective-permute-start(bf16[704,1024]{1,0:T(8,128)(2,1)} %get-tuple-element.92), channel_id=1, source_target_pairs={{0,8},{8,0},{16,24},{24,16},{1,9},{9,1},{17,25},{25,17},{2,10},{10... | collective-permute-start | bytes 4325384 | tf_op jit(solution)/shard_map/ppermute | solution.py:20
  305.6 32.9 %collective-permute-start.19 = (bf16[512,1024]{1,0:T(8,128)(2,1)}, bf16[512,1024]{1,0:T(8,128)(2,1)}, u32[]{:S(2)}, u32[]{:S(2)}) collective-permute-start(bf16[512,1024]{1,0:T(8,128)(2,1)} %shard_map.305), channel_id=1, source_target_pairs={{0,1},{1,0},{2,3},{3,2},{4,5},{5,4},{6,7},{7,6},{8,9},{9,8},{10,11... | collective-permute-start | bytes 3145736 | tf_op jit(solution)/shard_map/ppermute | solution.py:20
  312.7 18.6 %collective-permute-start.18 = (bf16[352,1024]{1,0:T(8,128)(2,1)}, bf16[352,1024]{1,0:T(8,128)(2,1)}, u32[]{:S(2)}, u32[]{:S(2)}) collective-permute-start(bf16[352,1024]{1,0:T(8,128)(2,1)} %slice.395), channel_id=1, source_target_pairs={{0,16},{8,24},{16,0},{24,8},{1,17},{9,25},{17,1},{25,9},{2,18},{10... | collective-permute-start | bytes 2162696 | tf_op jit(solution)/shard_map/ppermute | solution.py:20
  320.1 25.1 %all-to-all-start.3 = ((bf16[8,352,128]{2,1,0:T(8,128)(2,1)}), bf16[8,352,128]{2,1,0:T(8,128)(2,1)}, u32[]{:S(2)}, u32[]{:S(2)}) async-start(bf16[8,352,128]{2,1,0:T(8,128)(2,1)} %bitcast.239), calls=%async_computation.4 | async-start | bytes 1441792 | tf_op jit(solution)/shard_map/all_to_all | solution.py:141
  347.1 6.3 %collective-permute-start.20 = (bf16[2,1,2,352,128]{4,3,2,0,1:T(8,128)(2,1)}, bf16[2,1,2,352,128]{4,3,2,0,1:T(8,128)(2,1)S(1)}, u32[]{:S(2)}, u32[]{:S(2)}) collective-permute-start(bf16[2,1,2,352,128]{4,3,2,0,1:T(8,128)(2,1)} %fusion.27), channel_id=1, source_target_pairs={{0,8},{8,0},{16,24},{24,16},{1,9},{9,1},{17,25},{25,17},{2,10},{10... | collective-permute-start | bytes 1081352 | tf_op jit(solution)/shard_map/ppermute | solution.py:20
  348.2 33.1 %all-to-all-start.4 = ((bf16[8,400,128]{2,1,0:T(8,128)(2,1)}), bf16[8,400,128]{2,1,0:T(8,128)(2,1)}, u32[]{:S(2)}, u32[]{:S(2)}) async-start(bf16[8,400,128]{2,1,0:T(8,128)(2,1)} %pad_maximum_fusion.5), calls=%async_computation.5 | async-start | bytes 1638400 | tf_op jit(solution)/shard_map/all_to_all | solution.py:141
  355.5 10.9 %collective-permute-start.21 = (bf16[1,2,2,352,128]{4,3,2,1,0:T(8,128)(2,1)}, bf16[1,2,2,352,128]{4,3,2,1,0:T(8,128)(2,1)}, u32[]{:S(2)}, u32[]{:S(2)}) collective-permute-start(bf16[1,2,2,352,128]{4,3,2,1,0:T(8,128)(2,1)} %fusion.26), channel_id=1, source_target_pairs={{0,16},{8,24},{16,0},{24,8},{1,17},{9,25},{17,1},{25,9},{2,18},{10... | collective-permute-start | bytes 1081352 | tf_op jit(solution)/shard_map/ppermute | solution.py:20
  360.6 20.7 %collective-permute-start.22 = (bf16[256,1024]{1,0:T(8,128)(2,1)}, bf16[256,1024]{1,0:T(8,128)(2,1)}, u32[]{:S(2)}, u32[]{:S(2)}) collective-permute-start(bf16[256,1024]{1,0:T(8,128)(2,1)} %slice.400), channel_id=1, source_target_pairs={{0,2},{1,3},{2,0},{3,1},{4,6},{5,7},{6,4},{7,5},{8,10},{9,11},{10,... | collective-permute-start | bytes 1572872 | tf_op jit(solution)/shard_map/ppermute | solution.py:20
  382.9 4.2 %collective-permute-start.24 = (f32[8,128]{1,0:T(8,128)S(1)}, f32[8,128]{1,0:T(8,128)S(1)}, u32[]{:S(2)}, u32[]{:S(2)}) collective-permute-start(f32[8,128]{1,0:T(8,128)S(1)} %bitcast_reduce_fusion), channel_id=1, source_target_pairs={{0,8},{8,0},{16,24},{24,16},{1,9},{9,1},{17,25},{25,17},{2,10},{10... | collective-permute-start | bytes 12296 | tf_op jit(solution)/shard_map/ppermute | solution.py:20
  384.2 15.3 %collective-permute-start.23 = (bf16[128,1024]{1,0:T(8,128)(2,1)S(1)}, bf16[128,1024]{1,0:T(8,128)(2,1)S(1)}, u32[]{:S(2)}, u32[]{:S(2)}) collective-permute-start(bf16[128,1024]{1,0:T(8,128)(2,1)S(1)} %slice.401), channel_id=1, source_target_pairs={{0,4},{1,5},{2,6},{3,7},{4,0},{5,1},{6,2},{7,3},{8,12},{9,13},{10,... | collective-permute-start | bytes 786440 | tf_op jit(solution)/shard_map/ppermute | solution.py:20
  387.1 7.6 %collective-permute-start.25 = (f32[8,128]{1,0:T(8,128)S(1)}, f32[8,128]{1,0:T(8,128)S(1)}, u32[]{:S(2)}, u32[]{:S(2)}) collective-permute-start(f32[8,128]{1,0:T(8,128)S(1)} %add.202), channel_id=1, source_target_pairs={{0,16},{8,24},{16,0},{24,8},{1,17},{9,25},{17,1},{25,9},{2,18},{10... | collective-permute-start | bytes 12296 | tf_op jit(solution)/shard_map/ppermute | solution.py:20
  391.2 14.4 %all-to-all-start.5 = ((bf16[4,2,352,128]{3,2,1,0:T(8,128)(2,1)}), bf16[4,2,352,128]{3,2,1,0:T(8,128)(2,1)S(1)}, u32[]{:S(2)}, u32[]{:S(2)}) async-start(bf16[4,2,352,128]{3,2,1,0:T(8,128)(2,1)} %bitcast.74), calls=%async_computation.6 | async-start | bytes 1441792 | tf_op jit(solution)/shard_map/all_to_all | solution.py:103
  (69 other events, 472.1 us)
Sparse Core Ops, SparseCore 0:
  45.5 45.6 all-gather.2
  95.3 75.8 all-gather.4
  236.0 91.2 reduce-scatter.1

commit v6 on v5

--- a/solution.py
+++ b/solution.py
@@ -712,23 +712,10 @@
     grad_attended = lax.dot_general(
         weight_out, grad_a_all, (((0,), (1,)), ((), ())), preferred_element_type=WIDE
     ).astype(LOW)
-    half = attend_backward(
-        query, keys, values, grad_attended, attended_wide, log_total, mask, ones, 0, heads // 2
-    )
-    half, branch_far = together(half, branch_far)
     grad_mixed = attend_backward(
-        query,
-        keys,
-        values,
-        grad_attended,
-        attended_wide,
-        log_total,
-        mask,
-        ones,
-        heads // 2,
-        heads - heads // 2,
-        (half,),
-    )
+        query, keys, values, grad_attended, attended_wide, log_total, mask, ones, 0, heads
+    )
+    grad_mixed, branch_far = together(grad_mixed, branch_far)
     branch_b = branch_kept + branch_far.astype(WIDE) + shrink_shift
     output_parts = cut_width((middle + ff_scale * branch_b).astype(LOW))
     joined = grad_mixed.reshape(3 * head_cols, nx * block)

time: 422 us -> 421 us (level)
    pallas_call x2 -> x1, Pallas kernels: 22.3 us -> 22.1 us  [attend_backward(): pl.pallas_call(attend_backward_body, grid=(count,), in_specs=[head, head,...]
  transfers between devices with their start and end apart: 35 -> 35, of which waited for: 23 -> 21; matrix products, arithmetic and copies ran while one was open for 14% -> 14% of each run, Pallas kernels for 20% -> 20%
where the time goes in v6:
time: 421 us; the launch traced here: 415 us
  waiting for transfers between devices  175 us (42%)
  Pallas kernels  91.3 us (22%)
  starting transfers between devices  45.2 us (11%)
  other arithmetic  43.3 us (10%)
  local copies, waits for them, and re-layouts  38.5 us (9%)
  between operations  15.3 us (4%)
  matrix products  5.86 us (1%)
    ppermute x26, waiting for transfers between devices, swap(): return lax.ppermute(values, axis, [(k, k ^ bit) for k in range(size)])  122 us
    all_to_all x4, waiting for transfers between devices, cross(): return lax.all_to_all(parts, 'gy', split_axis=0, concat_axis=0, tiled=True)  30.3 us
    pallas_call x1, Pallas kernels, attend_backward(): pl.pallas_call(attend_backward_body, grid=(count,), in_specs=[head, head,...  22.1 us
    all_to_all x4, starting transfers between devices, cross(): return lax.all_to_all(parts, 'gy', split_axis=0, concat_axis=0, tiled=True)  21.8 us
    pallas_call x2, Pallas kernels, attend_forward(): pl.pallas_call(attend_forward_body, grid=(count,), in_specs=[head, head,...  20.7 us
    unnamed x138, local copies, waits for them, and re-layouts  20.7 us
    all_to_all x1, waiting for transfers between devices, to_rows(): parts = lax.all_to_all(parts, 'gx', split_axis=0, concat_axis=0, tiled=True)  18.6 us
    ppermute x26, starting transfers between devices, swap(): return lax.ppermute(values, axis, [(k, k ^ bit) for k in range(size)])  15.4 us
  transfers between devices with their start and end apart: 35, of which 21 were waited for; matrix products, arithmetic and copies ran while one was open for 14% of the time, Pallas kernels for 20%

profile of v6, /device:TPU:0, one launch (start us, length us, event | category | flops | bytes accessed | tf_op | source)
XLA Modules:
  0.0 414.5 jit_solution(930260886420305881)
XLA Ops:
  10.2 4.4 %all-to-all-start = ((bf16[4,2,704,128]{3,2,1,0:T(8,128)(2,1)}), bf16[4,2,704,128]{3,2,1,0:T(8,128)(2,1)S(1)}, u32[]{:S(2)}, u32[]{:S(2)}) async-start(bf16[4,2,704,128]{3,2,1,0:T(8,128)(2,1)} %pad_maximum_fusion), calls=%async_computation | async-start | bytes 2883584 | tf_op jit(solution)/shard_map/all_to_all | solution.py:96
  14.7 18.6 %all-to-all-done = bf16[4,2,704,128]{3,2,1,0:T(8,128)(2,1)S(1)} async-done(((bf16[4,2,704,128]{3,2,1,0:T(8,128)(2,1)}), bf16[4,2,704,128]{3,2,1,0:T(8,128)(2,1)S(1)}, u32[]{:S(2)}, u32[]{:S(2)}) %all-to-all-start) | async-done | bytes 1441824 | tf_op jit(solution)/shard_map/all_to_all | solution.py:96
  35.2 6.7 %all-to-all-start.1 = ((bf16[8,384,128]{2,1,0:T(8,128)(2,1)}), bf16[8,384,128]{2,1,0:T(8,128)(2,1)S(1)}, u32[]{:S(2)}, u32[]{:S(2)}) async-start(bf16[8,384,128]{2,1,0:T(8,128)(2,1)} %pad_maximum_fusion.6), calls=%async_computation.1 | async-start | bytes 1572864 | tf_op jit(solution)/shard_map/all_to_all | solution.py:141
  44.1 22.5 %all-to-all-done.1 = bf16[8,384,128]{2,1,0:T(8,128)(2,1)S(1)} async-done(((bf16[8,384,128]{2,1,0:T(8,128)(2,1)}), bf16[8,384,128]{2,1,0:T(8,128)(2,1)S(1)}, u32[]{:S(2)}, u32[]{:S(2)}) %all-to-all-start.1) | async-done | bytes 786464 | tf_op jit(solution)/shard_map/all_to_all | solution.py:141
  68.4 5.2 %collective-permute-done.3 = bf16[1,128,256]{2,1,0:T(8,128)(2,1)S(1)} collective-permute-done((bf16[1,128,256]{2,1,0:T(8,128)(2,1)S(1)}, bf16[1,128,256]{2,1,0:T(8,128)(2,1)S(1)}, u32[]{:S(2)}, u32[]{:S(2)}) %collective-permute-start.3) | collective-permute-done | bytes 65568 | tf_op jit(solution)/shard_map/ppermute | solution.py:20
  73.7 9.3 %collective-permute-done = bf16[352,1024]{1,0:T(8,128)(2,1)} collective-permute-done((bf16[352,1024]{1,0:T(8,128)(2,1)S(1)}, bf16[352,1024]{1,0:T(8,128)(2,1)}, u32[]{:S(2)}, u32[]{:S(2)}) %collective-permute-start) | collective-permute-done | bytes 720928 | tf_op jit(solution)/shard_map/ppermute | solution.py:20
  87.5 4.2 %all-to-all-start.2 = ((bf16[8,352,128]{2,1,0:T(8,128)(2,1)}), bf16[8,352,128]{2,1,0:T(8,128)(2,1)}, u32[]{:S(2)}, u32[]{:S(2)}) async-start(bf16[8,352,128]{2,1,0:T(8,128)(2,1)} %get-tuple-element.66), calls=%async_computation.2 | async-start | bytes 1441792 | tf_op jit(solution)/shard_map/all_to_all | solution.py:141
  94.5 4.8 %convolution_bitcast_fusion = f32[768,1408]{1,0:T(8,128)S(1)} fusion(bf16[1024,768]{1,0:T(8,128)(2,1)} %all-gather.3.cloned.1.call-done.weight_ref, bf16[704,1024]{1,0:T(8,128)(2,1)} %collective-permute-done.1.ff_ref, bf16[352,1024]{1,0:T(8,128)(2,1)} %collective-permute-done, bf16[352,1024]{1,0:T(8,128)(2,1)S(1)} %add_convert_fusion.3), kind=kOutput, calls=%fused_computation | convolution fusion | flops 2223243264 | bytes 8781824 | tf_op jit(solution)/shard_map/dot_general | solution.py:669
  99.8 10.6 %shard_map.296 = (bf16[256,1408]{1,0:T(8,128)(2,1)S(1)}, f32[256,1408]{1,0:T(8,128)S(1)}, f32[4,1,1408]{2,1,0:T(1,128)S(1)}) custom-call(bf16[256,1408]{1,0:T(8,128)(2,1)S(1)} %get-tuple-element.211.q_ref, bf16[256,1408]{1,0:T(8,128)(2,1)S(1)} %slice.397.k_ref, bf16[256,1408]{1,0:T(8,128)(2,1)S(1)} %get-tuple-element.210.v_ref, ...), custom_call_target="tpu_custom_call" | custom-call | flops 12180258816 | bytes 2162688 | tf_op jit(solution)/shard_map/pallas_call | solution.py:241
  112.4 7.8 %all-to-all-done.2 = bf16[8,352,128]{2,1,0:T(8,128)(2,1)} async-done(((bf16[8,352,128]{2,1,0:T(8,128)(2,1)}), bf16[8,352,128]{2,1,0:T(8,128)(2,1)}, u32[]{:S(2)}, u32[]{:S(2)}) %all-to-all-start.2) | async-done | bytes 720928 | tf_op jit(solution)/shard_map/all_to_all | solution.py:141
  123.0 10.1 %shard_map.297 = (bf16[256,1408]{1,0:T(8,128)(2,1)S(1)}, f32[256,1408]{1,0:T(8,128)S(1)}, f32[4,1,1408]{2,1,0:T(1,128)S(1)}) custom-call(bf16[256,1408]{1,0:T(8,128)(2,1)S(1)} %get-tuple-element.211.q_ref, bf16[256,1408]{1,0:T(8,128)(2,1)S(1)} %slice.397.k_ref, ...), custom_call_target="tpu_custom_call", output_to_operand_aliasing={{0}: (5, {}), {1}: (6, {}), {2}: (7, {})} | custom-call | flops 12180258816 | bytes 2162688 | tf_op jit(solution)/shard_map/pallas_call | solution.py:241
  142.7 17.9 %collective-permute-done.7 = bf16[352,1024]{1,0:T(8,128)(2,1)S(1)} collective-permute-done((bf16[352,1024]{1,0:T(8,128)(2,1)S(1)}, bf16[352,1024]{1,0:T(8,128)(2,1)S(1)}, u32[]{:S(2)}, u32[]{:S(2)}) %collective-permute-start.7) | collective-permute-done | bytes 720928 | tf_op jit(solution)/shard_map/ppermute | solution.py:20
  162.1 17.2 %collective-permute-done.9 = bf16[352,1024]{1,0:T(8,128)(2,1)S(1)} collective-permute-done((bf16[352,1024]{1,0:T(8,128)(2,1)S(1)}, bf16[352,1024]{1,0:T(8,128)(2,1)S(1)}, u32[]{:S(2)}, u32[]{:S(2)}) %collective-permute-start.9) | collective-permute-done | bytes 720928 | tf_op jit(solution)/shard_map/ppermute | solution.py:20
  188.7 9.8 %shard_map.299 = (bf16[1408,1024]{1,0:T(8,128)(2,1)S(1)}, f32[1408,1024]{1,0:T(8,128)}, f32[704,1024]{1,0:T(8,128)S(1)}, bf16[704,1024]{1,0:T(8,128)(2,1)}) custom-call(bf16[704,1024]{1,0:T(8,128)(2,1)S(1)} %copy-done.5, bf16[704,1024]{1,0:T(8,128)(2,1)S(1)} %copy-done.25, bf16[1024,2048]{1,0:T(8,128)(2,1)S(1)} %copy-done.19, ...), custom_call_target="tpu_custom_call" | custom-call | flops 11811160064 | bytes 20054016 | tf_op jit(solution)/shard_map/pallas_call | solution.py:398
  198.5 8.8 %shard_map.300 = (bf16[1408,1024]{1,0:T(8,128)(2,1)S(1)}, f32[704,1024]{1,0:T(8,128)S(1)}, bf16[704,1024]{1,0:T(8,128)(2,1)S(1)}, f32[1,1024]{1,0:T(1,128)S(1)}) custom-call(bf16[704,1024]{1,0:T(8,128)(2,1)} %pad_maximum_fusion.2.near_ref.gn_ref, bf16[704,1024]{1,0:T(8,128)(2,1)} %collective-permute-done.8.far_ref.gf_ref, bf16[1024,2048]{1,0:T(8,128)(2,1)S(1)} %copy-done.20, ...), custom_call_target="tpu_custom_call" | custom-call | flops 11811160064 | bytes 20054016 | tf_op jit(solution)/shard_map/pallas_call | solution.py:418
  207.9 3.5 collective-permute-done.11
  215.3 11.1 %shard_map.301 = bf16[1024,2048]{1,0:T(8,128)(2,1)} custom-call(bf16[704,1024]{1,0:T(8,128)(2,1)} %pad_maximum_fusion.2.near_ref.gn_ref, bf16[704,1024]{1,0:T(8,128)(2,1)} %collective-permute-done.8.far_ref.gf_ref, bf16[704,1024]{1,0:T(8,128)(2,1)S(1)} %copy-done.6, bf16[704,1024]{1,0:T(8,128)(2,1)S(1)} %copy-done.26, ...), custom_call_target="tpu_custom_call" | custom-call | flops 11811160064 | bytes 15728640 | tf_op jit(solution)/shard_map/pallas_call | solution.py:477
  226.4 6.7 %collective-permute-done.12 = bf16[352,1024]{1,0:T(8,128)(2,1)} collective-permute-done((bf16[352,1024]{1,0:T(8,128)(2,1)}, bf16[352,1024]{1,0:T(8,128)(2,1)}, u32[]{:S(2)}, u32[]{:S(2)}) %collective-permute-start.12) | collective-permute-done | bytes 720928 | tf_op jit(solution)/shard_map/ppermute | solution.py:20
  235.9 3.9 multiply_reduce_fusion.2
  242.2 15.2 %collective-permute-done.13 = bf16[352,1024]{1,0:T(8,128)(2,1)S(1)} collective-permute-done((bf16[352,1024]{1,0:T(8,128)(2,1)S(1)}, bf16[352,1024]{1,0:T(8,128)(2,1)S(1)}, u32[]{:S(2)}, u32[]{:S(2)}) %collective-permute-start.13) | collective-permute-done | bytes 720928 | tf_op jit(solution)/shard_map/ppermute | solution.py:20
  262.1 22.1 %shard_map.302 = bf16[3,256,1408]{2,1,0:T(8,128)(2,1)S(1)} custom-call(bf16[256,1408]{1,0:T(8,128)(2,1)S(1)} %copy-done.14, bf16[256,1408]{1,0:T(8,128)(2,1)S(1)} %copy-done.10, bf16[256,1408]{1,0:T(8,128)(2,1)S(1)} %copy-done.12, bf16[256,1408]{1,0:T(8,128)(2,1)S(1)} %fusion.11.g_ref, f32[256,1408]{1,0:T(8,128)S(1)} %copy-done.35, ...), custom_call_target="tpu_custom_call" | custom-call | flops 28420603904 | bytes 7208960 | tf_op jit(solution)/shard_map/pallas_call | solution.py:300
  285.1 4.6 %shard_map.303 = (f32[704,1024]{1,0:T(8,128)S(1)}, bf16[704,1024]{1,0:T(8,128)(2,1)}) custom-call(bf16[768,1408]{1,0:T(8,128)(2,1)S(1)} %bitcast.231, bf16[1024,768]{1,0:T(8,128)(2,1)S(1)} %copy-done.21), custom_call_target="tpu_custom_call" | custom-call | flops 2214592512 | bytes 8060928 | tf_op jit(solution)/shard_map/pallas_call | solution.py:507
  295.7 6.5 %shard_map.304 = bf16[512,1024]{1,0:T(8,128)(2,1)} custom-call(s32[1]{0:T(128)} %bitcast.39.place_ref, bf16[704,1024]{1,0:T(8,128)(2,1)S(1)} %copy-done.1, bf16[704,1024]{1,0:T(8,128)(2,1)} %collective-permute-done.1.ff_ref, bf16[704,1024]{1,0:T(8,128)(2,1)S(1)} %copy-done.3, bf16[704,1024]{1,0:T(8,128)(2,1)S(1)} %copy-done.23, ...), custom_call_target="tpu_custom_call" | custom-call | flops 2952790016 | bytes 7864320 | tf_op jit(solution)/shard_map/pallas_call | solution.py:558
  303.4 3.5 convert_add_fusion
  311.1 5.6 %shard_map.305 = f32[512,1024]{1,0:T(8,128)S(1)} custom-call(s32[1]{0:T(128)} %bitcast.39.place_ref, bf16[704,1024]{1,0:T(8,128)(2,1)S(1)} %copy-done.1, bf16[704,1024]{1,0:T(8,128)(2,1)} %collective-permute-done.1.ff_ref, bf16[704,1024]{1,0:T(8,128)(2,1)S(1)} %copy-done.3, bf16[704,1024]{1,0:T(8,128)(2,1)S(1)} %copy-done.23, ...), custom_call_target="tpu_custom_call" | custom-call | flops 2952790016 | bytes 7864320 | tf_op jit(solution)/shard_map/pallas_call | solution.py:558
  316.7 6.1 %all-to-all-start.3 = ((bf16[8,352,128]{2,1,0:T(8,128)(2,1)}), bf16[8,352,128]{2,1,0:T(8,128)(2,1)}, u32[]{:S(2)}, u32[]{:S(2)}) async-start(bf16[8,352,128]{2,1,0:T(8,128)(2,1)} %bitcast.239), calls=%async_computation.4 | async-start | bytes 1441792 | tf_op jit(solution)/shard_map/all_to_all | solution.py:141
  322.8 5.1 %collective-permute-done.18 = bf16[352,1024]{1,0:T(8,128)(2,1)} collective-permute-done((bf16[352,1024]{1,0:T(8,128)(2,1)}, bf16[352,1024]{1,0:T(8,128)(2,1)}, u32[]{:S(2)}, u32[]{:S(2)}) %collective-permute-start.18) | collective-permute-done | bytes 720928 | tf_op jit(solution)/shard_map/ppermute | solution.py:20
  327.8 11.9 %collective-permute-done.19 = bf16[512,1024]{1,0:T(8,128)(2,1)} collective-permute-done((bf16[512,1024]{1,0:T(8,128)(2,1)}, bf16[512,1024]{1,0:T(8,128)(2,1)}, u32[]{:S(2)}, u32[]{:S(2)}) %collective-permute-start.19) | collective-permute-done | bytes 1048608 | tf_op jit(solution)/shard_map/ppermute | solution.py:20
  348.4 4.8 %all-to-all-start.4 = ((bf16[8,400,128]{2,1,0:T(8,128)(2,1)}), bf16[8,400,128]{2,1,0:T(8,128)(2,1)}, u32[]{:S(2)}, u32[]{:S(2)}) async-start(bf16[8,400,128]{2,1,0:T(8,128)(2,1)} %pad_maximum_fusion.5), calls=%async_computation.5 | async-start | bytes 1638400 | tf_op jit(solution)/shard_map/all_to_all | solution.py:141
  368.4 12.6 %collective-permute-done.22 = bf16[256,1024]{1,0:T(8,128)(2,1)} collective-permute-done((bf16[256,1024]{1,0:T(8,128)(2,1)}, bf16[256,1024]{1,0:T(8,128)(2,1)}, u32[]{:S(2)}, u32[]{:S(2)}) %collective-permute-start.22) | collective-permute-done | bytes 524320 | tf_op jit(solution)/shard_map/ppermute | solution.py:20
  394.8 4.4 %collective-permute-done.23 = bf16[128,1024]{1,0:T(8,128)(2,1)S(1)} collective-permute-done((bf16[128,1024]{1,0:T(8,128)(2,1)S(1)}, bf16[128,1024]{1,0:T(8,128)(2,1)S(1)}, u32[]{:S(2)}, u32[]{:S(2)}) %collective-permute-start.23) | collective-permute-done | bytes 262176 | tf_op jit(solution)/shard_map/ppermute | solution.py:20
  401.2 4.0 all-to-all-done.5
  (298 shorter events, 109.8 us)
Async XLA Ops:
  10.2 23.1 %all-to-all-start = ((bf16[4,2,704,128]{3,2,1,0:T(8,128)(2,1)}), bf16[4,2,704,128]{3,2,1,0:T(8,128)(2,1)S(1)}, u32[]{:S(2)}, u32[]{:S(2)}) async-start(bf16[4,2,704,128]{3,2,1,0:T(8,128)(2,1)} %pad_maximum_fusion), calls=%async_computation | async-start | bytes 2883584 | tf_op jit(solution)/shard_map/all_to_all | solution.py:96
  35.2 31.4 %all-to-all-start.1 = ((bf16[8,384,128]{2,1,0:T(8,128)(2,1)}), bf16[8,384,128]{2,1,0:T(8,128)(2,1)S(1)}, u32[]{:S(2)}, u32[]{:S(2)}) async-start(bf16[8,384,128]{2,1,0:T(8,128)(2,1)} %pad_maximum_fusion.6), calls=%async_computation.1 | async-start | bytes 1572864 | tf_op jit(solution)/shard_map/all_to_all | solution.py:141
  41.9 52.7 %all-gather.3.cloned.1.call-start = ((), (), s32[]{:S(2)}) async-start(), calls=%async_computation.7 | async-start | bytes 1769472 | tf_op jit(solution)/shard_map/all_gather | solution.py:644
  67.3 15.8 %collective-permute-start = (bf16[352,1024]{1,0:T(8,128)(2,1)S(1)}, bf16[352,1024]{1,0:T(8,128)(2,1)}, u32[]{:S(2)}, u32[]{:S(2)}) collective-permute-start(bf16[352,1024]{1,0:T(8,128)(2,1)S(1)} %add_convert_fusion.3), channel_id=1, source_target_pairs={{0,16},{8,24},{16,0},{24,8},{1,17},{9,25},{17,1},{25,9},{2,18},{10... | collective-permute-start | bytes 2162696 | tf_op jit(solution)/shard_map/ppermute | solution.py:20
  68.4 5.2 %collective-permute-start.3 = (bf16[1,128,256]{2,1,0:T(8,128)(2,1)S(1)}, bf16[1,128,256]{2,1,0:T(8,128)(2,1)S(1)}, u32[]{:S(2)}, u32[]{:S(2)}) collective-permute-start(bf16[1,128,256]{2,1,0:T(8,128)(2,1)S(1)} %bitcast.249), channel_id=1, source_target_pairs={{0,4},{1,5},{2,6},{3,7},{4,0},{5,1},{6,2},{7,3},{8,12},{9,13},{10,... | collective-permute-start | bytes 196616 | tf_op jit(solution)/shard_map/ppermute | solution.py:20
  73.7 10.8 %collective-permute-start.4 = (bf16[2,128,256]{2,1,0:T(8,128)(2,1)S(1)}, bf16[2,128,256]{2,1,0:T(8,128)(2,1)S(1)}, u32[]{:S(2)}, u32[]{:S(2)}) collective-permute-start(bf16[2,128,256]{2,1,0:T(8,128)(2,1)S(1)} %maximum_bitcast_fusion.1), channel_id=1, source_target_pairs={{0,2},{1,3},{2,0},{3,1},{4,6},{5,7},{6,4},{7,5},{8,10},{9,11},{10,... | collective-permute-start | bytes 393224 | tf_op jit(solution)/shard_map/ppermute | solution.py:20
  84.3 10.2 %collective-permute-start.1 = (bf16[704,1024]{1,0:T(8,128)(2,1)S(1)}, bf16[704,1024]{1,0:T(8,128)(2,1)}, u32[]{:S(2)}, u32[]{:S(2)}) collective-permute-start(bf16[704,1024]{1,0:T(8,128)(2,1)S(1)} %pad_maximum_fusion.1.fn_ref), channel_id=1, source_target_pairs={{0,8},{8,0},{16,24},{24,16},{1,9},{9,1},{17,25},{25,17},{2,10},{10... | collective-permute-start | bytes 4325384 | tf_op jit(solution)/shard_map/ppermute | solution.py:20
  84.6 9.7 %collective-permute-start.5 = (bf16[4,128,256]{2,1,0:T(8,128)(2,1)S(1)}, bf16[4,128,256]{2,1,0:T(8,128)(2,1)S(1)}, u32[]{:S(2)}, u32[]{:S(2)}) collective-permute-start(bf16[4,128,256]{2,1,0:T(8,128)(2,1)S(1)} %bitcast.246), channel_id=1, source_target_pairs={{0,1},{1,0},{2,3},{3,2},{4,5},{5,4},{6,7},{7,6},{8,9},{9,8},{10,11... | collective-permute-start | bytes 786440 | tf_op jit(solution)/shard_map/ppermute | solution.py:20
  87.5 32.7 %all-to-all-start.2 = ((bf16[8,352,128]{2,1,0:T(8,128)(2,1)}), bf16[8,352,128]{2,1,0:T(8,128)(2,1)}, u32[]{:S(2)}, u32[]{:S(2)}) async-start(bf16[8,352,128]{2,1,0:T(8,128)(2,1)} %get-tuple-element.66), calls=%async_computation.2 | async-start | bytes 1441792 | tf_op jit(solution)/shard_map/all_to_all | solution.py:141
  91.7 92.1 %all-gather.5.cloned.1.call-start = ((), (), s32[]{:S(2)}) async-start(), calls=%async_computation.8 | async-start | bytes 4718592 | tf_op jit(solution)/shard_map/all_gather | solution.py:657
  92.5 247.3 %reduce-scatter.2.cloned.1.call-start = ((), (), s32[]{:S(2)}) async-start(), calls=%async_computation.9 | async-start | bytes 4718592 | tf_op jit(solution)/shard_map/reduce_scatter | solution.py:701
  121.5 14.6 %collective-permute-start.2 = (bf16[352,1024]{1,0:T(8,128)(2,1)S(1)}, bf16[352,1024]{1,0:T(8,128)(2,1)S(1)}, u32[]{:S(2)}, u32[]{:S(2)}) collective-permute-start(bf16[352,1024]{1,0:T(8,128)(2,1)S(1)} %fusion.16), channel_id=1, source_target_pairs={{0,16},{8,24},{16,0},{24,8},{1,17},{9,25},{17,1},{25,9},{2,18},{10... | collective-permute-start | bytes 2162696 | tf_op jit(solution)/shard_map/ppermute | solution.py:20
  142.3 18.2 %collective-permute-start.7 = (bf16[352,1024]{1,0:T(8,128)(2,1)S(1)}, bf16[352,1024]{1,0:T(8,128)(2,1)S(1)}, u32[]{:S(2)}, u32[]{:S(2)}) collective-permute-start(bf16[352,1024]{1,0:T(8,128)(2,1)S(1)} %slice.396), channel_id=1, source_target_pairs={{0,16},{8,24},{16,0},{24,8},{1,17},{9,25},{17,1},{25,9},{2,18},{10... | collective-permute-start | bytes 2162696 | tf_op jit(solution)/shard_map/ppermute | solution.py:20
  161.7 17.5 %collective-permute-start.9 = (bf16[352,1024]{1,0:T(8,128)(2,1)S(1)}, bf16[352,1024]{1,0:T(8,128)(2,1)S(1)}, u32[]{:S(2)}, u32[]{:S(2)}) collective-permute-start(bf16[352,1024]{1,0:T(8,128)(2,1)S(1)} %add_convert_fusion.2), channel_id=1, source_target_pairs={{0,16},{8,24},{16,0},{24,8},{1,17},{9,25},{17,1},{25,9},{2,18},{10... | collective-permute-start | bytes 2162696 | tf_op jit(solution)/shard_map/ppermute | solution.py:20
  181.0 17.5 %collective-permute-start.8 = (bf16[704,1024]{1,0:T(8,128)(2,1)}, bf16[704,1024]{1,0:T(8,128)(2,1)}, u32[]{:S(2)}, u32[]{:S(2)}) collective-permute-start(bf16[704,1024]{1,0:T(8,128)(2,1)} %pad_maximum_fusion.2.near_ref.gn_ref), channel_id=1, source_target_pairs={{0,8},{8,0},{16,24},{24,16},{1,9},{9,1},{17,25},{25,17},{2,10},{10... | collective-permute-start | bytes 4325384 | tf_op jit(solution)/shard_map/ppermute | solution.py:20
  207.3 4.1 collective-permute-start.11
  207.5 32.9 %collective-permute-start.14 = (bf16[704,1024]{1,0:T(8,128)(2,1)}, bf16[704,1024]{1,0:T(8,128)(2,1)}, u32[]{:S(2)}, u32[]{:S(2)}) collective-permute-start(bf16[704,1024]{1,0:T(8,128)(2,1)} %get-tuple-element.85), channel_id=1, source_target_pairs={{0,8},{8,0},{16,24},{24,16},{1,9},{9,1},{17,25},{25,17},{2,10},{10... | collective-permute-start | bytes 4325384 | tf_op jit(solution)/shard_map/ppermute | solution.py:20
  214.6 18.5 %collective-permute-start.12 = (bf16[352,1024]{1,0:T(8,128)(2,1)}, bf16[352,1024]{1,0:T(8,128)(2,1)}, u32[]{:S(2)}, u32[]{:S(2)}) collective-permute-start(bf16[352,1024]{1,0:T(8,128)(2,1)} %slice.395), channel_id=1, source_target_pairs={{0,16},{8,24},{16,0},{24,8},{1,17},{9,25},{17,1},{25,9},{2,18},{10... | collective-permute-start | bytes 2162696 | tf_op jit(solution)/shard_map/ppermute | solution.py:20
  240.0 17.4 %collective-permute-start.13 = (bf16[352,1024]{1,0:T(8,128)(2,1)S(1)}, bf16[352,1024]{1,0:T(8,128)(2,1)S(1)}, u32[]{:S(2)}, u32[]{:S(2)}) collective-permute-start(bf16[352,1024]{1,0:T(8,128)(2,1)S(1)} %multiply_convert_fusion), channel_id=1, source_target_pairs={{0,16},{8,24},{16,0},{24,8},{1,17},{9,25},{17,1},{25,9},{2,18},{10... | collective-permute-start | bytes 2162696 | tf_op jit(solution)/shard_map/ppermute | solution.py:20
  259.0 25.2 %collective-permute-start.16 = (bf16[352,1024]{1,0:T(8,128)(2,1)S(1)}, bf16[352,1024]{1,0:T(8,128)(2,1)S(1)}, u32[]{:S(2)}, u32[]{:S(2)}) collective-permute-start(bf16[352,1024]{1,0:T(8,128)(2,1)S(1)} %slice.394), channel_id=1, source_target_pairs={{0,16},{8,24},{16,0},{24,8},{1,17},{9,25},{17,1},{25,9},{2,18},{10... | collective-permute-start | bytes 2162696 | tf_op jit(solution)/shard_map/ppermute | solution.py:20
  289.8 12.4 %collective-permute-start.17 = (bf16[704,1024]{1,0:T(8,128)(2,1)}, bf16[704,1024]{1,0:T(8,128)(2,1)}, u32[]{:S(2)}, u32[]{:S(2)}) collective-permute-start(bf16[704,1024]{1,0:T(8,128)(2,1)} %get-tuple-element.92), channel_id=1, source_target_pairs={{0,8},{8,0},{16,24},{24,16},{1,9},{9,1},{17,25},{25,17},{2,10},{10... | collective-permute-start | bytes 4325384 | tf_op jit(solution)/shard_map/ppermute | solution.py:20
  302.2 37.6 %collective-permute-start.19 = (bf16[512,1024]{1,0:T(8,128)(2,1)}, bf16[512,1024]{1,0:T(8,128)(2,1)}, u32[]{:S(2)}, u32[]{:S(2)}) collective-permute-start(bf16[512,1024]{1,0:T(8,128)(2,1)} %shard_map.304), channel_id=1, source_target_pairs={{0,1},{1,0},{2,3},{3,2},{4,5},{5,4},{6,7},{7,6},{8,9},{9,8},{10,11... | collective-permute-start | bytes 3145736 | tf_op jit(solution)/shard_map/ppermute | solution.py:20
  309.3 18.6 %collective-permute-start.18 = (bf16[352,1024]{1,0:T(8,128)(2,1)}, bf16[352,1024]{1,0:T(8,128)(2,1)}, u32[]{:S(2)}, u32[]{:S(2)}) collective-permute-start(bf16[352,1024]{1,0:T(8,128)(2,1)} %slice.393), channel_id=1, source_target_pairs={{0,16},{8,24},{16,0},{24,8},{1,17},{9,25},{17,1},{25,9},{2,18},{10... | collective-permute-start | bytes 2162696 | tf_op jit(solution)/shard_map/ppermute | solution.py:20
  316.7 28.7 %all-to-all-start.3 = ((bf16[8,352,128]{2,1,0:T(8,128)(2,1)}), bf16[8,352,128]{2,1,0:T(8,128)(2,1)}, u32[]{:S(2)}, u32[]{:S(2)}) async-start(bf16[8,352,128]{2,1,0:T(8,128)(2,1)} %bitcast.239), calls=%async_computation.4 | async-start | bytes 1441792 | tf_op jit(solution)/shard_map/all_to_all | solution.py:141
  347.3 5.9 %collective-permute-start.20 = (bf16[2,1,2,352,128]{4,3,2,0,1:T(8,128)(2,1)}, bf16[2,1,2,352,128]{4,3,2,0,1:T(8,128)(2,1)S(1)}, u32[]{:S(2)}, u32[]{:S(2)}) collective-permute-start(bf16[2,1,2,352,128]{4,3,2,0,1:T(8,128)(2,1)} %fusion.27), channel_id=1, source_target_pairs={{0,8},{8,0},{16,24},{24,16},{1,9},{9,1},{17,25},{25,17},{2,10},{10... | collective-permute-start | bytes 1081352 | tf_op jit(solution)/shard_map/ppermute | solution.py:20
  348.4 32.6 %all-to-all-start.4 = ((bf16[8,400,128]{2,1,0:T(8,128)(2,1)}), bf16[8,400,128]{2,1,0:T(8,128)(2,1)}, u32[]{:S(2)}, u32[]{:S(2)}) async-start(bf16[8,400,128]{2,1,0:T(8,128)(2,1)} %pad_maximum_fusion.5), calls=%async_computation.5 | async-start | bytes 1638400 | tf_op jit(solution)/shard_map/all_to_all | solution.py:141
  355.3 10.9 %collective-permute-start.21 = (bf16[1,2,2,352,128]{4,3,2,1,0:T(8,128)(2,1)}, bf16[1,2,2,352,128]{4,3,2,1,0:T(8,128)(2,1)}, u32[]{:S(2)}, u32[]{:S(2)}) collective-permute-start(bf16[1,2,2,352,128]{4,3,2,1,0:T(8,128)(2,1)} %fusion.26), channel_id=1, source_target_pairs={{0,16},{8,24},{16,0},{24,8},{1,17},{9,25},{17,1},{25,9},{2,18},{10... | collective-permute-start | bytes 1081352 | tf_op jit(solution)/shard_map/ppermute | solution.py:20
  360.1 20.8 %collective-permute-start.22 = (bf16[256,1024]{1,0:T(8,128)(2,1)}, bf16[256,1024]{1,0:T(8,128)(2,1)}, u32[]{:S(2)}, u32[]{:S(2)}) collective-permute-start(bf16[256,1024]{1,0:T(8,128)(2,1)} %slice.398), channel_id=1, source_target_pairs={{0,2},{1,3},{2,0},{3,1},{4,6},{5,7},{6,4},{7,5},{8,10},{9,11},{10,... | collective-permute-start | bytes 1572872 | tf_op jit(solution)/shard_map/ppermute | solution.py:20
  382.6 4.3 %collective-permute-start.24 = (f32[8,128]{1,0:T(8,128)S(1)}, f32[8,128]{1,0:T(8,128)S(1)}, u32[]{:S(2)}, u32[]{:S(2)}) collective-permute-start(f32[8,128]{1,0:T(8,128)S(1)} %bitcast_reduce_fusion), channel_id=1, source_target_pairs={{0,8},{8,0},{16,24},{24,16},{1,9},{9,1},{17,25},{25,17},{2,10},{10... | collective-permute-start | bytes 12296 | tf_op jit(solution)/shard_map/ppermute | solution.py:20
  383.9 15.3 %collective-permute-start.23 = (bf16[128,1024]{1,0:T(8,128)(2,1)S(1)}, bf16[128,1024]{1,0:T(8,128)(2,1)S(1)}, u32[]{:S(2)}, u32[]{:S(2)}) collective-permute-start(bf16[128,1024]{1,0:T(8,128)(2,1)S(1)} %slice.399), channel_id=1, source_target_pairs={{0,4},{1,5},{2,6},{3,7},{4,0},{5,1},{6,2},{7,3},{8,12},{9,13},{10,... | collective-permute-start | bytes 786440 | tf_op jit(solution)/shard_map/ppermute | solution.py:20
  386.9 7.4 %collective-permute-start.25 = (f32[8,128]{1,0:T(8,128)S(1)}, f32[8,128]{1,0:T(8,128)S(1)}, u32[]{:S(2)}, u32[]{:S(2)}) collective-permute-start(f32[8,128]{1,0:T(8,128)S(1)} %add.202), channel_id=1, source_target_pairs={{0,16},{8,24},{16,0},{24,8},{1,17},{9,25},{17,1},{25,9},{2,18},{10... | collective-permute-start | bytes 12296 | tf_op jit(solution)/shard_map/ppermute | solution.py:20
  390.7 14.4 %all-to-all-start.5 = ((bf16[4,2,352,128]{3,2,1,0:T(8,128)(2,1)}), bf16[4,2,352,128]{3,2,1,0:T(8,128)(2,1)S(1)}, u32[]{:S(2)}, u32[]{:S(2)}) async-start(bf16[4,2,352,128]{3,2,1,0:T(8,128)(2,1)} %bitcast.74), calls=%async_computation.6 | async-start | bytes 1441792 | tf_op jit(solution)/shard_map/all_to_all | solution.py:103
  (69 other events, 473.2 us)
Sparse Core Ops, SparseCore 0:
  45.5 45.6 all-gather.2
  95.3 75.8 all-gather.4
  236.0 93.9 reduce-scatter.1
